TPU v7x, 32 devices: a whole 2x2x4 slice. The times are simulated.
32 devices in a mesh: chan: 4 (over y, core), facet: 8 (over z, x).
Axes of the slice: x: 2, y: 2, z: 4, core: 2. Of those that a mesh axis runs over, the one named last changes fastest.
Arguments:
- visibilities: bfloat16 [16, 8, 4, 32768], P(None, None, 'chan', 'facet'), may hold values from -6 to 6
- w_kernel: bfloat16 [32, 2, 8], replicated, may hold values from -2 to 2
- w_index: int32 [4, 32768], P(None, 'facet'), may hold values from 0 to 31
- cell_offsets: int32 [2, 4, 32768], P(None, None, 'facet'), may hold values from 0 to 24
- block_sub: int32 [4, 64], P(None, 'facet'), may hold values from 0 to 31
- intersection_rows: int32 [8, 32], replicated, may hold values from 0 to 63, as said below
- intersection_count: int32 [8], replicated, may hold values from 1 to 32, as said below
Outputs:
- sky_image: float32 [16, 4, 64, 16384], P('chan', None, None, 'facet')
Inputs may be any that keep to these rules, and one draw needn't show every extreme that they name: `intersection_rows`: the rows in one facet's list are distinct. `intersection_count`: some facet other than the last has exactly 32 entries in use.
All inputs are finite; a program needn't handle non-finite values.
Results may differ from a plain program's by a relative error of at most 0.0059.
Values may be sent and summed in bfloat16 or wider, within the bound.
No kernel may reach another device: no remote copies, remote signals or barrier semaphores. Data moves between devices by JAX's collectives and lax.ppermute only.
A program may use at most 128 MiB of HBM per device.

v0:
```python
import math

import jax
import jax.numpy as jnp
from jax import lax
from jax.sharding import PartitionSpec as P

BLK = 512
SG = 32
NSUB = 32
FX = 2048
FY = 64
MARGIN = 128


def shifted(block, axis, distance):
    devices = range(lax.axis_size(axis))
    route = [(i - distance, i) for i in devices if i - distance in devices]
    return lax.ppermute(block, axis, route)


def anchors(sub_index, side_len, period):
    span = period // side_len
    row_anchor = (jnp.mod(sub_index * 37, span) - span // 2) * side_len
    col_anchor = (jnp.mod(sub_index * 53 + 5, span) - span // 2) * side_len
    return (row_anchor, col_anchor)


def row_tables(sub_index, side_len, height, period):
    row_anchor, col_anchor = anchors(sub_index, side_len, period)
    cell_ids = jnp.arange(side_len, dtype=jnp.int32)
    line_ids = jnp.arange(height, dtype=jnp.int32) - height // 2
    phase_int = (row_anchor[:, None, None] + cell_ids[None, None, :]) * line_ids[None, :, None]
    radians = jnp.mod(phase_int, period).astype(jnp.float32) * (2.0 * math.pi / period)
    return (jnp.cos(radians).astype(jnp.bfloat16), jnp.sin(radians).astype(jnp.bfloat16))


def col_tables(sub_index, side_len, col_ids, period):
    row_anchor, col_anchor = anchors(sub_index, side_len, period)
    cell_ids = jnp.arange(side_len, dtype=jnp.int32)
    phase_int = (col_anchor[:, None, None] + cell_ids[None, :, None]) * (col_ids - period // 2)[
        None, None, :
    ]
    radians = jnp.mod(phase_int, period).astype(jnp.float32) * (2.0 * math.pi / period)
    return (jnp.cos(radians).astype(jnp.bfloat16), (-jnp.sin(radians)).astype(jnp.bfloat16))


def place_kernel(values, offsets, side_len):
    distance = jnp.arange(side_len, dtype=jnp.int32)[:, None] - offsets[None, :]
    running = jnp.zeros((values.shape[0], side_len, offsets.shape[0]), jnp.float32)
    for tap_idx in range(values.shape[1]):
        running = (
            running + values[:, tap_idx, None, :] * (distance == tap_idx).astype(jnp.float32)[None]
        )
    return running


def combine(products, side_len, row_width):
    real_part = products[:, :side_len, :row_width] - products[:, side_len:, row_width:]
    imag_part = products[:, :side_len, row_width:] + products[:, side_len:, :row_width]
    return jnp.stack([real_part, imag_part], axis=1)


def block_terms(vis_part, plane_ids, cell_pos, kernel, side_len, block_len):
    planes = kernel.shape[0]
    plane_pick = (jnp.arange(planes, dtype=jnp.int32)[:, None] == plane_ids[None, :]).astype(
        jnp.float32
    )
    values = jnp.einsum(
        "wqk,wr->qkr", kernel.astype(jnp.float32), plane_pick, precision=lax.Precision.HIGHEST
    )
    left_kern = place_kernel(values, cell_pos[0], side_len).astype(jnp.bfloat16)
    right_kern = place_kernel(values, cell_pos[1], side_len)
    num_pols = vis_part.shape[1] // 2
    vis_real = vis_part[:, :num_pols].astype(jnp.float32)[:, :, None, :]
    vis_imag = vis_part[:, num_pols:].astype(jnp.float32)[:, :, None, :]
    y_real = (vis_real * right_kern[0][None, None] - vis_imag * right_kern[1][None, None]).astype(
        jnp.bfloat16
    )
    y_imag = (vis_real * right_kern[1][None, None] + vis_imag * right_kern[0][None, None]).astype(
        jnp.bfloat16
    )
    num_rows = plane_ids.shape[0]
    blocks = num_rows // block_len
    row_width = vis_part.shape[0] * num_pols * side_len
    stacked = jnp.concatenate(
        [
            y_real.reshape(row_width, blocks, block_len),
            y_imag.reshape(row_width, blocks, block_len),
        ],
        axis=0,
    )
    left_flat = left_kern.reshape(2 * side_len, blocks, block_len)
    products = lax.dot_general(
        left_flat, stacked, (((2,), (2,)), ((1,), (1,))), preferred_element_type=jnp.float32
    )
    return combine(products, side_len, row_width)


def to_rows(subgrid, row_cos, row_sin, img_scale):
    sub_real = subgrid[:, 0]
    sub_imag = subgrid[:, 1]

    def apply_table(table, data):
        return jnp.einsum("gyu,guq->gyq", table, data, preferred_element_type=jnp.float32)

    real_part = apply_table(row_cos, sub_real) - apply_table(row_sin, sub_imag)
    imag_part = apply_table(row_cos, sub_imag) + apply_table(row_sin, sub_real)
    return (jnp.stack([real_part, imag_part], axis=1) * img_scale).astype(jnp.bfloat16)


def project(image_sum, row_image, first_sub, col_ids, period):
    num_items = row_image.shape[0]
    group_len = math.gcd(num_items, 8)
    side_len = SG
    mixed = image_sum.shape[0]
    shaped = row_image.reshape(num_items, 2, row_image.shape[2], mixed, side_len)

    def add_group(turn_idx, running):
        row_piece = lax.dynamic_slice_in_dim(shaped, turn_idx * group_len, group_len, 0)
        sub_index = first_sub + turn_idx * group_len + jnp.arange(group_len, dtype=jnp.int32)
        col_cos, col_sin = col_tables(sub_index, side_len, col_ids, period)
        col_table = jnp.stack([col_cos, col_sin], axis=1)
        return running + jnp.einsum(
            "grycv,grvx->cyx", row_piece, col_table, preferred_element_type=jnp.float32
        )

    return lax.fori_loop(0, num_items // group_len, add_group, image_sum)


def shards(
    visibilities, w_kernel, w_index, cell_offsets, block_sub, intersection_rows, intersection_count
):
    turned = lax.all_to_all(visibilities, "chan", split_axis=0, concat_axis=2, tiled=True)
    groups = lax.axis_size("chan")
    facets = lax.axis_size("facet")
    num_chans = turned.shape[0]
    num_pols = turned.shape[1] // 2
    side_len = SG
    per_dev = w_index.shape[1] // BLK
    row_width = num_chans * num_pols * side_len

    def grid_group(group_id):
        vis_part = lax.dynamic_index_in_dim(turned, group_id, 2, keepdims=False)
        plane_ids = lax.dynamic_index_in_dim(w_index, group_id, 0, keepdims=False)
        cell_pos = lax.dynamic_index_in_dim(cell_offsets, group_id, 1, keepdims=False)
        return block_terms(vis_part, plane_ids, cell_pos, w_kernel, side_len, BLK)

    grid_parts = lax.map(grid_group, jnp.arange(groups, dtype=jnp.int32))
    blocks = groups * per_dev
    grid_parts = grid_parts.reshape(blocks, 2 * side_len * row_width)
    sub_ids = block_sub.reshape(blocks)
    plane_pick = (jnp.arange(NSUB, dtype=jnp.int32)[:, None] == sub_ids[None, :]).astype(
        jnp.float32
    )
    img_scale = 1.0 / math.sqrt(groups * facets * w_index.shape[1])
    period = FX * facets
    facet_id = lax.axis_index("facet")
    col_ids = facet_id * FX + jnp.arange(FX, dtype=jnp.int32)
    image = jnp.zeros((num_chans * num_pols, FY, FX), jnp.float32)
    partial_sum = jnp.dot(plane_pick, grid_parts, precision=lax.Precision.HIGHEST)
    summed = lax.psum(partial_sum, "facet")
    subgrid = summed.reshape(NSUB, 2, side_len, row_width).astype(jnp.bfloat16)
    sub_index = jnp.arange(NSUB, dtype=jnp.int32)
    row_cos, row_sin = row_tables(sub_index, side_len, FY, period)
    row_image = to_rows(subgrid, row_cos, row_sin, img_scale)
    image = project(image, row_image, 0, col_ids, period)
    line_ids = jnp.arange(FY, dtype=jnp.int32)
    slot_ids = jnp.arange(intersection_rows.shape[1], dtype=jnp.int32)
    edge_cols = image[:, :, FX - MARGIN :]
    listed = lax.dynamic_index_in_dim(intersection_rows, facet_id, 0, keepdims=False)
    in_use = lax.dynamic_index_in_dim(intersection_count, facet_id, 0, keepdims=False)
    row_keep = jnp.sum(
        ((listed[:, None] == line_ids[None, :]) & (slot_ids[:, None] < in_use)).astype(jnp.float32),
        axis=0,
    )
    arrived = shifted(edge_cols * row_keep[None, :, None], "facet", 1)
    sky_image = jnp.concatenate([image[:, :, :MARGIN] + arrived, image[:, :, MARGIN:]], axis=2)
    return sky_image.reshape(num_chans, num_pols, FY, FX)


def solution(mesh):
    return jax.shard_map(
        shards,
        mesh=mesh,
        in_specs=(
            P(None, None, "chan", "facet"),
            P(),
            P(None, "facet"),
            P(None, None, "facet"),
            P(None, "facet"),
            P(),
            P(),
        ),
        out_specs=P("chan", None, None, "facet"),
        check_vma=False,
    )
```

profile of v0, /device:TPU:0, one launch (start us, length us, event | category | flops | bytes accessed | tf_op | source)
XLA Modules:
  0.0 424.0 jit_solution(3462052901594539061)
XLA Ops:
  0.0 4.4 %all-to-all-start = ((bf16[16,8,1,4096]{3,1,2,0:T(8,128)(2,1)}), bf16[16,8,1,4096]{3,1,2,0:T(8,128)(2,1)S(1)}, u32[]{:S(2)}, u32[]{:S(2)}) async-start(bf16[16,8,1,4096]{3,1,2,0:T(8,128)(2,1)} %param.11), calls=%async_computation | async-start | bytes 2097152 | tf_op jit(solution)/shard_map/all_to_all | solution.py:134
  7.9 11.0 %all-to-all-done = bf16[16,8,1,4096]{3,1,2,0:T(8,128)(2,1)S(1)} async-done(((bf16[16,8,1,4096]{3,1,2,0:T(8,128)(2,1)}), bf16[16,8,1,4096]{3,1,2,0:T(8,128)(2,1)S(1)}, u32[]{:S(2)}, u32[]{:S(2)}) %all-to-all-start) | async-done | bytes 1048608 | tf_op jit(solution)/shard_map/all_to_all | solution.py:134
  18.8 90.8 %while.27 = (s32[]{:T(128)}, f32[4,8,2,32,512]{4,3,2,1,0:T(8,128)}, s32[4]{0:T(128)S(1)}, s32[4,4096]{1,0:T(4,128)}, bf16[32,2,8]{0,2,1:T(8,128)(2,1)}, /*index=...) while((s32[]{:T(128)}, f32[4,8,2,32,512]{4,3,2,1,0:T(8,128)}, ...), condition=%wide.region_1.2_spmd, body=%wide.region_0.1_spmd.sunk | while | flops 587988992 | bytes 84559040 | solution.py:149
  109.7 5.0 %reshape.590 = f32[32,32768]{1,0:T(8,128)} reshape(f32[4,8,2,32,512]{4,3,2,1,0:T(8,128)} %get-tuple-element.178) | data formatting | bytes 8388608 | tf_op jit(solution)/shard_map/reshape | solution.py:151
  114.7 6.2 %fusion.60 = f32[32,32768]{1,0:T(8,128)} fusion(f32[32,32768]{1,0:T(8,128)} %reshape.590, s32[32]{0:T(128)S(1)} %eq.182), kind=kOutput, calls=%fused_computation.121 | convolution fusion | flops 402654208 | bytes 8388736 | tf_op jit(solution)/shard_map/dot_general | solution.py:161
  120.9 168.0 %all-reduce.1 = bf16[32,32768]{1,0:T(8,128)(2,1)} all-reduce(f32[32,32768]{1,0:T(8,128)} %fusion.60), channel_id=1, replica_groups=mesh['chan'=4,'facet'=8] {'facet'}, use_global_device_ids=true, to_apply=%region_2.3 | all-reduce | flops 1048576 | bytes 6291456 | tf_op jit(solution)/shard_map/psum | solution.py:162
  293.9 4.0 fusion.55
  298.0 4.2 convolution_add_fusion
  302.2 6.8 %copy.38 = f32[32,64,512]{1,2,0:T(8,128)} copy(f32[32,64,512]{2,1,0:T(8,128)} %convolution_add_fusion) | data formatting | bytes 8388608 | tf_op jit(solution)/shard_map/add | solution.py:108
  309.0 5.8 %convolution_subtract_fusion = f32[32,64,512]{2,1,0:T(8,128)} fusion(f32[32,64,512]{2,1,0:T(8,128)} %fusion.55, bf16[32,2,32,512]{3,2,1,0:T(8,128)(2,1)S(1)} %bitcast.145, s32[64]{0:T(128)S(1)} %iota_add_fusion.2, s32[32,32]{1,0:T(8,128)S(1)} %iota_add_fusion.1), kind=kOutput, calls=%fused_computation.100 | convolution fusion | flops 69140480 | bytes 9454080 | tf_op jit(solution)/shard_map/gyu,guq->gyq/dot_general | solution.py:105
  314.8 6.9 %copy.37 = f32[32,64,512]{1,2,0:T(8,128)} copy(f32[32,64,512]{2,1,0:T(8,128)} %convolution_subtract_fusion) | data formatting | bytes 8388608 | tf_op jit(solution)/shard_map/sub | solution.py:107
  321.7 9.8 %fusion.54 = bf16[32,2,64,16,32]{2,4,3,0,1:T(8,128)(2,1)} fusion(f32[32,1,64,16,32]{2,4,3,0,1:T(8,128)} %bitcast.140, f32[32,1,64,16,32]{2,4,3,0,1:T(8,128)} %bitcast.141), kind=kLoop, calls=%fused_computation.97 | loop fusion | flops 6291456 | bytes 12582912 | tf_op jit(solution)/shard_map/convert_element_type | solution.py:109
  331.5 73.2 %while.28 = (s32[]{:T(128)}, f32[16,64,2048]{2,1,0:T(8,128)}, bf16[32,2,64,16,32]{2,4,3,0,1:T(8,128)(2,1)}, s32[]{:T(128)}, s32[]{:T(128)}, /*index=5*/s32[]{:T(128)}, s32[]{:T(128)}, s32[]{:T(128)}) while((s32[]{:T(128)}, f32[16,64,2048]{2,1,0:T(8,128)}, bf16[32,2,64,16,32]{2,4,3,0,1:T(8,128)(2,1)}, s32[]{:T(128)}, s32[]{:T(128)}, ...), condition=%wide.region_4.5_spmd.clone, body=%wide.region_3.4_spmd.clone.sunk | while | flops 2164789760 | bytes 23087328 | solution.py:128
  331.6 8.9 %cosine_convert_fusion.5 = (bf16[8,1,32,2048]{3,2,1,0:T(8,128)(2,1)S(1)}, bf16[8,1,32,2048]{3,2,1,0:T(8,128)(2,1)S(1)}) fusion(s32[2048]{0:T(1024)S(1)} %add_add_fusion.2, s32[8,32]{1,0:T(8,128)S(1)} %iota_add_fusion.4), kind=kLoop, calls=%fused_computation.85.clone.1 | loop fusion | flops 8912896 | bytes 2106368 | tf_op jit(solution)/shard_map/while/body/eval_jaxpr/convert_element_type | solution.py:45
  340.5 7.4 %bitcast_add_fusion.2 = f32[16,64,2048]{2,1,0:T(8,128)} fusion(f32[16,64,2048]{2,1,0:T(8,128)} %get-tuple-element.474, pred[]{:T(512)S(6)} %compare.19, bf16[8,1,32,2048]{3,2,1,0:T(8,128)(2,1)S(1)} %get-tuple-element.430, bf16[8,1,32,2048]{3,2,1,0:T(8,128)(2,1)S(1)} %get-tuple-element.431, bf16[32,2,64,16,32]{2,4,3,0,1:T(8,128)(2,1)} %get-tuple-element.483, ...), kind=kOutput, calls=%fused_computation.71.clone.1 | convolution fusion | flops 2155872256 | bytes 20971524 | tf_op jit(solution)/shard_map/while/body/eval_jaxpr/grycv,grvx->cyx/dot_general | solution.py:124
  348.0 8.9 %cosine_convert_fusion.5 = (bf16[8,1,32,2048]{3,2,1,0:T(8,128)(2,1)S(1)}, bf16[8,1,32,2048]{3,2,1,0:T(8,128)(2,1)S(1)}) fusion(s32[2048]{0:T(1024)S(1)} %add_add_fusion.2, s32[8,32]{1,0:T(8,128)S(1)} %iota_add_fusion.4), kind=kLoop, calls=%fused_computation.85.clone.1 | loop fusion | flops 8912896 | bytes 2106368 | tf_op jit(solution)/shard_map/while/body/eval_jaxpr/convert_element_type | solution.py:45
  357.0 9.9 %bitcast_add_fusion.2 = f32[16,64,2048]{2,1,0:T(8,128)} fusion(f32[16,64,2048]{2,1,0:T(8,128)} %get-tuple-element.474, pred[]{:T(512)S(6)} %compare.19, bf16[8,1,32,2048]{3,2,1,0:T(8,128)(2,1)S(1)} %get-tuple-element.430, bf16[8,1,32,2048]{3,2,1,0:T(8,128)(2,1)S(1)} %get-tuple-element.431, bf16[32,2,64,16,32]{2,4,3,0,1:T(8,128)(2,1)} %get-tuple-element.483, ...), kind=kOutput, calls=%fused_computation.71.clone.1 | convolution fusion | flops 2155872256 | bytes 20971524 | tf_op jit(solution)/shard_map/while/body/eval_jaxpr/grycv,grvx->cyx/dot_general | solution.py:124
  367.0 8.9 %cosine_convert_fusion.5 = (bf16[8,1,32,2048]{3,2,1,0:T(8,128)(2,1)S(1)}, bf16[8,1,32,2048]{3,2,1,0:T(8,128)(2,1)S(1)}) fusion(s32[2048]{0:T(1024)S(1)} %add_add_fusion.2, s32[8,32]{1,0:T(8,128)S(1)} %iota_add_fusion.4), kind=kLoop, calls=%fused_computation.85.clone.1 | loop fusion | flops 8912896 | bytes 2106368 | tf_op jit(solution)/shard_map/while/body/eval_jaxpr/convert_element_type | solution.py:45
  375.9 9.9 %bitcast_add_fusion.2 = f32[16,64,2048]{2,1,0:T(8,128)} fusion(f32[16,64,2048]{2,1,0:T(8,128)} %get-tuple-element.474, pred[]{:T(512)S(6)} %compare.19, bf16[8,1,32,2048]{3,2,1,0:T(8,128)(2,1)S(1)} %get-tuple-element.430, bf16[8,1,32,2048]{3,2,1,0:T(8,128)(2,1)S(1)} %get-tuple-element.431, bf16[32,2,64,16,32]{2,4,3,0,1:T(8,128)(2,1)} %get-tuple-element.483, ...), kind=kOutput, calls=%fused_computation.71.clone.1 | convolution fusion | flops 2155872256 | bytes 20971524 | tf_op jit(solution)/shard_map/while/body/eval_jaxpr/grycv,grvx->cyx/dot_general | solution.py:124
  385.9 8.9 %cosine_convert_fusion.5 = (bf16[8,1,32,2048]{3,2,1,0:T(8,128)(2,1)S(1)}, bf16[8,1,32,2048]{3,2,1,0:T(8,128)(2,1)S(1)}) fusion(s32[2048]{0:T(1024)S(1)} %add_add_fusion.2, s32[8,32]{1,0:T(8,128)S(1)} %iota_add_fusion.4), kind=kLoop, calls=%fused_computation.85.clone.1 | loop fusion | flops 8912896 | bytes 2106368 | tf_op jit(solution)/shard_map/while/body/eval_jaxpr/convert_element_type | solution.py:45
  394.8 9.9 %bitcast_add_fusion.2 = f32[16,64,2048]{2,1,0:T(8,128)} fusion(f32[16,64,2048]{2,1,0:T(8,128)} %get-tuple-element.474, pred[]{:T(512)S(6)} %compare.19, bf16[8,1,32,2048]{3,2,1,0:T(8,128)(2,1)S(1)} %get-tuple-element.430, bf16[8,1,32,2048]{3,2,1,0:T(8,128)(2,1)S(1)} %get-tuple-element.431, bf16[32,2,64,16,32]{2,4,3,0,1:T(8,128)(2,1)} %get-tuple-element.483, ...), kind=kOutput, calls=%fused_computation.71.clone.1 | convolution fusion | flops 2155872256 | bytes 20971524 | tf_op jit(solution)/shard_map/while/body/eval_jaxpr/grycv,grvx->cyx/dot_general | solution.py:124
  407.3 3.8 slice.85
  411.1 7.1 %collective-permute-done = f32[16,64,128]{2,1,0:T(8,128)S(1)} collective-permute-done((f32[16,64,128]{2,1,0:T(8,128)S(1)}, f32[16,64,128]{2,1,0:T(8,128)S(1)}, u32[]{:S(2)}, u32[]{:S(2)}) %collective-permute-start) | collective-permute-done | bytes 524320 | tf_op jit(solution)/shard_map/ppermute | solution.py:19
  419.4 4.6 %pad_maximum_fusion = f32[16,64,2048]{2,1,0:T(8,128)} fusion(f32[16,64,1920]{2,1,0:T(8,128)S(1)} %slice.85, f32[16,64,128]{2,1,0:T(8,128)S(1)} %slice_add_fusion.1), kind=kLoop, calls=%fused_computation.98 | loop fusion | flops 2097152 | bytes 16777216 | tf_op jit(solution)/shard_map/concatenate | solution.py:178
  (134 shorter events, 94.7 us)
Async XLA Ops:
  0.0 7.2 %copy-start = (s32[8,32]{1,0:T(8,128)S(1)}, s32[8,32]{1,0:T(8,128)}, u32[]{:S(2)}) copy-start(s32[8,32]{1,0:T(8,128)} %param.16) | copy-start | bytes 3076
  0.0 18.8 %all-to-all-start = ((bf16[16,8,1,4096]{3,1,2,0:T(8,128)(2,1)}), bf16[16,8,1,4096]{3,1,2,0:T(8,128)(2,1)S(1)}, u32[]{:S(2)}, u32[]{:S(2)}) async-start(bf16[16,8,1,4096]{3,1,2,0:T(8,128)(2,1)} %param.11), calls=%async_computation | async-start | bytes 2097152 | tf_op jit(solution)/shard_map/all_to_all | solution.py:134
  331.5 73.2 %copy-start.2 = (f32[64]{0:T(128)S(1)}, f32[64]{0:T(128)}, u32[]{:S(2)}) copy-start(f32[64]{0:T(128)} %convert_reduce_fusion) | copy-start | bytes 772
  405.8 12.4 %collective-permute-start = (f32[16,64,128]{2,1,0:T(8,128)S(1)}, f32[16,64,128]{2,1,0:T(8,128)S(1)}, u32[]{:S(2)}, u32[]{:S(2)}) collective-permute-start(f32[16,64,128]{2,1,0:T(8,128)S(1)} %slice_multiply_fusion), channel_id=1, source_target_pairs={{0,1},{1,2},{2,3},{3,4},{4,5},{5,6},{6,7},{8,9},{9,10},{10,11},{11... | collective-permute-start | bytes 1572872 | tf_op jit(solution)/shard_map/ppermute | solution.py:19
  419.4 4.6 %copy-start.1 = (s32[8,32]{1,0:T(8,128)S(1)}, s32[8,32]{1,0:T(8,128)}, u32[]{:S(2)}) copy-start(s32[8,32]{1,0:T(8,128)} %param.16) | copy-start | bytes 3076
where the time goes:
time: 426 us; the launch traced here: 424 us
  blocking collectives  168 us (39%)
  other arithmetic  78.2 us (18%)
  matrix products  75.8 us (18%)
  local copies, waits for them, and re-layouts  69.1 us (16%)
  waiting for transfers between devices  18.1 us (4%)
  loops' own time  8.9 us (2%)
  starting transfers between devices  5.84 us (1%)
    psum x1, blocking collectives, shards(): summed = lax.psum(partial_sum, 'facet')  168 us
    dot_general x4, matrix products, add_group(): jnp.einsum('grycv,grvx->cyx', row_piece, col_table, preferred_element_typ...  37 us
    convert_element_type x4, other arithmetic, col_tables(): jnp.cos(radians).astype(jnp.bfloat16)  35.7 us
    while x28, local copies, waits for them, and re-layouts  19.7 us
    dot_general x4, matrix products, apply_table(): jnp.einsum('gyu,guq->gyq', table, data, preferred_element_type=jnp.float32)  16.7 us
    dot_general x4, matrix products, block_terms(): lax.dot_general(left_flat, stacked, (((2,), (2,)), ((1,), (1,))), preferr...  12.2 us
    all_to_all x1, waiting for transfers between devices, shards(): lax.all_to_all(visibilities, 'chan', split_axis=0, concat_axis=2, tiled=T...  11 us
    convert_element_type x4, other arithmetic, block_terms(): (vis_real * right_kern[0][None, None] - vis_imag * right_kern[1][None, No...  10.5 us
  transfers between devices with their start and end apart: 2, of which 2 were waited for; matrix products, arithmetic and copies ran while one was open for 2% of the time, Pallas kernels for 0%

commit v1 on v0

v1 whole, which is shorter than its diff:
```python
import functools
import math

import jax
import jax.numpy as jnp
from jax import lax
from jax.experimental import pallas as pl
from jax.experimental.pallas import tpu as pltpu
from jax.sharding import Mesh
from jax.sharding import PartitionSpec as P

BLK = 512
SG = 32
NSUB = 32
FX = 2048
FY = 64
MARGIN = 128
LANES = 128
PACK = LANES // SG
SETS = NSUB // PACK
CHAN = ("y", "core")
FACET = ("z1", "z0", "x")


def swap(block, axis):
    return shift(block, axis, 1)


def shift(block, axis, distance):
    size = lax.axis_size(axis)
    return lax.ppermute(block, axis, [(i, (i + distance) % size) for i in range(size)])


def grid_kernel(place_ref, sub_ref, taps_ref, rows_ref, *refs, row_len):
    out_refs, sums_ref = refs[:-1], refs[-1]
    step = pl.program_id(0)
    lines = rows_ref.shape[1]
    pols = lines // 4
    half = pols // 2
    cells = 2 * pols * SG
    blocks = row_len // BLK
    pieces = lines // blocks
    width = row_len // lines

    @pl.when(step == 0)
    def _():
        sums_ref[...] = jnp.zeros_like(sums_ref)

    taps = taps_ref[...]
    ids = rows_ref[0, :, row_len : row_len + 3 * width].astype(jnp.float32).astype(jnp.int32)
    cell = lax.broadcasted_iota(jnp.int32, (8, BLK), 0)
    line_id = lax.broadcasted_iota(jnp.int32, (lines, BLK), 0)

    def listed(kind, block):
        part = ids[:, kind * width : (kind + 1) * width]
        found = [part[k : k + 1] for k in range(pieces * block, pieces * (block + 1))]
        return jnp.concatenate(found, axis=1) if pieces > 1 else found[0]

    def pick(values, index, axis):
        found = [
            jnp.take_along_axis(
                values if axis else values[:, c : c + LANES], index[:, c : c + LANES], axis=axis
            )
            for c in range(0, BLK, LANES)
        ]
        return jnp.concatenate(found, axis=1)

    def spread(values, offset):
        distance = cell - offset
        keep = [
            (distance + 8 * tile >= 0) & (distance + 8 * tile < 8) for tile in range(SG // 8)
        ]
        turned = [pick(values[8 * q : 8 * q + 8], distance & 7, 0) for q in range(2)]
        return [
            jnp.concatenate([jnp.where(m, part, 0.0) for m in keep], axis=0) for part in turned
        ]

    for block in range(blocks):
        plane = jnp.broadcast_to(listed(0, block), (16, BLK))
        values = pick(taps, plane, 1)
        left = jnp.concatenate(spread(values, listed(1, block)), axis=0).astype(jnp.bfloat16)
        kern_re, kern_im = spread(values, listed(2, block))
        vis = rows_ref[0, :, block * BLK : (block + 1) * BLK].astype(jnp.float32)
        vis = pltpu.roll(vis, place_ref[0] * (lines // 2), 0)
        turned = jnp.where(
            line_id % pols < half, pltpu.roll(vis, lines - half, 0), pltpu.roll(vis, half, 0)
        )
        vis = jnp.where(place_ref[1] == 1, turned, vis)
        real, imag = [], []
        for first in (0, 2 * pols):
            for row in range(first, first + pols):
                vis_re = vis[row : row + 1]
                vis_im = vis[row + pols : row + pols + 1]
                real.append((vis_re * kern_re - vis_im * kern_im).astype(jnp.bfloat16))
                imag.append((vis_re * kern_im + vis_im * kern_re).astype(jnp.bfloat16))
        weighted = jnp.concatenate(real + imag, axis=0)
        sub = sub_ref[step * blocks + block]
        sums_ref[sub] += lax.dot_general(
            left, weighted, (((1,), (1,)), ((), ())), preferred_element_type=jnp.float32
        )

    @pl.when(step == pl.num_programs(0) - 1)
    def _():
        slot = lax.broadcasted_iota(jnp.int32, (2 * SG, LANES), 1) // SG

        def finish(group, carry):
            parts = []
            for k in range(PACK):
                raw = sums_ref[group * PACK + k]
                real = raw[:SG, :cells] - raw[SG:, cells:]
                imag = raw[:SG, cells:] + raw[SG:, :cells]
                parts.append(jnp.concatenate([real, imag], axis=0))
            for pol in range(2 * pols):
                tile = slice(pol // PACK * LANES, (pol // PACK + 1) * LANES)
                packed = jnp.zeros((2 * SG, LANES), jnp.float32)
                for k in range(PACK):
                    move = (k - pol) % PACK * SG
                    part = parts[k][:, tile]
                    part = pltpu.roll(part, move, 1) if move else part
                    packed = jnp.where(slot == k, part, packed)
                out_refs[pol // half][pol % half, group] = packed.astype(jnp.bfloat16)
            return carry

        lax.fori_loop(0, SETS, finish, 0)


def grid_rows(place, sub_ids, taps, rows, row_len):
    sources, lines, width = rows.shape
    pols = lines // 4
    shape = (pols // 2, SETS, 2 * SG, LANES)
    whole = pl.BlockSpec(shape, lambda s, *_: (0, 0, 0, 0))
    flops = 2 * sources * row_len * 2 * SG * 4 * pols * SG
    return pl.pallas_call(
        functools.partial(grid_kernel, row_len=row_len),
        out_shape=[jax.ShapeDtypeStruct(shape, jnp.bfloat16)] * 4,
        grid_spec=pltpu.PrefetchScalarGridSpec(
            num_scalar_prefetch=2,
            grid=(sources,),
            in_specs=[
                pl.BlockSpec(taps.shape, lambda s, *_: (0, 0)),
                pl.BlockSpec((1, lines, width), lambda s, *_: (s, 0, 0)),
            ],
            out_specs=[whole] * 4,
            scratch_shapes=[pltpu.VMEM((NSUB, 2 * SG, 4 * pols * SG), jnp.float32)],
        ),
        compiler_params=pltpu.CompilerParams(vmem_limit_bytes=32 << 20),
        cost_estimate=pl.CostEstimate(flops=flops, bytes_accessed=3 << 20, transcendentals=0),
        name="grid_rows",
    )(place, sub_ids, taps, rows)


def table_kernel(first_ref, out_ref, *, period):
    group = pl.program_id(0)
    cells = PACK * SG
    row = lax.broadcasted_iota(jnp.int32, (cells, LANES), 0)
    lane = lax.broadcasted_iota(jnp.int32, (cells, LANES), 1)
    span = period // SG
    sub = group * PACK + row // SG
    cell = (lax.rem(sub * 53 + 5, span) - span // 2) * SG + row % SG
    unit = 2.0 * math.pi / period

    def angle(column):
        return jnp.mod(cell * column, period).astype(jnp.float32) * unit

    tiles = out_ref.shape[1] // LANES
    start = jnp.where(lane == tiles - 1, -MARGIN, lane * LANES)
    fine, coarse = angle(lane), angle(first_ref[0] + start)
    fine_cos, fine_sin = jnp.cos(fine), jnp.sin(fine)
    coarse_cos, coarse_sin = jnp.cos(coarse), jnp.sin(coarse)
    for tile in range(tiles):
        columns = slice(tile * LANES, (tile + 1) * LANES)
        tile_cos = coarse_cos[:, tile : tile + 1]
        tile_sin = coarse_sin[:, tile : tile + 1]
        full_cos = tile_cos * fine_cos - tile_sin * fine_sin
        full_sin = tile_sin * fine_cos + tile_cos * fine_sin
        out_ref[:cells, columns] = full_cos.astype(jnp.bfloat16)
        out_ref[cells:, columns] = (-full_sin).astype(jnp.bfloat16)


def col_table(first, period, width):
    depth = 2 * NSUB * SG
    return pl.pallas_call(
        functools.partial(table_kernel, period=period),
        out_shape=jax.ShapeDtypeStruct((depth, width), jnp.bfloat16),
        grid_spec=pltpu.PrefetchScalarGridSpec(
            num_scalar_prefetch=1,
            grid=(SETS,),
            in_specs=[],
            out_specs=pl.BlockSpec((depth // SETS, width), lambda g, *_: (g, 0)),
        ),
        cost_estimate=pl.CostEstimate(
            flops=8 * depth * width, bytes_accessed=2 * depth * width, transcendentals=1 << 19
        ),
        name="col_table",
    )(first)


def row_table(period):
    sub = jnp.arange(NSUB, dtype=jnp.int32)
    span = period // SG
    anchor = (jnp.mod(sub * 37, span) - span // 2) * SG
    cell_ids = jnp.arange(SG, dtype=jnp.int32)
    line_ids = jnp.arange(FY, dtype=jnp.int32) - FY // 2
    phase = (anchor[:, None, None] + cell_ids[None, None, :]) * line_ids[None, :, None]
    radians = jnp.mod(phase, period).astype(jnp.float32) * (2.0 * math.pi / period)
    cos, sin = jnp.cos(radians), jnp.sin(radians)
    turn = jnp.stack([jnp.stack([cos, -sin], 2), jnp.stack([sin, cos], 2)], 1)
    turn = turn.reshape(SETS, PACK, 2 * FY, 2 * SG).transpose(0, 2, 1, 3)
    return turn.reshape(SETS, 2 * FY, PACK * 2 * SG).astype(jnp.bfloat16)


def image_kernel(place_ref, *refs, parts, scale):
    piece_refs = refs[:parts]
    turn_ref, table_ref, edge_ref, keep_ref = refs[parts : parts + 4]
    out_ref, rows_ref = refs[-2:]
    step = pl.program_id(0)
    per = piece_refs[0].shape[0]
    columns = out_ref.shape[2]

    @pl.when(step == 0)
    def _():
        slot = lax.broadcasted_iota(jnp.int32, (2 * SG, 2 * LANES), 1) % LANES // SG
        flat = [(part, i) for part in range(parts) for i in range(per)]

        def group_rows(group, carry):
            for k in range(0, len(flat), 2):
                pair = [piece_refs[part][i, group] for part, i in flat[k : k + 2]]
                pair = jnp.concatenate(pair, axis=1)
                zero = jnp.zeros_like(pair)
                spread = [jnp.where(slot == s, pair, zero) for s in range(PACK)]
                spread = jnp.concatenate(spread, axis=0)
                turned = jnp.dot(turn_ref[group], spread, preferred_element_type=jnp.float32)
                turned = (turned * scale).astype(jnp.bfloat16)
                for m in range(2):
                    for q in range(2):
                        rows_ref[
                            group, (k + m) * FY : (k + m + 1) * FY, q * LANES : (q + 1) * LANES
                        ] = turned[q * FY : (q + 1) * FY, m * LANES : (m + 1) * LANES]
            return carry

        lax.fori_loop(0, SETS, group_rows, 0)

    lines = jnp.concatenate([rows_ref[group] for group in range(SETS)], axis=1)
    total = jnp.dot(lines, table_ref[...], preferred_element_type=jnp.float32)
    total = total.reshape(parts * per, FY, columns)
    for part in range(parts):
        where = pl.ds(lax.rem(place_ref[1] + part, 2) * per, per)
        out_ref[where] = total[part * per : (part + 1) * per]

    @pl.when(step == 0)
    def _():
        edge = jnp.dot(lines, edge_ref[...], preferred_element_type=jnp.float32)
        edge = edge.reshape(parts * per, FY, MARGIN) * keep_ref[...][None]
        for part in range(parts):
            where = pl.ds(lax.rem(place_ref[1] + part, 2) * per, per)
            out_ref[where, :, :MARGIN] += edge[part * per : (part + 1) * per]


def add_image(image, place, pieces, turn, table, keep, total_pols, scale):
    parts, per = len(pieces), pieces[0].shape[0]
    pols = parts * per
    columns = 512
    depth = table.shape[0]
    width = table.shape[1] - MARGIN

    def whole(array):
        return pl.BlockSpec(array.shape, lambda s, *_: (0,) * array.ndim)

    operands = [*pieces, turn, table, table, keep]
    in_specs = [whole(piece) for piece in pieces] + [
        whole(turn),
        pl.BlockSpec((depth, columns), lambda s, *_: (0, s)),
        pl.BlockSpec((depth, MARGIN), lambda s, *_: (0, width // MARGIN)),
        whole(keep),
    ]
    aliases = {}
    if image is not None:
        operands.append(image)
        in_specs.append(pl.BlockSpec(memory_space=pl.ANY))
        aliases = {len(operands): 0}
    return pl.pallas_call(
        functools.partial(image_kernel, parts=parts, scale=scale),
        out_shape=jax.ShapeDtypeStruct((total_pols, FY, width), jnp.float32),
        grid_spec=pltpu.PrefetchScalarGridSpec(
            num_scalar_prefetch=1,
            grid=(width // columns,),
            in_specs=in_specs,
            out_specs=pl.BlockSpec((pols, FY, columns), lambda s, place: (place[0], 0, s)),
            scratch_shapes=[pltpu.VMEM((SETS, pols * FY, 2 * LANES), jnp.bfloat16)],
        ),
        input_output_aliases=aliases,
        compiler_params=pltpu.CompilerParams(vmem_limit_bytes=32 << 20),
        cost_estimate=pl.CostEstimate(
            flops=2 * pols * FY * depth * width,
            bytes_accessed=2 * depth * width + 4 * pols * FY * width,
            transcendentals=0,
        ),
        name="add_image",
    )(place, *operands)


def shards(
    visibilities, w_kernel, w_index, cell_offsets, block_sub, intersection_rows, intersection_count
):
    cores, east = lax.axis_size("core"), lax.axis_size("x")
    north, upper = lax.axis_size("y"), lax.axis_size("z0")
    groups, facets = north * cores, lax.axis_size(FACET)
    num_chans, num_parts, _, row_len = visibilities.shape
    num_pols = num_parts // 2
    own_chans = num_chans // groups
    shares = upper * east
    chan_shares = math.gcd(shares, own_chans)
    pol_shares = shares // chan_shares
    per_chan, per_pol = own_chans // chan_shares, num_pols // pol_shares
    pols = per_chan * per_pol
    lines = 4 * pols
    period = FX * facets
    facet_id = lax.axis_index(FACET)
    group_id = lax.axis_index(CHAN)
    core, z1, z0, x = (lax.axis_index(axis) for axis in ("core", "z1", "z0", "x"))

    vis = visibilities.reshape(
        north, cores, chan_shares, per_chan, 2, pol_shares, per_pol, row_len
    )
    vis = vis.transpose(0, 2, 5, 1, 4, 3, 6, 7).reshape(north * shares, lines, row_len)
    plane = lax.dynamic_slice_in_dim(w_index, group_id, 1, 0)
    cells = lax.dynamic_slice_in_dim(cell_offsets, group_id, 1, 1).reshape(2, row_len)
    ids = jnp.concatenate([plane, cells], axis=0).reshape(3, lines, row_len // lines)
    ids = ids.transpose(1, 0, 2).reshape(lines, 3 * row_len // lines)
    blocks = row_len // BLK
    subs = lax.dynamic_slice_in_dim(block_sub, group_id, 1, 0).reshape(blocks, 1, 1)
    subs = jnp.broadcast_to(subs, (blocks, lines // blocks, LANES)).reshape(lines, LANES)
    ids = jnp.concatenate([ids, subs], axis=1).astype(jnp.bfloat16)
    ids = jnp.broadcast_to(ids[None], (north * shares,) + ids.shape)
    sent = jnp.concatenate([vis, ids], axis=2)
    rows = lax.all_to_all(sent, ("y", "z0", "x"), split_axis=0, concat_axis=0, tiled=True)
    sub_ids = rows[:, :: lines // blocks, -1].astype(jnp.int32).reshape(-1)

    taps = w_kernel.astype(jnp.float32).transpose(1, 2, 0).reshape(-1, w_kernel.shape[0])
    taps = jnp.pad(taps, ((0, 0), (0, LANES - taps.shape[1])))
    first = jnp.reshape(facet_id * FX - period // 2, (1,)).astype(jnp.int32)
    table = col_table(first, period, FX + MARGIN)
    turn = row_table(period)

    ahead = jnp.maximum(facet_id - 1, 0)
    listed = lax.dynamic_index_in_dim(intersection_rows, ahead, 0, keepdims=False)
    in_use = lax.dynamic_index_in_dim(intersection_count, ahead, 0, keepdims=False)
    in_use = jnp.where(facet_id > 0, in_use, 0)
    line_ids = jnp.arange(FY, dtype=jnp.int32)
    slot_ids = jnp.arange(intersection_rows.shape[1], dtype=jnp.int32)
    keep = (listed[None, :] == line_ids[:, None]) & (slot_ids[None, :] < in_use)
    keep = jnp.sum(keep.astype(jnp.float32), axis=1, keepdims=True)
    keep = jnp.broadcast_to(keep, (FY, MARGIN))

    def total(*arrays):
        return sum(a.astype(jnp.float32) for a in arrays).astype(jnp.bfloat16)

    place = jnp.stack([core, z1]).astype(jnp.int32)
    keep_own, send_own, keep_other, send_other = grid_rows(place, sub_ids, taps, rows, row_len)
    far = total(send_own, swap(send_other, "core"))
    own = total(keep_own, swap(keep_other, "core"), swap(far, "z1"))
    scale = 1.0 / math.sqrt(groups * facets * row_len)

    image = None
    mine = [own, swap(own, "z1")]
    for z_step in range(upper):
        here = mine if z_step == 0 else [shift(piece, "z0", z_step) for piece in mine]
        for x_step in range(east):
            pieces = here if x_step == 0 else [shift(piece, "x", x_step) for piece in here]
            share = lax.rem(z0 + upper - z_step, upper) * east + lax.rem(x + east - x_step, east)
            spot = jnp.stack([share, z1]).astype(jnp.int32)
            image = add_image(
                image, spot, pieces, turn, table, keep, own_chans * num_pols, scale
            )
    return image.reshape(own_chans, num_pols, FY, FX)


def solution(mesh):
    groups, facets = mesh.shape["chan"], mesh.shape["facet"]
    inner = Mesh(
        mesh.devices.reshape(groups // 2, 2, 2, 2, facets // 4), CHAN + FACET
    )
    return jax.shard_map(
        shards,
        mesh=inner,
        in_specs=(
            P(None, None, CHAN, FACET),
            P(),
            P(None, FACET),
            P(None, None, FACET),
            P(None, FACET),
            P(),
            P(),
        ),
        out_specs=P(CHAN, None, None, FACET),
        check_vma=False,
    )
```

time: 426 us -> 122 us (0.29)
  blocking collectives: 168 us -> 0 us
  matrix products: 75.8 us -> 0 us
  other arithmetic: 78.2 us -> 8.59 us
  local copies, waits for them, and re-layouts: 69.1 us -> 8.77 us
  Pallas kernels: 0 us -> 55.1 us
  waiting for transfers between devices: 18.1 us -> 31 us
  starting transfers between devices: 5.84 us -> 16.8 us
  loops' own time: 8.9 us -> 0 us
    psum x1 -> x0, blocking collectives: 168 us -> none  [shards(): summed = lax.psum(partial_sum, 'facet')]
    dot_general x13 -> x0, matrix products: 72.2 us -> none  [the longest x4 37 us: add_group(): jnp.einsum('grycv,grvx->cyx', row_piece, col_table, preferred_element_typ...]
    convert_element_type x25 -> x3, other arithmetic: 62.3 us -> 1.36 us  [the longest x2 1.15 us: total(): return sum((a.astype(jnp.float32) for a in arrays)).astype(jnp.bfloat16)]
    pallas_call x0 -> x6, Pallas kernels: none -> 55.1 us  [the longest x4 28.2 us: add_image(): pl.pallas_call(functools.partial(image_kernel, parts=parts, scale=scale),...]
    while x28 -> x0, local copies, waits for them, and re-layouts: 19.7 us -> none
    convert_element_type x8 -> x3, local copies, waits for them, and re-layouts: 11.5 us -> 0.74 us  [the longest x2 0.66 us: row_table(): return turn.reshape(SETS, 2 * FY, PACK * 2 * SG).astype(jnp.bfloat16)]
    ppermute x1 -> x10, starting transfers between devices: 1.47 us -> 10.6 us  [shift(): lax.ppermute(block, axis, [(i, (i + distance) % size) for i in range(size)])]
    another operation x2 -> x0, loops' own time: 8.9 us -> none  [the longest x1 8.86 us: shards(): grid_parts = lax.map(grid_group, jnp.arange(groups, dtype=jnp.int32))]
  transfers between devices with their start and end apart: 2 -> 11, of which waited for: 2 -> 2; matrix products, arithmetic and copies ran while one was open for 2% -> 5% of each run, Pallas kernels for 0% -> 26%
where the time goes in v1:
time: 122 us; the launch traced here: 121 us
  Pallas kernels  55.1 us (45%)
  waiting for transfers between devices  31 us (25%)
  starting transfers between devices  16.8 us (14%)
  local copies, waits for them, and re-layouts  8.77 us (7%)
  other arithmetic  8.59 us (7%)
    pallas_call x4, Pallas kernels, add_image(): pl.pallas_call(functools.partial(image_kernel, parts=parts, scale=scale),...  28.2 us
    all_to_all x1, waiting for transfers between devices, shards(): lax.all_to_all(sent, ('y', 'z0', 'x'), split_axis=0, concat_axis=0, tiled...  19.2 us
    pallas_call x1, Pallas kernels, grid_rows(): pl.pallas_call(functools.partial(grid_kernel, row_len=row_len), out_shape...  16.3 us
    ppermute x10, waiting for transfers between devices, shift(): lax.ppermute(block, axis, [(i, (i + distance) % size) for i in range(size)])  11.8 us
    pallas_call x1, Pallas kernels, col_table(): pl.pallas_call(functools.partial(table_kernel, period=period), out_shape=...  10.6 us
    ppermute x10, starting transfers between devices, shift(): lax.ppermute(block, axis, [(i, (i + distance) % size) for i in range(size)])  10.6 us
    all_to_all x1, starting transfers between devices, shards(): lax.all_to_all(sent, ('y', 'z0', 'x'), split_axis=0, concat_axis=0, tiled...  6.18 us
    another operation x4, other arithmetic  5.11 us
  transfers between devices with their start and end apart: 11, of which 2 were waited for; matrix products, arithmetic and copies ran while one was open for 5% of the time, Pallas kernels for 26%

profile of v1, /device:TPU:0, one launch (start us, length us, event | category | flops | bytes accessed | tf_op | source)
XLA Modules:
  0.0 121.2 jit_solution(12520591026927102573)
XLA Ops:
  0.0 1.0 convert_reduce_fusion.1
  1.0 0.9 convert_reduce_fusion.3
  2.0 0.7 fusion.7
  2.9 1.5 %reshape.160 = bf16[2,2,4,1,2,1,4,4096]{7,6,4,2,1,0,5,3:T(4,128)(2,1)S(1)} reshape(bf16[16,8,1,4096]{3,1,2,0:T(8,128)(2,1)} %param.7) | data formatting | bytes 2097152 | tf_op jit(solution)/shard_map/reshape | solution.py:322
  4.3 0.6 copy.38
  5.4 1.1 pad_maximum_fusion
  6.5 6.2 %all-to-all-start = ((bf16[8,16,4992]{2,1,0:T(8,128)(2,1)}), bf16[8,16,4992]{2,1,0:T(8,128)(2,1)S(1)}, u32[]{:S(2)}, u32[]{:S(2)}) async-start(bf16[8,16,4992]{2,1,0:T(8,128)(2,1)} %pad_maximum_fusion), calls=%async_computation | async-start | bytes 2555904 | tf_op jit(solution)/shard_map/all_to_all | solution.py:336
  12.8 19.2 %all-to-all-done.rows_ref = bf16[8,16,4992]{2,1,0:T(8,128)(2,1)S(1)} async-done(((bf16[8,16,4992]{2,1,0:T(8,128)(2,1)}), bf16[8,16,4992]{2,1,0:T(8,128)(2,1)S(1)}, u32[]{:S(2)}, u32[]{:S(2)}) %all-to-all-start) | async-done | bytes 1277984 | tf_op jit(solution)/shard_map/all_to_all | solution.py:336
  32.5 16.3 %grid_rows.1 = (bf16[2,8,64,128]{3,2,1,0:T(8,128)(2,1)S(1)}, bf16[2,8,64,128]{3,2,1,0:T(8,128)(2,1)S(1)}, bf16[2,8,64,128]{3,2,1,0:T(8,128)(2,1)S(1)}, bf16[2,8,64,128]{3,2,1,0:T(8,128)(2,1)S(1)}) custom-call(s32[2]{0:T(128)S(1)} %pad_add_fusion.1.place_ref, s32[64]{0:T(128)S(1)} %reshape.166.sub_ref, f32[16,128]{1,0:T(8,128)S(1)} %pad_convert_fusion.taps_ref, ...), custom_call_target="tpu_custom_call" | custom-call | flops 2147483648 | bytes 3145728 | tf_op jit(solution)/shard_map/grid_rows/pallas_call | solution.py:133
  48.8 2.5 %negate_convert_fusion = (bf16[32,64,1,32]{1,3,2,0:T(8,128)(2,1)S(1)}, bf16[32,64,1,32]{1,3,2,0:T(8,128)(2,1)S(1)}, bf16[32,64,1,32]{1,3,2,0:T(8,128)(2,1)S(1)}) fusion(s32[64]{0:T(128)S(1)} %iota_add_fusion.1, s32[32,32]{1,0:T(8,128)S(1)} %iota_add_fusion), kind=kLoop, calls=%fused_computation.13 | loop fusion | flops 1179648 | bytes 397568 | tf_op jit(solution)/shard_map/convert.12
  51.3 0.6 dynamic_slice.21
  53.5 2.6 %collective-permute-start.2 = (bf16[2,8,64,128]{3,2,1,0:T(8,128)(2,1)S(1)}, bf16[2,8,64,128]{3,2,1,0:T(8,128)(2,1)S(1)}, u32[]{:S(2)}, u32[]{:S(2)}) collective-permute-start(bf16[2,8,64,128]{3,2,1,0:T(8,128)(2,1)S(1)} %add_convert_fusion.1), channel_id=1, source_target_pairs={{0,4},{4,0},{1,5},{5,1},{2,6},{6,2},{3,7},{7,3},{8,12},{12,8},{9,1... | collective-permute-start | bytes 786440 | tf_op jit(solution)/shard_map/ppermute | solution.py:31
  56.4 11.7 %collective-permute-done.2 = bf16[2,8,64,128]{3,2,1,0:T(8,128)(2,1)S(1)} collective-permute-done((bf16[2,8,64,128]{3,2,1,0:T(8,128)(2,1)S(1)}, bf16[2,8,64,128]{3,2,1,0:T(8,128)(2,1)S(1)}, u32[]{:S(2)}, u32[]{:S(2)}) %collective-permute-start.2) | collective-permute-done | bytes 262176 | tf_op jit(solution)/shard_map/ppermute | solution.py:31
  68.1 1.1 add_convert_fusion.refs_0_
  69.4 3.1 %collective-permute-start.3 = (bf16[2,8,64,128]{3,2,1,0:T(8,128)(2,1)S(1)}, bf16[2,8,64,128]{3,2,1,0:T(8,128)(2,1)S(1)}, u32[]{:S(2)}, u32[]{:S(2)}) collective-permute-start(bf16[2,8,64,128]{3,2,1,0:T(8,128)(2,1)S(1)} %add_convert_fusion.refs_0_), channel_id=1, source_target_pairs={{0,2},{2,0},{1,3},{3,1},{4,6},{6,4},{5,7},{7,5},{8,10},{10,8},{9,1... | collective-permute-start | bytes 786440 | tf_op jit(solution)/shard_map/ppermute | solution.py:31
  72.6 1.1 copy.29
  74.3 10.6 %col_table.1.refs_3_.refs_4_ = bf16[2048,2176]{1,0:T(8,128)(2,1)} custom-call(s32[1]{0:T(128)} %bitcast.12.first_ref), custom_call_target="tpu_custom_call" | custom-call | flops 35651584 | bytes 8912896 | tf_op jit(solution)/shard_map/col_table/pallas_call | solution.py:182
  85.1 2.0 %collective-permute-start.9 = (bf16[2,8,64,128]{3,2,1,0:T(8,128)(2,1)S(1)}, bf16[2,8,64,128]{3,2,1,0:T(8,128)(2,1)S(1)}, u32[]{:S(2)}, u32[]{:S(2)}) collective-permute-start(bf16[2,8,64,128]{3,2,1,0:T(8,128)(2,1)S(1)} %collective-permute-done.5.refs_1_), channel_id=1, source_target_pairs={{0,1},{1,0},{2,3},{3,2},{4,5},{5,4},{6,7},{7,6},{8,9},{9,8},{10,11... | collective-permute-start | bytes 786440 | tf_op jit(solution)/shard_map/ppermute | solution.py:31
  87.4 3.5 %copy-done.1 = bf16[2048,2176]{1,0:T(8,128)(2,1)S(1)} copy-done((bf16[2048,2176]{1,0:T(8,128)(2,1)S(1)}, bf16[2048,2176]{1,0:T(8,128)(2,1)}, u32[]{:S(2)}) %copy-start.1) | copy-done | bytes 8912920
  91.0 7.1 %add_image.4.refs_6_ = f32[16,64,2048]{2,1,0:T(8,128)} custom-call(s32[2]{0:T(128)S(1)} %pad_add_fusion.4.place_ref, bf16[2,8,64,128]{3,2,1,0:T(8,128)(2,1)S(1)} %add_convert_fusion.refs_0_, bf16[2,8,64,128]{3,2,1,0:T(8,128)(2,1)S(1)} %collective-permute-done.5.refs_1_, bf16[8,128,256]{2,1,0:T(8,128)(2,1)S(1)} %copy.33.refs_2_, ...), custom_call_target="tpu_custom_call" | custom-call | flops 2147483648 | bytes 10485760 | tf_op jit(solution)/shard_map/add_image/pallas_call | solution.py:281
  98.0 1.9 %collective-permute-start.7 = (bf16[2,8,64,128]{3,2,1,0:T(8,128)(2,1)S(1)}, bf16[2,8,64,128]{3,2,1,0:T(8,128)(2,1)S(1)}, u32[]{:S(2)}, u32[]{:S(2)}) collective-permute-start(bf16[2,8,64,128]{3,2,1,0:T(8,128)(2,1)S(1)} %collective-permute-done.6.refs_1_), channel_id=1, source_target_pairs={{0,1},{1,0},{2,3},{3,2},{4,5},{5,4},{6,7},{7,6},{8,9},{9,8},{10,11... | collective-permute-start | bytes 786440 | tf_op jit(solution)/shard_map/ppermute | solution.py:31
  100.0 7.1 %add_image.5.refs_6_ = f32[16,64,2048]{2,1,0:T(8,128)} custom-call(s32[2]{0:T(128)S(1)} %pad_add_fusion.3.place_ref, bf16[2,8,64,128]{3,2,1,0:T(8,128)(2,1)S(1)} %collective-permute-done.8.refs_0_, bf16[2,8,64,128]{3,2,1,0:T(8,128)(2,1)S(1)} %collective-permute-done.9.refs_1_, ...), custom_call_target="tpu_custom_call", output_to_operand_aliasing={{}: (7, {})} | custom-call | flops 2147483648 | bytes 10485760 | tf_op jit(solution)/shard_map/add_image/pallas_call | solution.py:281
  107.1 7.1 %add_image.6.refs_6_ = f32[16,64,2048]{2,1,0:T(8,128)} custom-call(s32[2]{0:T(128)S(1)} %pad_add_fusion.2.place_ref, bf16[2,8,64,128]{3,2,1,0:T(8,128)(2,1)S(1)} %collective-permute-done.3.refs_0_, bf16[2,8,64,128]{3,2,1,0:T(8,128)(2,1)S(1)} %collective-permute-done.6.refs_1_, ...), custom_call_target="tpu_custom_call", output_to_operand_aliasing={{}: (7, {})} | custom-call | flops 2147483648 | bytes 10485760 | tf_op jit(solution)/shard_map/add_image/pallas_call | solution.py:281
  114.1 7.1 %add_image.7 = f32[16,64,2048]{2,1,0:T(8,128)} custom-call(s32[2]{0:T(128)S(1)} %pad_add_fusion.place_ref, bf16[2,8,64,128]{3,2,1,0:T(8,128)(2,1)S(1)} %collective-permute-done.4.refs_0_, bf16[2,8,64,128]{3,2,1,0:T(8,128)(2,1)S(1)} %collective-permute-done.7.refs_1_, bf16[8,128,256]{2,1,0:T(8,128)(2,1)S(1)} %copy.33.refs_2_, ...), custom_call_target="tpu_custom_call", output_to_operand_aliasing={{}: (7, {})} | custom-call | flops 2147483648 | bytes 10485760 | tf_op jit(solution)/shard_map/add_image/pallas_call | solution.py:281
  (53 shorter events, 3.7 us)
Async XLA Ops:
  0.0 56.1 %copy-start = (s32[8,32]{1,0:T(8,128)S(1)}, s32[8,32]{1,0:T(8,128)}, u32[]{:S(2)}) copy-start(s32[8,32]{1,0:T(8,128)} %param.12) | copy-start | bytes 3076
  5.3 7.4 %copy-start.2 = (bf16[32,2,8]{0,2,1:T(8,128)(2,1)S(1)}, bf16[32,2,8]{0,2,1:T(8,128)(2,1)}, u32[]{:S(2)}) copy-start(bf16[32,2,8]{0,2,1:T(8,128)(2,1)} %param.8) | copy-start | bytes 3076
  6.5 25.6 %all-to-all-start = ((bf16[8,16,4992]{2,1,0:T(8,128)(2,1)}), bf16[8,16,4992]{2,1,0:T(8,128)(2,1)S(1)}, u32[]{:S(2)}, u32[]{:S(2)}) async-start(bf16[8,16,4992]{2,1,0:T(8,128)(2,1)} %pad_maximum_fusion), calls=%async_computation | async-start | bytes 2555904 | tf_op jit(solution)/shard_map/all_to_all | solution.py:336
  32.5 18.9 %copy-start.3 = (s32[8]{0:T(128)S(1)}, s32[8]{0:T(128)}, u32[]{:S(2)}) copy-start(s32[8]{0:T(128)} %param.13) | copy-start | bytes 100
  48.7 4.7 %collective-permute-start.1 = (bf16[2,8,64,128]{3,2,1,0:T(8,128)(2,1)S(1)}, bf16[2,8,64,128]{3,2,1,0:T(8,128)(2,1)S(1)}, u32[]{:S(2)}, u32[]{:S(2)}) collective-permute-start(bf16[2,8,64,128]{3,2,1,0:T(8,128)(2,1)S(1)} %get-tuple-element.12), channel_id=1, source_target_pairs={{0,8},{8,0},{1,9},{9,1},{2,10},{10,2},{3,11},{11,3},{4,12},{12,4},... | collective-permute-start | bytes 786440 | tf_op jit(solution)/shard_map/ppermute | solution.py:31
  52.9 3.5 %collective-permute-start = (bf16[2,8,64,128]{3,2,1,0:T(8,128)(2,1)S(1)}, bf16[2,8,64,128]{3,2,1,0:T(8,128)(2,1)}, u32[]{:S(2)}, u32[]{:S(2)}) collective-permute-start(bf16[2,8,64,128]{3,2,1,0:T(8,128)(2,1)S(1)} %get-tuple-element.10), channel_id=1, source_target_pairs={{0,8},{8,0},{1,9},{9,1},{2,10},{10,2},{3,11},{11,3},{4,12},{12,4},... | collective-permute-start | bytes 786440 | tf_op jit(solution)/shard_map/ppermute | solution.py:31
  53.5 14.6 %collective-permute-start.2 = (bf16[2,8,64,128]{3,2,1,0:T(8,128)(2,1)S(1)}, bf16[2,8,64,128]{3,2,1,0:T(8,128)(2,1)S(1)}, u32[]{:S(2)}, u32[]{:S(2)}) collective-permute-start(bf16[2,8,64,128]{3,2,1,0:T(8,128)(2,1)S(1)} %add_convert_fusion.1), channel_id=1, source_target_pairs={{0,4},{4,0},{1,5},{5,1},{2,6},{6,2},{3,7},{7,3},{8,12},{12,8},{9,1... | collective-permute-start | bytes 786440 | tf_op jit(solution)/shard_map/ppermute | solution.py:31
  69.2 15.9 %collective-permute-start.5 = (bf16[2,8,64,128]{3,2,1,0:T(8,128)(2,1)S(1)}, bf16[2,8,64,128]{3,2,1,0:T(8,128)(2,1)S(1)}, u32[]{:S(2)}, u32[]{:S(2)}) collective-permute-start(bf16[2,8,64,128]{3,2,1,0:T(8,128)(2,1)S(1)} %add_convert_fusion.refs_0_), channel_id=1, source_target_pairs={{0,4},{4,0},{1,5},{5,1},{2,6},{6,2},{3,7},{7,3},{8,12},{12,8},{9,1... | collective-permute-start | bytes 786440 | tf_op jit(solution)/shard_map/ppermute | solution.py:31
  69.4 17.9 %collective-permute-start.3 = (bf16[2,8,64,128]{3,2,1,0:T(8,128)(2,1)S(1)}, bf16[2,8,64,128]{3,2,1,0:T(8,128)(2,1)S(1)}, u32[]{:S(2)}, u32[]{:S(2)}) collective-permute-start(bf16[2,8,64,128]{3,2,1,0:T(8,128)(2,1)S(1)} %add_convert_fusion.refs_0_), channel_id=1, source_target_pairs={{0,2},{2,0},{1,3},{3,1},{4,6},{6,4},{5,7},{7,5},{8,10},{10,8},{9,1... | collective-permute-start | bytes 786440 | tf_op jit(solution)/shard_map/ppermute | solution.py:31
  85.1 14.9 %collective-permute-start.8 = (bf16[2,8,64,128]{3,2,1,0:T(8,128)(2,1)S(1)}, bf16[2,8,64,128]{3,2,1,0:T(8,128)(2,1)S(1)}, u32[]{:S(2)}, u32[]{:S(2)}) collective-permute-start(bf16[2,8,64,128]{3,2,1,0:T(8,128)(2,1)S(1)} %add_convert_fusion.refs_0_), channel_id=1, source_target_pairs={{0,1},{1,0},{2,3},{3,2},{4,5},{5,4},{6,7},{7,6},{8,9},{9,8},{10,11... | collective-permute-start | bytes 786440 | tf_op jit(solution)/shard_map/ppermute | solution.py:31
  85.1 14.8 %collective-permute-start.9 = (bf16[2,8,64,128]{3,2,1,0:T(8,128)(2,1)S(1)}, bf16[2,8,64,128]{3,2,1,0:T(8,128)(2,1)S(1)}, u32[]{:S(2)}, u32[]{:S(2)}) collective-permute-start(bf16[2,8,64,128]{3,2,1,0:T(8,128)(2,1)S(1)} %collective-permute-done.5.refs_1_), channel_id=1, source_target_pairs={{0,1},{1,0},{2,3},{3,2},{4,5},{5,4},{6,7},{7,6},{8,9},{9,8},{10,11... | collective-permute-start | bytes 786440 | tf_op jit(solution)/shard_map/ppermute | solution.py:31
  87.2 10.9 %collective-permute-start.6 = (bf16[2,8,64,128]{3,2,1,0:T(8,128)(2,1)S(1)}, bf16[2,8,64,128]{3,2,1,0:T(8,128)(2,1)S(1)}, u32[]{:S(2)}, u32[]{:S(2)}) collective-permute-start(bf16[2,8,64,128]{3,2,1,0:T(8,128)(2,1)S(1)} %collective-permute-done.5.refs_1_), channel_id=1, source_target_pairs={{0,2},{2,0},{1,3},{3,1},{4,6},{6,4},{5,7},{7,5},{8,10},{10,8},{9,1... | collective-permute-start | bytes 786440 | tf_op jit(solution)/shard_map/ppermute | solution.py:31
  87.3 26.9 %collective-permute-start.4 = (bf16[2,8,64,128]{3,2,1,0:T(8,128)(2,1)S(1)}, bf16[2,8,64,128]{3,2,1,0:T(8,128)(2,1)S(1)}, u32[]{:S(2)}, u32[]{:S(2)}) collective-permute-start(bf16[2,8,64,128]{3,2,1,0:T(8,128)(2,1)S(1)} %collective-permute-done.3.refs_0_), channel_id=1, source_target_pairs={{0,1},{1,0},{2,3},{3,2},{4,5},{5,4},{6,7},{7,6},{8,9},{9,8},{10,11... | collective-permute-start | bytes 786440 | tf_op jit(solution)/shard_map/ppermute | solution.py:31
  87.4 3.5 %copy-start.1 = (bf16[2048,2176]{1,0:T(8,128)(2,1)S(1)}, bf16[2048,2176]{1,0:T(8,128)(2,1)}, u32[]{:S(2)}) copy-start(bf16[2048,2176]{1,0:T(8,128)(2,1)} %col_table.1.refs_3_.refs_4_) | copy-start | bytes 26738692
  98.0 16.1 %collective-permute-start.7 = (bf16[2,8,64,128]{3,2,1,0:T(8,128)(2,1)S(1)}, bf16[2,8,64,128]{3,2,1,0:T(8,128)(2,1)S(1)}, u32[]{:S(2)}, u32[]{:S(2)}) collective-permute-start(bf16[2,8,64,128]{3,2,1,0:T(8,128)(2,1)S(1)} %collective-permute-done.6.refs_1_), channel_id=1, source_target_pairs={{0,1},{1,0},{2,3},{3,2},{4,5},{5,4},{6,7},{7,6},{8,9},{9,8},{10,11... | collective-permute-start | bytes 786440 | tf_op jit(solution)/shard_map/ppermute | solution.py:31

commit v2 on v1

v2 whole, which is shorter than its diff:
```python
import functools
import math

import jax
import jax.numpy as jnp
from jax import lax
from jax.experimental import pallas as pl
from jax.experimental.pallas import tpu as pltpu
from jax.sharding import Mesh
from jax.sharding import PartitionSpec as P

BLK = 512
SG = 32
NSUB = 32
FX = 2048
FY = 64
MARGIN = 128
LANES = 128
PACK = LANES // SG
SETS = NSUB // PACK
CHAN = ("y", "core")
FACET = ("z1", "z0", "x")


def swap(block, axis):
    return lax.ppermute(block, axis, [(0, 1), (1, 0)])


def pack_kernel(group_ref, vis_ref, plane_ref, cell_ref, sub_ref, first_ref, second_ref, *, shares):
    chan_shares, pol_shares, per_chan, per_pol, cores = shares
    num_pols = vis_ref.shape[1] // 2
    row_len = vis_ref.shape[2]
    lines = first_ref.shape[1]
    width = row_len // lines
    half = per_pol // 2
    group = group_ref[0]

    def folded(row):
        row = row.astype(jnp.float32)
        return jnp.concatenate([row[:, k * width : (k + 1) * width] for k in range(lines)], axis=0)

    subs = sub_ref[pl.ds(group, 1), :].astype(jnp.float32)
    subs = jnp.concatenate([subs, jnp.zeros((1, LANES - subs.shape[1]), jnp.float32)], axis=1)
    ids = [
        folded(plane_ref[pl.ds(group, 1), :]),
        folded(cell_ref[0, pl.ds(group, 1), :]),
        folded(cell_ref[1, pl.ds(group, 1), :]),
        jnp.broadcast_to(subs, (lines, LANES)),
    ]
    ids = jnp.concatenate(ids, axis=1).astype(jnp.bfloat16)
    dest = 0
    for north in range(first_ref.shape[0] // (chan_shares * pol_shares)):
        for chan_share in range(chan_shares):
            for pol_share in range(pol_shares):
                found = ([], [])
                for core in range(cores):
                    chans = (north * cores + core) * chan_shares + chan_share
                    chans = [
                        vis_ref[chans * per_chan + k].astype(jnp.float32) for k in range(per_chan)
                    ]
                    for part in range(2):
                        start = part * num_pols + pol_share * per_pol
                        for vis in chans:
                            found[0].append(vis[start : start + half])
                            found[1].append(vis[start + half : start + per_pol])
                first_ref[dest, :, :row_len] = jnp.concatenate(found[0], 0).astype(jnp.bfloat16)
                first_ref[dest, :, row_len:] = ids
                second_ref[dest] = jnp.concatenate(found[1], 0).astype(jnp.bfloat16)
                dest += 1


def pack_rows(group, vis, planes, cells, subs, shares, dests, lines):
    row_len = vis.shape[2]
    extra = 3 * row_len // lines + LANES
    vmem = pl.BlockSpec(memory_space=pltpu.VMEM)
    return pl.pallas_call(
        functools.partial(pack_kernel, shares=shares),
        out_shape=[
            jax.ShapeDtypeStruct((dests, lines, row_len + extra), jnp.bfloat16),
            jax.ShapeDtypeStruct((dests, lines, row_len), jnp.bfloat16),
        ],
        grid_spec=pltpu.PrefetchScalarGridSpec(
            num_scalar_prefetch=1, grid=(), in_specs=[vmem] * 4, out_specs=[vmem] * 2
        ),
        compiler_params=pltpu.CompilerParams(vmem_limit_bytes=24 << 20),
        cost_estimate=pl.CostEstimate(flops=1 << 20, bytes_accessed=3 << 20, transcendentals=0),
        name="pack_rows",
    )(group, vis, planes, cells, subs)


def grid_kernel(place_ref, sub_ref, taps_ref, ids_ref, rows_ref, *refs, row_len, ids_from):
    own_ref, other_ref, sums_ref = refs[-3:]
    step = pl.program_id(0)
    lines = rows_ref.shape[1]
    pols = lines // 4
    cells = 2 * pols * SG
    blocks = row_len // BLK
    width = row_len // lines

    @pl.when(step == 0)
    def _():
        sums_ref[...] = jnp.zeros_like(sums_ref)

    taps = taps_ref[...]
    ids = ids_ref[0, :, ids_from : ids_from + 3 * width].astype(jnp.float32).astype(jnp.int32)
    cell = lax.broadcasted_iota(jnp.int32, (8, BLK), 0)

    def listed(kind, block):
        found = []
        for start in range(block * BLK, (block + 1) * BLK, min(BLK, width)):
            line, column = start // width, kind * width + start % width
            found.append(ids[line : line + 1, column : column + min(BLK, width)])
        return jnp.concatenate(found, axis=1) if len(found) > 1 else found[0]

    def pick(values, index, axis):
        found = [
            jnp.take_along_axis(
                values if axis else values[:, c : c + LANES], index[:, c : c + LANES], axis=axis
            )
            for c in range(0, BLK, LANES)
        ]
        return jnp.concatenate(found, axis=1)

    def spread(values, offset):
        distance = cell - offset
        keep = [
            (distance + 8 * tile >= 0) & (distance + 8 * tile < 8) for tile in range(SG // 8)
        ]
        turned = [pick(values[8 * q : 8 * q + 8], distance & 7, 0) for q in range(2)]
        return [
            jnp.concatenate([jnp.where(m, part, 0.0) for m in keep], axis=0) for part in turned
        ]

    for block in range(blocks):
        plane = jnp.broadcast_to(listed(0, block), (16, BLK))
        values = pick(taps, plane, 1)
        left = jnp.concatenate(spread(values, listed(1, block)), axis=0).astype(jnp.bfloat16)
        kern_re, kern_im = spread(values, listed(2, block))
        vis = rows_ref[0, :, block * BLK : (block + 1) * BLK].astype(jnp.float32)
        vis = pltpu.roll(vis, place_ref[0] * (lines // 2), 0)
        real, imag = [], []
        for first in (0, 2 * pols):
            for row in range(first, first + pols):
                vis_re = vis[row : row + 1]
                vis_im = vis[row + pols : row + pols + 1]
                real.append((vis_re * kern_re - vis_im * kern_im).astype(jnp.bfloat16))
                imag.append((vis_re * kern_im + vis_im * kern_re).astype(jnp.bfloat16))
        weighted = jnp.concatenate(real + imag, axis=0)
        sub = sub_ref[step * blocks + block]
        sums_ref[sub] += lax.dot_general(
            left, weighted, (((1,), (1,)), ((), ())), preferred_element_type=jnp.float32
        )

    @pl.when(step == pl.num_programs(0) - 1)
    def _():
        slot = lax.broadcasted_iota(jnp.int32, (2 * SG, LANES), 1) // SG

        def finish(group, carry):
            parts = []
            for k in range(PACK):
                raw = sums_ref[group * PACK + k]
                real = raw[:SG, :cells] - raw[SG:, cells:]
                imag = raw[:SG, cells:] + raw[SG:, :cells]
                part = jnp.concatenate([real, imag], axis=0)
                if cells < LANES:
                    part = jnp.concatenate([part, jnp.zeros_like(part)], axis=1)
                parts.append(part)
            for pol in range(2 * pols):
                tile = slice(pol // PACK * LANES, (pol // PACK + 1) * LANES)
                packed = jnp.zeros((2 * SG, LANES), jnp.float32)
                for k in range(PACK):
                    move = (k - pol) % PACK * SG
                    part = parts[k][:, tile]
                    part = pltpu.roll(part, move, 1) if move else part
                    packed = jnp.where(slot == k, part, packed)
                out_ref = own_ref if pol < pols else other_ref
                out_ref[pol % pols, group] = packed.astype(jnp.bfloat16)
            return carry

        lax.fori_loop(0, SETS, finish, 0)


def grid_rows(place, sub_ids, taps, ids, rows, row_len, token):
    sources, lines, _ = rows.shape
    pols = lines // 4
    shape = (pols, SETS, 2 * SG, LANES)
    whole = pl.BlockSpec(shape, lambda s, *_: (0, 0, 0, 0))
    flops = 2 * sources * row_len * 2 * SG * 4 * pols * SG
    return pl.pallas_call(
        functools.partial(grid_kernel, row_len=row_len, ids_from=row_len),
        out_shape=[jax.ShapeDtypeStruct(shape, jnp.bfloat16)] * 2,
        grid_spec=pltpu.PrefetchScalarGridSpec(
            num_scalar_prefetch=2,
            grid=(sources,),
            in_specs=[
                pl.BlockSpec(taps.shape, lambda s, *_: (0, 0)),
                pl.BlockSpec((1,) + ids.shape[1:], lambda s, *_: (s, 0, 0)),
                pl.BlockSpec((1,) + rows.shape[1:], lambda s, *_: (s, 0, 0)),
                pl.BlockSpec(memory_space=pl.ANY),
            ],
            out_specs=[whole] * 2,
            scratch_shapes=[pltpu.VMEM((NSUB, 2 * SG, 4 * pols * SG), jnp.float32)],
        ),
        compiler_params=pltpu.CompilerParams(vmem_limit_bytes=16 << 20),
        cost_estimate=pl.CostEstimate(
            flops=flops * 8, bytes_accessed=2 << 20, transcendentals=0
        ),
        name="grid_rows",
    )(place, sub_ids, taps, ids, rows, token)


def tables_kernel(facet_ref, listed_ref, count_ref, table_ref, turn_ref, keep_ref, *, period):
    facet = facet_ref[0]
    span = period // SG
    unit = 2.0 * math.pi / period

    def angle(phase):
        return jnp.mod(phase, period).astype(jnp.float32) * unit

    cells = PACK * SG
    row = lax.broadcasted_iota(jnp.int32, (cells, LANES), 0)
    lane = lax.broadcasted_iota(jnp.int32, (cells, LANES), 1)
    tiles = table_ref.shape[1] // LANES
    start = facet * FX - period // 2 + jnp.where(lane == tiles - 1, -MARGIN, lane * LANES)
    turn_shape = (2 * FY, 2 * PACK * SG)
    turn_row = lax.broadcasted_iota(jnp.int32, turn_shape, 0)
    turn_lane = lax.broadcasted_iota(jnp.int32, turn_shape, 1)

    def group_tables(group, carry):
        sub = group * PACK + row // SG
        cell = (lax.rem(sub * 53 + 5, span) - span // 2) * SG + row % SG
        fine, coarse = angle(cell * lane), angle(cell * start)
        fine_cos, fine_sin = jnp.cos(fine), jnp.sin(fine)
        coarse_cos, coarse_sin = jnp.cos(coarse), jnp.sin(coarse)
        base = pl.multiple_of(group * 2 * cells, 2 * cells)
        for tile in range(tiles):
            columns = slice(tile * LANES, (tile + 1) * LANES)
            tile_cos = coarse_cos[:, tile : tile + 1]
            tile_sin = coarse_sin[:, tile : tile + 1]
            full_cos = tile_cos * fine_cos - tile_sin * fine_sin
            full_sin = tile_sin * fine_cos + tile_cos * fine_sin
            table_ref[pl.ds(base, cells), columns] = full_cos.astype(jnp.bfloat16)
            table_ref[pl.ds(base + cells, cells), columns] = (-full_sin).astype(jnp.bfloat16)
        sub = group * PACK + turn_lane // (2 * SG)
        cell = (lax.rem(sub * 37, span) - span // 2) * SG + turn_lane % SG
        quarter = turn_lane // SG % 2 - turn_row // FY
        phase = cell * (turn_row % FY - FY // 2) + quarter * (period // 4)
        turn_ref[group] = jnp.cos(angle(phase)).astype(jnp.bfloat16)
        return carry

    lax.fori_loop(0, SETS, group_tables, 0)
    line = lax.broadcasted_iota(jnp.int32, (FY, MARGIN), 0)
    before = jnp.maximum(facet - 1, 0)
    in_use = jnp.where(facet > 0, count_ref[before], 0)

    def mark(k, keep):
        return jnp.where((line == listed_ref[before, k]) & (k < in_use), 1.0, keep)

    keep_ref[...] = lax.fori_loop(
        0, listed_ref.shape[1], mark, jnp.zeros((FY, MARGIN), jnp.float32)
    )


def make_tables(facet, listed, counts, period):
    depth, width = 2 * NSUB * SG, FX + MARGIN
    vmem = pl.BlockSpec(memory_space=pltpu.VMEM)
    return pl.pallas_call(
        functools.partial(tables_kernel, period=period),
        out_shape=[
            jax.ShapeDtypeStruct((depth, width), jnp.bfloat16),
            jax.ShapeDtypeStruct((SETS, 2 * FY, 2 * PACK * SG), jnp.bfloat16),
            jax.ShapeDtypeStruct((FY, MARGIN), jnp.float32),
        ],
        grid_spec=pltpu.PrefetchScalarGridSpec(
            num_scalar_prefetch=3, grid=(), in_specs=[], out_specs=[vmem] * 3
        ),
        compiler_params=pltpu.CompilerParams(vmem_limit_bytes=16 << 20),
        cost_estimate=pl.CostEstimate(
            flops=8 * depth * width, bytes_accessed=2 * depth * width, transcendentals=1 << 19
        ),
        name="make_tables",
    )(facet, listed, counts)


def image_kernel(place_ref, *refs, parts, scale, columns):
    piece_refs = refs[:parts]
    turn_ref, table_ref, keep_ref = refs[parts : parts + 3]
    out_ref, lines_ref, done_ref, sems = refs[-4:]
    per = piece_refs[0].shape[0]
    width = table_ref.shape[1] - MARGIN
    slot = lax.broadcasted_iota(jnp.int32, (2 * SG, 2 * LANES), 1) % LANES // SG
    flat = [(part, i) for part in range(parts) for i in range(per)]

    def group_rows(group, carry):
        base = pl.multiple_of(group * 2 * LANES, 2 * LANES)
        for k in range(0, len(flat), 2):
            pair = [piece_refs[part][i, group] for part, i in flat[k : k + 2]]
            pair = jnp.concatenate(pair, axis=1)
            zero = jnp.zeros_like(pair)
            spread = [jnp.where(slot == s, pair, zero) for s in range(PACK)]
            spread = jnp.concatenate(spread, axis=0)
            turned = jnp.dot(turn_ref[group], spread, preferred_element_type=jnp.float32)
            turned = (turned * scale).astype(jnp.bfloat16)
            for m in range(2):
                for q in range(2):
                    lines_ref[
                        (k + m) * FY : (k + m + 1) * FY, pl.ds(base + q * LANES, LANES)
                    ] = turned[q * FY : (q + 1) * FY, m * LANES : (m + 1) * LANES]
        return carry

    lax.fori_loop(0, SETS, group_rows, 0)
    lines = lines_ref[...]

    def copy(step, part):
        return pltpu.make_async_copy(
            done_ref.at[step % 2, pl.ds(part * per, per)],
            out_ref.at[pl.ds(place_ref[part], per), :, pl.ds(step * columns, columns)],
            sems.at[step % 2, part],
        )

    steps = width // columns
    for step in range(steps):
        if step >= 2:
            for part in range(parts):
                copy(step - 2, part).wait()
        block = table_ref[:, step * columns : (step + 1) * columns]
        total = jnp.dot(lines, block, preferred_element_type=jnp.float32)
        done_ref[step % 2] = total.reshape(parts * per, FY, columns)
        if step == 0:
            edge = jnp.dot(lines, table_ref[:, width:], preferred_element_type=jnp.float32)
            edge = edge.reshape(parts * per, FY, MARGIN) * keep_ref[...][None]
            done_ref[0, :, :, :MARGIN] += edge
        for part in range(parts):
            copy(step, part).start()
    for step in range(max(steps - 2, 0), steps):
        for part in range(parts):
            copy(step, part).wait()


def add_image(image, place, pieces, turn, table, keep, total_pols, scale):
    parts, per = len(pieces), pieces[0].shape[0]
    pols = parts * per
    columns = 512
    depth = table.shape[0]
    width = table.shape[1] - MARGIN
    vmem = pl.BlockSpec(memory_space=pltpu.VMEM)
    operands = [*pieces, turn, table, keep]
    in_specs = [vmem] * len(operands)
    aliases = {}
    if image is not None:
        operands.append(image)
        in_specs.append(pl.BlockSpec(memory_space=pl.ANY))
        aliases = {len(operands): 0}
    return pl.pallas_call(
        functools.partial(image_kernel, parts=parts, scale=scale, columns=columns),
        out_shape=jax.ShapeDtypeStruct((total_pols, FY, width), jnp.float32),
        grid_spec=pltpu.PrefetchScalarGridSpec(
            num_scalar_prefetch=1,
            grid=(),
            in_specs=in_specs,
            out_specs=pl.BlockSpec(memory_space=pl.ANY),
            scratch_shapes=[
                pltpu.VMEM((pols * FY, depth), jnp.bfloat16),
                pltpu.VMEM((2, pols, FY, columns), jnp.float32),
                pltpu.SemaphoreType.DMA((2, parts)),
            ],
        ),
        input_output_aliases=aliases,
        compiler_params=pltpu.CompilerParams(vmem_limit_bytes=28 << 20),
        cost_estimate=pl.CostEstimate(
            flops=2 * pols * FY * depth * width,
            bytes_accessed=2 * depth * width + 4 * pols * FY * width,
            transcendentals=0,
        ),
        name="add_image",
    )(place, *operands)


def shards(
    visibilities, w_kernel, w_index, cell_offsets, block_sub, intersection_rows, intersection_count
):
    cores, east = lax.axis_size("core"), lax.axis_size("x")
    north, upper = lax.axis_size("y"), lax.axis_size("z0")
    groups, facets = north * cores, lax.axis_size(FACET)
    num_chans, num_parts, _, row_len = visibilities.shape
    num_pols = num_parts // 2
    own_chans = num_chans // groups
    shares = upper * east
    chan_shares = math.gcd(shares, own_chans)
    pol_shares = shares // chan_shares
    per_chan, per_pol = own_chans // chan_shares, num_pols // pol_shares
    lines = 2 * per_chan * per_pol
    blocks = row_len // BLK
    period = FX * facets
    z0, x = lax.axis_index("z0"), lax.axis_index("x")

    def scalar(value):
        return jnp.reshape(value, (1,)).astype(jnp.int32)

    vis = visibilities.reshape(num_chans, num_parts, row_len)
    sent = pack_rows(
        scalar(lax.axis_index(CHAN)),
        vis,
        w_index,
        cell_offsets,
        block_sub,
        (chan_shares, pol_shares, per_chan, per_pol, cores),
        north * shares,
        lines,
    )
    rows = [
        lax.all_to_all(part, ("y", "z0", "x"), split_axis=0, concat_axis=0, tiled=True)
        for part in sent
    ]
    sub_ids = rows[0][:, 0, -LANES : blocks - LANES].astype(jnp.int32).reshape(-1)
    table, turn, keep = make_tables(
        scalar(lax.axis_index(FACET)), intersection_rows, intersection_count, period
    )
    taps = w_kernel.astype(jnp.float32).transpose(1, 2, 0).reshape(-1, w_kernel.shape[0])
    taps = jnp.pad(taps, ((0, 0), (0, LANES - taps.shape[1])))

    def total(*arrays):
        return sum(a.astype(jnp.float32) for a in arrays).astype(jnp.bfloat16)

    place = scalar(lax.axis_index("core"))
    scale = 1.0 / math.sqrt(groups * facets * row_len)
    image = None
    token = keep
    for half in range(2):
        own, other = grid_rows(place, sub_ids, taps, rows[0], rows[half], row_len, token)
        token = own
        both = total(own, swap(other, "core"))
        mine = total(both, swap(both, "z1"))
        pieces, spots = [], []
        for z_step in range(upper):
            for x_step in range(east):
                route = [
                    (a * east + b, (a + z_step) % upper * east + (b + x_step) % east)
                    for a in range(upper)
                    for b in range(east)
                ]
                piece = lax.ppermute(mine, ("z0", "x"), route) if z_step + x_step else mine
                pieces.append(piece)
                share = lax.rem(z0 + upper - z_step, upper) * east
                share = share + lax.rem(x + east - x_step, east)
                spots.append(share * per_chan * per_pol + half * (per_chan * per_pol // 2))
        spots = jnp.stack(spots).astype(jnp.int32)
        image = add_image(image, spots, pieces, turn, table, keep, own_chans * num_pols, scale)
    return image.reshape(own_chans, num_pols, FY, FX)


def solution(mesh):
    groups, facets = mesh.shape["chan"], mesh.shape["facet"]
    inner = Mesh(
        mesh.devices.reshape(groups // 2, 2, 2, 2, facets // 4), CHAN + FACET
    )
    return jax.shard_map(
        shards,
        mesh=inner,
        in_specs=(
            P(None, None, CHAN, FACET),
            P(),
            P(None, FACET),
            P(None, None, FACET),
            P(None, FACET),
            P(),
            P(),
        ),
        out_specs=P(CHAN, None, None, FACET),
        check_vma=False,
    )
```

time: 122 us -> 117 us (0.959)
  other arithmetic: 8.59 us -> 1.16 us
  starting transfers between devices: 16.8 us -> 23.1 us
  waiting for transfers between devices: 31 us -> 26.3 us
  local copies, waits for them, and re-layouts: 8.77 us -> 12.1 us
  Pallas kernels: 55.1 us -> 53.4 us
    all_to_all x1 -> x2, waiting for transfers between devices: 19.2 us -> 0.01 us  [shards(): lax.all_to_all(part, ('y', 'z0', 'x'), split_axis=0, concat_axis=0, tiled...]
    ppermute x10, waiting for transfers between devices: 11.8 us -> 26.3 us  [the longest x4 18.6 us: swap(): return lax.ppermute(block, axis, [(0, 1), (1, 0)])]
    unnamed x9 -> x16, local copies, waits for them, and re-layouts: 3.56 us -> 12 us
    another operation x11 -> x2, other arithmetic: 5.9 us -> 0.15 us  [shards(): spots = jnp.stack(spots).astype(jnp.int32)]
    all_to_all x1 -> x2, starting transfers between devices: 6.18 us -> 11.3 us  [shards(): lax.all_to_all(part, ('y', 'z0', 'x'), split_axis=0, concat_axis=0, tiled...]
    reshape x3 -> x0, local copies, waits for them, and re-layouts: 2.36 us -> none  [the longest x2 2.08 us: shards(): visibilities.reshape(north, cores, chan_shares, per_chan, 2, pol_shares,...]
    pallas_call x6, Pallas kernels: 55.1 us -> 53.4 us  [the longest x2 19.6 us: grid_rows(): pl.pallas_call(functools.partial(grid_kernel, row_len=row_len, ids_from=r...]
    ppermute x10, starting transfers between devices: 10.6 us -> 11.8 us  [the longest x6 7.55 us: shards(): piece = lax.ppermute(mine, ('z0', 'x'), route) if z_step + x_step else mine]
  transfers between devices with their start and end apart: 11 -> 12, of which waited for: 2 -> 4; matrix products, arithmetic and copies ran while one was open for 5% -> 1% of each run, Pallas kernels for 26% -> 37%
where the time goes in v2:
time: 117 us; the launch traced here: 116 us
  Pallas kernels  53.4 us (46%)
  waiting for transfers between devices  26.3 us (22%)
  starting transfers between devices  23.1 us (20%)
  local copies, waits for them, and re-layouts  12.1 us (10%)
    pallas_call x2, Pallas kernels, grid_rows(): pl.pallas_call(functools.partial(grid_kernel, row_len=row_len, ids_from=r...  19.6 us
    ppermute x4, waiting for transfers between devices, swap(): return lax.ppermute(block, axis, [(0, 1), (1, 0)])  18.6 us
    pallas_call x2, Pallas kernels, add_image(): pl.pallas_call(functools.partial(image_kernel, parts=parts, scale=scale,...  18 us
    pallas_call x1, Pallas kernels, make_tables(): pl.pallas_call(functools.partial(tables_kernel, period=period), out_shape...  14.2 us
    unnamed x16, local copies, waits for them, and re-layouts  12 us
    all_to_all x2, starting transfers between devices, shards(): lax.all_to_all(part, ('y', 'z0', 'x'), split_axis=0, concat_axis=0, tiled...  11.3 us
    ppermute x6, waiting for transfers between devices, shards(): piece = lax.ppermute(mine, ('z0', 'x'), route) if z_step + x_step else mine  7.65 us
    ppermute x6, starting transfers between devices, shards(): piece = lax.ppermute(mine, ('z0', 'x'), route) if z_step + x_step else mine  7.55 us
  transfers between devices with their start and end apart: 12, of which 4 were waited for; matrix products, arithmetic and copies ran while one was open for 1% of the time, Pallas kernels for 37%

profile of v2, /device:TPU:0, one launch (start us, length us, event | category | flops | bytes accessed | tf_op | source)
XLA Modules:
  0.0 116.3 jit_solution(18059864608646256197)
XLA Ops:
  0.0 1.2 %copy-done.2 = bf16[16,8,1,4096]{3,1,2,0:T(8,128)(2,1)S(1)} copy-done((bf16[16,8,1,4096]{3,1,2,0:T(8,128)(2,1)S(1)}, bf16[16,8,1,4096]{3,1,2,0:T(8,128)(2,1)}, u32[]{:S(2)}) %copy-start.2) | copy-done | bytes 1048600
  1.2 0.9 copy-done.3
  2.1 0.8 copy-done.4
  3.7 1.6 %pack_rows.1 = (bf16[8,8,5760]{2,1,0:T(8,128)(2,1)}, bf16[8,8,4096]{2,1,0:T(8,128)(2,1)}) custom-call(s32[1]{0:T(128)} %bitcast.5.group_ref, bf16[16,8,4096]{2,1,0:T(8,128)(2,1)S(1)} %bitcast.16, s32[4,4096]{1,0:T(4,128)S(1)} %copy-done.4, s32[2,4,4096]{2,1,0:T(4,128)S(1)} %copy-done.3, s32[4,8]{1,0:T(4,128)S(1)} %copy-done.5), custom_call_target="tpu_custom_call" | custom-call | flops 1048576 | bytes 3145728 | tf_op jit(solution)/shard_map/pack_rows/pallas_call | solution.py:76
  5.2 6.2 %all-to-all-start = ((bf16[8,8,5760]{2,1,0:T(8,128)(2,1)}), bf16[8,8,5760]{2,1,0:T(8,128)(2,1)S(1)}, u32[]{:S(2)}, u32[]{:S(2)}) async-start(bf16[8,8,5760]{2,1,0:T(8,128)(2,1)} %get-tuple-element.14), calls=%async_computation | async-start | bytes 1474560 | tf_op jit(solution)/shard_map/all_to_all | solution.py:412
  12.7 14.2 %make_tables.1 = (bf16[2048,2176]{1,0:T(8,128)(2,1)S(1)}, bf16[8,128,256]{2,1,0:T(8,128)(2,1)S(1)}, f32[64,128]{1,0:T(8,128)S(1)}) custom-call(s32[1]{0:T(128)} %bitcast.9.facet_ref, s32[8,32]{1,0:T(8,128)S(1)} %copy-done.6, s32[8]{0:T(128)S(1)} %copy-done.7), custom_call_target="tpu_custom_call" | custom-call | flops 35651584 | bytes 8912896 | tf_op jit(solution)/shard_map/make_tables/pallas_call | solution.py:267
  27.0 3.5 %copy-done = bf16[2048,2176]{1,0:T(8,128)(2,1)} copy-done((bf16[2048,2176]{1,0:T(8,128)(2,1)}, bf16[2048,2176]{1,0:T(8,128)(2,1)S(1)}, u32[]{:S(2)}) %copy-start) | copy-done | bytes 8912920
  30.4 0.7 pad_convert_fusion.taps_ref
  31.1 5.1 %all-to-all-start.1 = ((bf16[8,8,4096]{2,1,0:T(8,128)(2,1)}), bf16[8,8,4096]{2,1,0:T(8,128)(2,1)S(1)}, u32[]{:S(2)}, u32[]{:S(2)}) async-start(bf16[8,8,4096]{2,1,0:T(8,128)(2,1)} %get-tuple-element.15), calls=%async_computation.1 | async-start | bytes 1048576 | tf_op jit(solution)/shard_map/all_to_all | solution.py:412
  36.3 9.8 %grid_rows.2 = (bf16[2,8,64,128]{3,2,1,0:T(8,128)(2,1)S(1)}, bf16[2,8,64,128]{3,2,1,0:T(8,128)(2,1)S(1)}) custom-call(s32[1]{0:T(128)} %bitcast.4.place_ref, s32[64]{0:T(128)S(1)} %reshape.29.sub_ref, f32[16,128]{1,0:T(8,128)S(1)} %pad_convert_fusion.taps_ref, bf16[8,8,5760]{2,1,0:T(8,128)(2,1)S(1)} %all-to-all-done.ids_ref.rows_ref, ...), custom_call_target="tpu_custom_call" | custom-call | flops 8589934592 | bytes 2097152 | tf_op jit(solution)/shard_map/grid_rows/pallas_call | solution.py:189
  46.2 9.8 %grid_rows.3 = (bf16[2,8,64,128]{3,2,1,0:T(8,128)(2,1)S(1)}, bf16[2,8,64,128]{3,2,1,0:T(8,128)(2,1)S(1)}) custom-call(s32[1]{0:T(128)} %bitcast.4.place_ref, s32[64]{0:T(128)S(1)} %reshape.29.sub_ref, f32[16,128]{1,0:T(8,128)S(1)} %pad_convert_fusion.taps_ref, bf16[8,8,5760]{2,1,0:T(8,128)(2,1)S(1)} %all-to-all-done.ids_ref.rows_ref, ...), custom_call_target="tpu_custom_call" | custom-call | flops 8589934592 | bytes 2097152 | tf_op jit(solution)/shard_map/grid_rows/pallas_call | solution.py:189
  56.7 2.6 %collective-permute-start.6 = (bf16[2,8,64,128]{3,2,1,0:T(8,128)(2,1)S(1)}, bf16[2,8,64,128]{3,2,1,0:T(8,128)(2,1)S(1)}, u32[]{:S(2)}, u32[]{:S(2)}) collective-permute-start(bf16[2,8,64,128]{3,2,1,0:T(8,128)(2,1)S(1)} %add_convert_fusion.1), channel_id=1, source_target_pairs={{0,4},{4,0},{1,5},{5,1},{2,6},{6,2},{3,7},{7,3},{8,12},{12,8},{9,1... | collective-permute-start | bytes 786440 | tf_op jit(solution)/shard_map/ppermute | solution.py:26
  59.5 1.0 collective-permute-start.1
  60.5 17.5 %collective-permute-done.6 = bf16[2,8,64,128]{3,2,1,0:T(8,128)(2,1)S(1)} collective-permute-done((bf16[2,8,64,128]{3,2,1,0:T(8,128)(2,1)S(1)}, bf16[2,8,64,128]{3,2,1,0:T(8,128)(2,1)S(1)}, u32[]{:S(2)}, u32[]{:S(2)}) %collective-permute-start.6) | collective-permute-done | bytes 262176 | tf_op jit(solution)/shard_map/ppermute | solution.py:26
  78.1 1.4 %collective-permute-start.9 = (bf16[2,8,64,128]{3,2,1,0:T(8,128)(2,1)S(1)}, bf16[2,8,64,128]{3,2,1,0:T(8,128)(2,1)S(1)}, u32[]{:S(2)}, u32[]{:S(2)}) collective-permute-start(bf16[2,8,64,128]{3,2,1,0:T(8,128)(2,1)S(1)} %add_convert_fusion.refs_0_), channel_id=1, source_target_pairs={{0,3},{1,2},{2,1},{3,0},{4,7},{5,6},{6,5},{7,4},{8,11},{9,10},{10,... | collective-permute-start | bytes 786440 | tf_op jit(solution)/shard_map/ppermute | solution.py:442
  79.5 2.2 %collective-permute-start.8 = (bf16[2,8,64,128]{3,2,1,0:T(8,128)(2,1)S(1)}, bf16[2,8,64,128]{3,2,1,0:T(8,128)(2,1)S(1)}, u32[]{:S(2)}, u32[]{:S(2)}) collective-permute-start(bf16[2,8,64,128]{3,2,1,0:T(8,128)(2,1)S(1)} %add_convert_fusion.refs_0_), channel_id=1, source_target_pairs={{0,2},{1,3},{2,0},{3,1},{4,6},{5,7},{6,4},{7,5},{8,10},{9,11},{10,... | collective-permute-start | bytes 786440 | tf_op jit(solution)/shard_map/ppermute | solution.py:442
  81.7 1.1 collective-permute-done.1
  82.9 2.1 %collective-permute-start.4 = (bf16[2,8,64,128]{3,2,1,0:T(8,128)(2,1)S(1)}, bf16[2,8,64,128]{3,2,1,0:T(8,128)(2,1)S(1)}, u32[]{:S(2)}, u32[]{:S(2)}) collective-permute-start(bf16[2,8,64,128]{3,2,1,0:T(8,128)(2,1)S(1)} %add_convert_fusion.2.refs_0_), channel_id=1, source_target_pairs={{0,3},{1,2},{2,1},{3,0},{4,7},{5,6},{6,5},{7,4},{8,11},{9,10},{10,... | collective-permute-start | bytes 786440 | tf_op jit(solution)/shard_map/ppermute | solution.py:442
  85.0 1.4 %collective-permute-start.3 = (bf16[2,8,64,128]{3,2,1,0:T(8,128)(2,1)S(1)}, bf16[2,8,64,128]{3,2,1,0:T(8,128)(2,1)S(1)}, u32[]{:S(2)}, u32[]{:S(2)}) collective-permute-start(bf16[2,8,64,128]{3,2,1,0:T(8,128)(2,1)S(1)} %add_convert_fusion.2.refs_0_), channel_id=1, source_target_pairs={{0,2},{1,3},{2,0},{3,1},{4,6},{5,7},{6,4},{7,5},{8,10},{9,11},{10,... | collective-permute-start | bytes 786440 | tf_op jit(solution)/shard_map/ppermute | solution.py:442
  86.4 3.5 %collective-permute-done.9.refs_3_ = bf16[2,8,64,128]{3,2,1,0:T(8,128)(2,1)S(1)} collective-permute-done((bf16[2,8,64,128]{3,2,1,0:T(8,128)(2,1)S(1)}, bf16[2,8,64,128]{3,2,1,0:T(8,128)(2,1)S(1)}, u32[]{:S(2)}, u32[]{:S(2)}) %collective-permute-start.9) | collective-permute-done | bytes 262176 | tf_op jit(solution)/shard_map/ppermute | solution.py:442
  90.4 4.2 %collective-permute-done.8.refs_2_ = bf16[2,8,64,128]{3,2,1,0:T(8,128)(2,1)S(1)} collective-permute-done((bf16[2,8,64,128]{3,2,1,0:T(8,128)(2,1)S(1)}, bf16[2,8,64,128]{3,2,1,0:T(8,128)(2,1)S(1)}, u32[]{:S(2)}, u32[]{:S(2)}) %collective-permute-start.8) | collective-permute-done | bytes 262176 | tf_op jit(solution)/shard_map/ppermute | solution.py:442
  94.5 3.5 %copy-done.1 = bf16[2048,2176]{1,0:T(8,128)(2,1)S(1)} copy-done((bf16[2048,2176]{1,0:T(8,128)(2,1)S(1)}, bf16[2048,2176]{1,0:T(8,128)(2,1)}, u32[]{:S(2)}) %copy-start.1) | copy-done | bytes 8912920
  98.1 9.0 %add_image.2.refs_7_ = f32[16,64,2048]{2,1,0:T(8,128)} custom-call(s32[4]{0:T(128)S(1)} %pad_add_fusion.1.place_ref, bf16[2,8,64,128]{3,2,1,0:T(8,128)(2,1)S(1)} %add_convert_fusion.refs_0_, bf16[2,8,64,128]{3,2,1,0:T(8,128)(2,1)S(1)} %collective-permute-done.7.refs_1_, bf16[2,8,64,128]{3,2,1,0:T(8,128)(2,1)S(1)} %collective-permute-done.8.refs_2_, ...), custom_call_target="tpu_custom_call" | custom-call | flops 4294967296 | bytes 12582912 | tf_op jit(solution)/shard_map/add_image/pallas_call | solution.py:354
  107.1 9.0 %add_image.3 = f32[16,64,2048]{2,1,0:T(8,128)} custom-call(s32[4]{0:T(128)S(1)} %pad_add_fusion.place_ref, bf16[2,8,64,128]{3,2,1,0:T(8,128)(2,1)S(1)} %add_convert_fusion.2.refs_0_, bf16[2,8,64,128]{3,2,1,0:T(8,128)(2,1)S(1)} %collective-permute-done.2.refs_1_, ...), custom_call_target="tpu_custom_call", output_to_operand_aliasing={{}: (8, {})} | custom-call | flops 4294967296 | bytes 12582912 | tf_op jit(solution)/shard_map/add_image/pallas_call | solution.py:354
  (31 shorter events, 3.7 us)
Async XLA Ops:
  0.0 1.2 %copy-start.2 = (bf16[16,8,1,4096]{3,1,2,0:T(8,128)(2,1)S(1)}, bf16[16,8,1,4096]{3,1,2,0:T(8,128)(2,1)}, u32[]{:S(2)}) copy-start(bf16[16,8,1,4096]{3,1,2,0:T(8,128)(2,1)} %param.7) | copy-start | bytes 3145732
  1.2 0.9 copy-start.3
  2.1 0.8 copy-start.4
  3.0 0.7 copy-start.5
  5.2 25.9 %all-to-all-start = ((bf16[8,8,5760]{2,1,0:T(8,128)(2,1)}), bf16[8,8,5760]{2,1,0:T(8,128)(2,1)S(1)}, u32[]{:S(2)}, u32[]{:S(2)}) async-start(bf16[8,8,5760]{2,1,0:T(8,128)(2,1)} %get-tuple-element.14), calls=%async_computation | async-start | bytes 1474560 | tf_op jit(solution)/shard_map/all_to_all | solution.py:412
  11.4 0.7 copy-start.6
  12.1 0.7 copy-start.7
  27.0 3.5 %copy-start = (bf16[2048,2176]{1,0:T(8,128)(2,1)}, bf16[2048,2176]{1,0:T(8,128)(2,1)S(1)}, u32[]{:S(2)}) copy-start(bf16[2048,2176]{1,0:T(8,128)(2,1)S(1)} %get-tuple-element.21.refs_5_) | copy-start | bytes 26738692
  31.1 15.1 %all-to-all-start.1 = ((bf16[8,8,4096]{2,1,0:T(8,128)(2,1)}), bf16[8,8,4096]{2,1,0:T(8,128)(2,1)S(1)}, u32[]{:S(2)}, u32[]{:S(2)}) async-start(bf16[8,8,4096]{2,1,0:T(8,128)(2,1)} %get-tuple-element.15), calls=%async_computation.1 | async-start | bytes 1048576 | tf_op jit(solution)/shard_map/all_to_all | solution.py:412
  46.1 10.5 %collective-permute-start.5 = (bf16[2,8,64,128]{3,2,1,0:T(8,128)(2,1)S(1)}, bf16[2,8,64,128]{3,2,1,0:T(8,128)(2,1)S(1)}, u32[]{:S(2)}, u32[]{:S(2)}) collective-permute-start(bf16[2,8,64,128]{3,2,1,0:T(8,128)(2,1)S(1)} %get-tuple-element.22), channel_id=1, source_target_pairs={{0,8},{8,0},{1,9},{9,1},{2,10},{10,2},{3,11},{11,3},{4,12},{12,4},... | collective-permute-start | bytes 786440 | tf_op jit(solution)/shard_map/ppermute | solution.py:26
  56.0 3.4 %collective-permute-start = (bf16[2,8,64,128]{3,2,1,0:T(8,128)(2,1)S(1)}, bf16[2,8,64,128]{3,2,1,0:T(8,128)(2,1)S(1)}, u32[]{:S(2)}, u32[]{:S(2)}) collective-permute-start(bf16[2,8,64,128]{3,2,1,0:T(8,128)(2,1)S(1)} %get-tuple-element.19), channel_id=1, source_target_pairs={{0,8},{8,0},{1,9},{9,1},{2,10},{10,2},{3,11},{11,3},{4,12},{12,4},... | collective-permute-start | bytes 786440 | tf_op jit(solution)/shard_map/ppermute | solution.py:26
  56.7 21.4 %collective-permute-start.6 = (bf16[2,8,64,128]{3,2,1,0:T(8,128)(2,1)S(1)}, bf16[2,8,64,128]{3,2,1,0:T(8,128)(2,1)S(1)}, u32[]{:S(2)}, u32[]{:S(2)}) collective-permute-start(bf16[2,8,64,128]{3,2,1,0:T(8,128)(2,1)S(1)} %add_convert_fusion.1), channel_id=1, source_target_pairs={{0,4},{4,0},{1,5},{5,1},{2,6},{6,2},{3,7},{7,3},{8,12},{12,8},{9,1... | collective-permute-start | bytes 786440 | tf_op jit(solution)/shard_map/ppermute | solution.py:26
  59.5 23.3 %collective-permute-start.1 = (bf16[2,8,64,128]{3,2,1,0:T(8,128)(2,1)S(1)}, bf16[2,8,64,128]{3,2,1,0:T(8,128)(2,1)S(1)}, u32[]{:S(2)}, u32[]{:S(2)}) collective-permute-start(bf16[2,8,64,128]{3,2,1,0:T(8,128)(2,1)S(1)} %add_convert_fusion.3), channel_id=1, source_target_pairs={{0,4},{4,0},{1,5},{5,1},{2,6},{6,2},{3,7},{7,3},{8,12},{12,8},{9,1... | collective-permute-start | bytes 786440 | tf_op jit(solution)/shard_map/ppermute | solution.py:26
  78.1 11.8 %collective-permute-start.9 = (bf16[2,8,64,128]{3,2,1,0:T(8,128)(2,1)S(1)}, bf16[2,8,64,128]{3,2,1,0:T(8,128)(2,1)S(1)}, u32[]{:S(2)}, u32[]{:S(2)}) collective-permute-start(bf16[2,8,64,128]{3,2,1,0:T(8,128)(2,1)S(1)} %add_convert_fusion.refs_0_), channel_id=1, source_target_pairs={{0,3},{1,2},{2,1},{3,0},{4,7},{5,6},{6,5},{7,4},{8,11},{9,10},{10,... | collective-permute-start | bytes 786440 | tf_op jit(solution)/shard_map/ppermute | solution.py:442
  79.5 15.1 %collective-permute-start.8 = (bf16[2,8,64,128]{3,2,1,0:T(8,128)(2,1)S(1)}, bf16[2,8,64,128]{3,2,1,0:T(8,128)(2,1)S(1)}, u32[]{:S(2)}, u32[]{:S(2)}) collective-permute-start(bf16[2,8,64,128]{3,2,1,0:T(8,128)(2,1)S(1)} %add_convert_fusion.refs_0_), channel_id=1, source_target_pairs={{0,2},{1,3},{2,0},{3,1},{4,6},{5,7},{6,4},{7,5},{8,10},{9,11},{10,... | collective-permute-start | bytes 786440 | tf_op jit(solution)/shard_map/ppermute | solution.py:442
  81.7 12.9 %collective-permute-start.7 = (bf16[2,8,64,128]{3,2,1,0:T(8,128)(2,1)S(1)}, bf16[2,8,64,128]{3,2,1,0:T(8,128)(2,1)S(1)}, u32[]{:S(2)}, u32[]{:S(2)}) collective-permute-start(bf16[2,8,64,128]{3,2,1,0:T(8,128)(2,1)S(1)} %add_convert_fusion.refs_0_), channel_id=1, source_target_pairs={{0,1},{1,0},{2,3},{3,2},{4,5},{5,4},{6,7},{7,6},{8,9},{9,8},{10,11... | collective-permute-start | bytes 786440 | tf_op jit(solution)/shard_map/ppermute | solution.py:442
  82.9 24.2 %collective-permute-start.4 = (bf16[2,8,64,128]{3,2,1,0:T(8,128)(2,1)S(1)}, bf16[2,8,64,128]{3,2,1,0:T(8,128)(2,1)S(1)}, u32[]{:S(2)}, u32[]{:S(2)}) collective-permute-start(bf16[2,8,64,128]{3,2,1,0:T(8,128)(2,1)S(1)} %add_convert_fusion.2.refs_0_), channel_id=1, source_target_pairs={{0,3},{1,2},{2,1},{3,0},{4,7},{5,6},{6,5},{7,4},{8,11},{9,10},{10,... | collective-permute-start | bytes 786440 | tf_op jit(solution)/shard_map/ppermute | solution.py:442
  85.0 22.1 %collective-permute-start.3 = (bf16[2,8,64,128]{3,2,1,0:T(8,128)(2,1)S(1)}, bf16[2,8,64,128]{3,2,1,0:T(8,128)(2,1)S(1)}, u32[]{:S(2)}, u32[]{:S(2)}) collective-permute-start(bf16[2,8,64,128]{3,2,1,0:T(8,128)(2,1)S(1)} %add_convert_fusion.2.refs_0_), channel_id=1, source_target_pairs={{0,2},{1,3},{2,0},{3,1},{4,6},{5,7},{6,4},{7,5},{8,10},{9,11},{10,... | collective-permute-start | bytes 786440 | tf_op jit(solution)/shard_map/ppermute | solution.py:442
  89.9 17.2 %collective-permute-start.2 = (bf16[2,8,64,128]{3,2,1,0:T(8,128)(2,1)S(1)}, bf16[2,8,64,128]{3,2,1,0:T(8,128)(2,1)S(1)}, u32[]{:S(2)}, u32[]{:S(2)}) collective-permute-start(bf16[2,8,64,128]{3,2,1,0:T(8,128)(2,1)S(1)} %add_convert_fusion.2.refs_0_), channel_id=1, source_target_pairs={{0,1},{1,0},{2,3},{3,2},{4,5},{5,4},{6,7},{7,6},{8,9},{9,8},{10,11... | collective-permute-start | bytes 786440 | tf_op jit(solution)/shard_map/ppermute | solution.py:442
  94.5 3.5 %copy-start.1 = (bf16[2048,2176]{1,0:T(8,128)(2,1)S(1)}, bf16[2048,2176]{1,0:T(8,128)(2,1)}, u32[]{:S(2)}) copy-start(bf16[2048,2176]{1,0:T(8,128)(2,1)} %copy-done) | copy-start | bytes 26738692

commit v3 on v2

--- a/solution.py
+++ b/solution.py
@@ -19,6 +19,7 @@
 PACK = LANES // SG
 SETS = NSUB // PACK
 CHAN = ("y", "core")
+VMEM_LIMIT = 56 << 20
 FACET = ("z1", "z0", "x")
 
 
@@ -26,7 +27,10 @@
     return lax.ppermute(block, axis, [(0, 1), (1, 0)])
 
 
-def pack_kernel(group_ref, vis_ref, plane_ref, cell_ref, sub_ref, first_ref, second_ref, *, shares):
+def pack_kernel(
+    group_ref, vis_from, plane_from, cell_from, sub_from, first_ref, second_ref, *refs, shares
+):
+    vis_ref, plane_ref, cell_ref, sub_ref, sems, vis_sems = refs
     chan_shares, pol_shares, per_chan, per_pol, cores = shares
     num_pols = vis_ref.shape[1] // 2
     row_len = vis_ref.shape[2]
@@ -34,6 +38,20 @@
     width = row_len // lines
     half = per_pol // 2
     group = group_ref[0]
+    small = [(plane_from, plane_ref), (cell_from, cell_ref), (sub_from, sub_ref)]
+    small = [pltpu.make_async_copy(*pair, sems.at[k]) for k, pair in enumerate(small)]
+    dests = first_ref.shape[0]
+    step = vis_ref.shape[0] // (dests // (chan_shares * pol_shares))
+    large = []
+    for k in range(vis_ref.shape[0] // step):
+        chans = pl.ds(k * step, step)
+        large.append(
+            pltpu.make_async_copy(vis_from.at[chans], vis_ref.at[chans], vis_sems.at[k])
+        )
+    for copy in small + large:
+        copy.start()
+    for copy in small:
+        copy.wait()
 
     def folded(row):
         row = row.astype(jnp.float32)
@@ -49,7 +67,8 @@
     ]
     ids = jnp.concatenate(ids, axis=1).astype(jnp.bfloat16)
     dest = 0
-    for north in range(first_ref.shape[0] // (chan_shares * pol_shares)):
+    for north, copy in enumerate(large):
+        copy.wait()
         for chan_share in range(chan_shares):
             for pol_share in range(pol_shares):
                 found = ([], [])
@@ -72,6 +91,7 @@
 def pack_rows(group, vis, planes, cells, subs, shares, dests, lines):
     row_len = vis.shape[2]
     extra = 3 * row_len // lines + LANES
+    norths = dests // (shares[0] * shares[1])
     vmem = pl.BlockSpec(memory_space=pltpu.VMEM)
     return pl.pallas_call(
         functools.partial(pack_kernel, shares=shares),
@@ -80,9 +100,14 @@
             jax.ShapeDtypeStruct((dests, lines, row_len), jnp.bfloat16),
         ],
         grid_spec=pltpu.PrefetchScalarGridSpec(
-            num_scalar_prefetch=1, grid=(), in_specs=[vmem] * 4, out_specs=[vmem] * 2
-        ),
-        compiler_params=pltpu.CompilerParams(vmem_limit_bytes=24 << 20),
+            num_scalar_prefetch=1,
+            grid=(),
+            in_specs=[pl.BlockSpec(memory_space=pl.ANY)] * 4,
+            out_specs=[vmem] * 2,
+            scratch_shapes=[pltpu.VMEM(a.shape, a.dtype) for a in (vis, planes, cells, subs)]
+            + [pltpu.SemaphoreType.DMA((3,)), pltpu.SemaphoreType.DMA((norths,))],
+        ),
+        compiler_params=pltpu.CompilerParams(vmem_limit_bytes=VMEM_LIMIT),
         cost_estimate=pl.CostEstimate(flops=1 << 20, bytes_accessed=3 << 20, transcendentals=0),
         name="pack_rows",
     )(group, vis, planes, cells, subs)
@@ -180,7 +205,7 @@
         lax.fori_loop(0, SETS, finish, 0)
 
 
-def grid_rows(place, sub_ids, taps, ids, rows, row_len, token):
+def grid_rows(place, sub_ids, taps, ids, rows, row_len, after):
     sources, lines, _ = rows.shape
     pols = lines // 4
     shape = (pols, SETS, 2 * SG, LANES)
@@ -196,8 +221,8 @@
                 pl.BlockSpec(taps.shape, lambda s, *_: (0, 0)),
                 pl.BlockSpec((1,) + ids.shape[1:], lambda s, *_: (s, 0, 0)),
                 pl.BlockSpec((1,) + rows.shape[1:], lambda s, *_: (s, 0, 0)),
-                pl.BlockSpec(memory_space=pl.ANY),
-            ],
+            ]
+            + [pl.BlockSpec(memory_space=pl.ANY)] * len(after),
             out_specs=[whole] * 2,
             scratch_shapes=[pltpu.VMEM((NSUB, 2 * SG, 4 * pols * SG), jnp.float32)],
         ),
@@ -206,80 +231,124 @@
             flops=flops * 8, bytes_accessed=2 << 20, transcendentals=0
         ),
         name="grid_rows",
-    )(place, sub_ids, taps, ids, rows, token)
-
-
-def tables_kernel(facet_ref, listed_ref, count_ref, table_ref, turn_ref, keep_ref, *, period):
+    )(place, sub_ids, taps, ids, rows, *after)
+
+
+def add_kernel(*refs, terms):
+    total = refs[0][...].astype(jnp.float32)
+    for ref in refs[1:terms]:
+        total = total + ref[...].astype(jnp.float32)
+    refs[-1][...] = total.astype(jnp.bfloat16)
+
+
+def add(terms, after=()):
+    vmem = pl.BlockSpec(memory_space=pltpu.VMEM)
+    return pl.pallas_call(
+        functools.partial(add_kernel, terms=len(terms)),
+        out_shape=jax.ShapeDtypeStruct(terms[0].shape, jnp.bfloat16),
+        in_specs=[vmem] * len(terms) + [pl.BlockSpec(memory_space=pl.ANY)] * len(after),
+        out_specs=vmem,
+        compiler_params=pltpu.CompilerParams(vmem_limit_bytes=4 << 20),
+        cost_estimate=pl.CostEstimate(flops=1 << 18, bytes_accessed=4 << 20, transcendentals=0),
+        name="add_sums",
+    )(*terms, *after)
+
+
+def wrapped(value, period):
+    if period & (period - 1):
+        return jnp.mod(value, period)
+    return value & (period - 1)
+
+
+def circle(phase, period):
+    phase = wrapped(phase, period)
+    quarter = lax.div(phase + period // 8, period // 4)
+    rest = phase - quarter * (period // 4)
+    angle = rest.astype(jnp.float32) * (2.0 * math.pi / period)
+    square = angle * angle
+    sin = -1.0 / 5040 + square * (1.0 / 362880)
+    sin = -1.0 / 6 + square * (1.0 / 120 + square * sin)
+    sin = angle + angle * square * sin
+    cos = -1.0 / 720 + square * (1.0 / 40320)
+    cos = 1.0 + square * (-0.5 + square * (1.0 / 24 + square * cos))
+    odd = (quarter & 1) == 1
+    full_cos, full_sin = jnp.where(odd, sin, cos), jnp.where(odd, cos, sin)
+    full_cos = jnp.where(((quarter + 1) & 2) == 2, -full_cos, full_cos)
+    return full_cos, jnp.where((quarter & 2) == 2, -full_sin, full_sin)
+
+
+def tables_kernel(facet_ref, listed_ref, count_ref, *refs, period):
+    table_ref, turn_ref, keep_ref = refs[-3:]
     facet = facet_ref[0]
+    group = pl.program_id(0)
     span = period // SG
-    unit = 2.0 * math.pi / period
-
-    def angle(phase):
-        return jnp.mod(phase, period).astype(jnp.float32) * unit
-
     cells = PACK * SG
     row = lax.broadcasted_iota(jnp.int32, (cells, LANES), 0)
     lane = lax.broadcasted_iota(jnp.int32, (cells, LANES), 1)
     tiles = table_ref.shape[1] // LANES
     start = facet * FX - period // 2 + jnp.where(lane == tiles - 1, -MARGIN, lane * LANES)
+    sub = group * PACK + (row >> 5)
+    cell = (wrapped(sub * 53 + 5, span) - span // 2) * SG + (row & (SG - 1))
+    fine_cos, fine_sin = circle(cell * lane, period)
+    coarse_cos, coarse_sin = circle(cell * start, period)
+    for tile in range(tiles):
+        columns = slice(tile * LANES, (tile + 1) * LANES)
+        tile_cos = coarse_cos[:, tile : tile + 1]
+        tile_sin = coarse_sin[:, tile : tile + 1]
+        full_cos = tile_cos * fine_cos - tile_sin * fine_sin
+        full_sin = tile_sin * fine_cos + tile_cos * fine_sin
+        table_ref[:cells, columns] = full_cos.astype(jnp.bfloat16)
+        table_ref[cells:, columns] = (-full_sin).astype(jnp.bfloat16)
+
     turn_shape = (2 * FY, 2 * PACK * SG)
-    turn_row = lax.broadcasted_iota(jnp.int32, turn_shape, 0)
-    turn_lane = lax.broadcasted_iota(jnp.int32, turn_shape, 1)
-
-    def group_tables(group, carry):
-        sub = group * PACK + row // SG
-        cell = (lax.rem(sub * 53 + 5, span) - span // 2) * SG + row % SG
-        fine, coarse = angle(cell * lane), angle(cell * start)
-        fine_cos, fine_sin = jnp.cos(fine), jnp.sin(fine)
-        coarse_cos, coarse_sin = jnp.cos(coarse), jnp.sin(coarse)
-        base = pl.multiple_of(group * 2 * cells, 2 * cells)
-        for tile in range(tiles):
-            columns = slice(tile * LANES, (tile + 1) * LANES)
-            tile_cos = coarse_cos[:, tile : tile + 1]
-            tile_sin = coarse_sin[:, tile : tile + 1]
-            full_cos = tile_cos * fine_cos - tile_sin * fine_sin
-            full_sin = tile_sin * fine_cos + tile_cos * fine_sin
-            table_ref[pl.ds(base, cells), columns] = full_cos.astype(jnp.bfloat16)
-            table_ref[pl.ds(base + cells, cells), columns] = (-full_sin).astype(jnp.bfloat16)
-        sub = group * PACK + turn_lane // (2 * SG)
-        cell = (lax.rem(sub * 37, span) - span // 2) * SG + turn_lane % SG
-        quarter = turn_lane // SG % 2 - turn_row // FY
-        phase = cell * (turn_row % FY - FY // 2) + quarter * (period // 4)
-        turn_ref[group] = jnp.cos(angle(phase)).astype(jnp.bfloat16)
-        return carry
-
-    lax.fori_loop(0, SETS, group_tables, 0)
-    line = lax.broadcasted_iota(jnp.int32, (FY, MARGIN), 0)
-    before = jnp.maximum(facet - 1, 0)
-    in_use = jnp.where(facet > 0, count_ref[before], 0)
-
-    def mark(k, keep):
-        return jnp.where((line == listed_ref[before, k]) & (k < in_use), 1.0, keep)
-
-    keep_ref[...] = lax.fori_loop(
-        0, listed_ref.shape[1], mark, jnp.zeros((FY, MARGIN), jnp.float32)
-    )
-
-
-def make_tables(facet, listed, counts, period):
+    row = lax.broadcasted_iota(jnp.int32, turn_shape, 0)
+    lane = lax.broadcasted_iota(jnp.int32, turn_shape, 1)
+    sub = group * PACK + (lane >> 6)
+    cell = (wrapped(sub * 37, span) - span // 2) * SG + (lane & (SG - 1))
+    quarter = (lane >> 5 & 1) - (row >> 6)
+    phase = cell * ((row & (FY - 1)) - FY // 2) + quarter * (period // 4)
+    turn_ref[0] = circle(phase, period)[0].astype(jnp.bfloat16)
+
+    @pl.when(group == 0)
+    def _():
+        line = lax.broadcasted_iota(jnp.int32, (FY, MARGIN), 0)
+        before = jnp.maximum(facet - 1, 0)
+        in_use = jnp.where(facet > 0, count_ref[before], 0)
+
+        def mark(k, keep):
+            return jnp.where((line == listed_ref[before, k]) & (k < in_use), 1.0, keep)
+
+        keep_ref[...] = lax.fori_loop(
+            0, listed_ref.shape[1], mark, jnp.zeros((FY, MARGIN), jnp.float32)
+        )
+
+
+def make_tables(facet, listed, counts, period, token):
     depth, width = 2 * NSUB * SG, FX + MARGIN
-    vmem = pl.BlockSpec(memory_space=pltpu.VMEM)
+    turn = (1, 2 * FY, 2 * PACK * SG)
     return pl.pallas_call(
         functools.partial(tables_kernel, period=period),
         out_shape=[
             jax.ShapeDtypeStruct((depth, width), jnp.bfloat16),
-            jax.ShapeDtypeStruct((SETS, 2 * FY, 2 * PACK * SG), jnp.bfloat16),
+            jax.ShapeDtypeStruct((SETS,) + turn[1:], jnp.bfloat16),
             jax.ShapeDtypeStruct((FY, MARGIN), jnp.float32),
         ],
         grid_spec=pltpu.PrefetchScalarGridSpec(
-            num_scalar_prefetch=3, grid=(), in_specs=[], out_specs=[vmem] * 3
+            num_scalar_prefetch=3,
+            grid=(SETS,),
+            in_specs=[pl.BlockSpec(memory_space=pl.ANY)],
+            out_specs=[
+                pl.BlockSpec((depth // SETS, width), lambda g, *_: (g, 0)),
+                pl.BlockSpec(turn, lambda g, *_: (g, 0, 0)),
+                pl.BlockSpec((FY, MARGIN), lambda g, *_: (0, 0)),
+            ],
         ),
         compiler_params=pltpu.CompilerParams(vmem_limit_bytes=16 << 20),
         cost_estimate=pl.CostEstimate(
             flops=8 * depth * width, bytes_accessed=2 * depth * width, transcendentals=1 << 19
         ),
         name="make_tables",
-    )(facet, listed, counts)
+    )(facet, listed, counts, token)
 
 
 def image_kernel(place_ref, *refs, parts, scale, columns):
@@ -337,7 +406,7 @@
             copy(step, part).wait()
 
 
-def add_image(image, place, pieces, turn, table, keep, total_pols, scale):
+def add_image(image, place, pieces, turn, table, keep, total_pols, scale, after):
     parts, per = len(pieces), pieces[0].shape[0]
     pols = parts * per
     columns = 512
@@ -346,6 +415,8 @@
     vmem = pl.BlockSpec(memory_space=pltpu.VMEM)
     operands = [*pieces, turn, table, keep]
     in_specs = [vmem] * len(operands)
+    operands.extend(after)
+    in_specs.extend([pl.BlockSpec(memory_space=pl.ANY)] * len(after))
     aliases = {}
     if image is not None:
         operands.append(image)
@@ -413,25 +484,18 @@
         for part in sent
     ]
     sub_ids = rows[0][:, 0, -LANES : blocks - LANES].astype(jnp.int32).reshape(-1)
-    table, turn, keep = make_tables(
-        scalar(lax.axis_index(FACET)), intersection_rows, intersection_count, period
-    )
     taps = w_kernel.astype(jnp.float32).transpose(1, 2, 0).reshape(-1, w_kernel.shape[0])
     taps = jnp.pad(taps, ((0, 0), (0, LANES - taps.shape[1])))
 
-    def total(*arrays):
-        return sum(a.astype(jnp.float32) for a in arrays).astype(jnp.bfloat16)
-
     place = scalar(lax.axis_index("core"))
     scale = 1.0 / math.sqrt(groups * facets * row_len)
-    image = None
-    token = keep
-    for half in range(2):
-        own, other = grid_rows(place, sub_ids, taps, rows[0], rows[half], row_len, token)
-        token = own
-        both = total(own, swap(other, "core"))
-        mine = total(both, swap(both, "z1"))
-        pieces, spots = [], []
+
+    def gridded(half, after):
+        own, other = grid_rows(place, sub_ids, taps, rows[0], rows[half], row_len, after)
+        return own, swap(other, "core")
+
+    def gathered(mine):
+        pieces = [mine]
         for z_step in range(upper):
             for x_step in range(east):
                 route = [
@@ -439,13 +503,37 @@
                     for a in range(upper)
                     for b in range(east)
                 ]
-                piece = lax.ppermute(mine, ("z0", "x"), route) if z_step + x_step else mine
-                pieces.append(piece)
+                if z_step + x_step:
+                    pieces.append(lax.ppermute(mine, ("z0", "x"), route))
+        return pieces
+
+    def spots(half):
+        found = []
+        for z_step in range(upper):
+            for x_step in range(east):
                 share = lax.rem(z0 + upper - z_step, upper) * east
                 share = share + lax.rem(x + east - x_step, east)
-                spots.append(share * per_chan * per_pol + half * (per_chan * per_pol // 2))
-        spots = jnp.stack(spots).astype(jnp.int32)
-        image = add_image(image, spots, pieces, turn, table, keep, own_chans * num_pols, scale)
+                found.append(share * per_chan * per_pol + half * (per_chan * per_pol // 2))
+        return jnp.stack(found).astype(jnp.int32)
+
+    first = add(gridded(0, ()))
+    first_far = swap(first, "z1")
+    second = gridded(1, (first,))
+    first = add((first, first_far), second[:1])
+    second = add(second, (first,))
+    second_far = swap(second, "z1")
+    first_pieces = gathered(first)
+    table, turn, keep = make_tables(
+        scalar(lax.axis_index(FACET)), intersection_rows, intersection_count, period, first
+    )
+    second = add((second, second_far))
+    second_pieces = gathered(second)
+    total_pols = own_chans * num_pols
+    image = None
+    for half, pieces, after in ((0, first_pieces, (second,)), (1, second_pieces, ())):
+        image = add_image(
+            image, spots(half), pieces, turn, table, keep, total_pols, scale, after
+        )
     return image.reshape(own_chans, num_pols, FY, FX)
 
 

time: 117 us -> 92.2 us (0.79)
  local copies, waits for them, and re-layouts: 12.1 us -> 0.09 us
  waiting for transfers between devices: 26.3 us -> 18.8 us
  Pallas kernels: 53.4 us -> 49.8 us
    ppermute x4, waiting for transfers between devices: 18.6 us -> 3.82 us  [swap(): return lax.ppermute(block, axis, [(0, 1), (1, 0)])]
    unnamed x16 -> x4, local copies, waits for them, and re-layouts: 12 us -> 0.01 us
    all_to_all x2, waiting for transfers between devices: 0.01 us -> 11.7 us  [shards(): lax.all_to_all(part, ('y', 'z0', 'x'), split_axis=0, concat_axis=0, tiled...]
    pallas_call x1, Pallas kernels: 14.2 us -> 8.91 us  [make_tables(): pl.pallas_call(functools.partial(tables_kernel, period=period), out_shape...]
    ppermute x6, waiting for transfers between devices: 7.65 us -> 3.32 us  [gathered(): pieces.append(lax.ppermute(mine, ('z0', 'x'), route))]
    ppermute x6, starting transfers between devices: 7.55 us -> 9.59 us  [gathered(): pieces.append(lax.ppermute(mine, ('z0', 'x'), route))]
    all_to_all x2, starting transfers between devices: 11.3 us -> 9.69 us  [shards(): lax.all_to_all(part, ('y', 'z0', 'x'), split_axis=0, concat_axis=0, tiled...]
    ppermute x4, starting transfers between devices: 4.28 us -> 2.87 us  [swap(): return lax.ppermute(block, axis, [(0, 1), (1, 0)])]
  transfers between devices with their start and end apart: 12 -> 12, of which waited for: 4 -> 5; matrix products, arithmetic and copies ran while one was open for 1% -> 1% of each run, Pallas kernels for 37% -> 41%
where the time goes in v3:
time: 92.2 us; the launch traced here: 91.8 us
  Pallas kernels  49.8 us (54%)
  starting transfers between devices  22.1 us (24%)
  waiting for transfers between devices  18.8 us (20%)
    pallas_call x2, Pallas kernels, grid_rows(): pl.pallas_call(functools.partial(grid_kernel, row_len=row_len, ids_from=r...  19.8 us
    pallas_call x2, Pallas kernels, add_image(): pl.pallas_call(functools.partial(image_kernel, parts=parts, scale=scale,...  18.1 us
    all_to_all x2, waiting for transfers between devices, shards(): lax.all_to_all(part, ('y', 'z0', 'x'), split_axis=0, concat_axis=0, tiled...  11.7 us
    all_to_all x2, starting transfers between devices, shards(): lax.all_to_all(part, ('y', 'z0', 'x'), split_axis=0, concat_axis=0, tiled...  9.69 us
    ppermute x6, starting transfers between devices, gathered(): pieces.append(lax.ppermute(mine, ('z0', 'x'), route))  9.59 us
    pallas_call x1, Pallas kernels, make_tables(): pl.pallas_call(functools.partial(tables_kernel, period=period), out_shape...  8.91 us
    ppermute x4, waiting for transfers between devices, swap(): return lax.ppermute(block, axis, [(0, 1), (1, 0)])  3.82 us
    ppermute x6, waiting for transfers between devices, gathered(): pieces.append(lax.ppermute(mine, ('z0', 'x'), route))  3.32 us
  transfers between devices with their start and end apart: 12, of which 5 were waited for; matrix products, arithmetic and copies ran while one was open for 1% of the time, Pallas kernels for 41%

profile of v3, /device:TPU:0, one launch (start us, length us, event | category | flops | bytes accessed | tf_op | source)
XLA Modules:
  0.0 91.8 jit_solution(8917535067291500930)
XLA Ops:
  0.0 2.7 %pack_rows.1 = (bf16[8,8,5760]{2,1,0:T(8,128)(2,1)}, bf16[8,8,4096]{2,1,0:T(8,128)(2,1)}) custom-call(s32[1]{0:T(128)} %bitcast.5.group_ref, bf16[16,8,4096]{2,1,0:T(8,128)(2,1)} %bitcast.16, s32[4,4096]{1,0:T(4,128)} %plane_from.1, s32[2,4,4096]{2,1,0:T(4,128)} %cell_from.1, s32[4,8]{1,0:T(4,128)} %sub_from.1), custom_call_target="tpu_custom_call" | custom-call | flops 1048576 | bytes 3145728 | tf_op jit(solution)/shard_map/pack_rows/pallas_call | solution.py:96
  2.7 6.2 %all-to-all-start = ((bf16[8,8,5760]{2,1,0:T(8,128)(2,1)}), bf16[8,8,5760]{2,1,0:T(8,128)(2,1)S(1)}, u32[]{:S(2)}, u32[]{:S(2)}) async-start(bf16[8,8,5760]{2,1,0:T(8,128)(2,1)} %get-tuple-element.14), calls=%async_computation | async-start | bytes 1474560 | tf_op jit(solution)/shard_map/all_to_all | solution.py:483
  8.9 0.7 pad_convert_fusion.taps_ref
  9.6 11.7 %all-to-all-done.ids_ref.rows_ref = bf16[8,8,5760]{2,1,0:T(8,128)(2,1)S(1)} async-done(((bf16[8,8,5760]{2,1,0:T(8,128)(2,1)}), bf16[8,8,5760]{2,1,0:T(8,128)(2,1)S(1)}, u32[]{:S(2)}, u32[]{:S(2)}) %all-to-all-start) | async-done | bytes 737312 | tf_op jit(solution)/shard_map/all_to_all | solution.py:483
  21.3 3.5 %all-to-all-start.1 = ((bf16[8,8,4096]{2,1,0:T(8,128)(2,1)}), bf16[8,8,4096]{2,1,0:T(8,128)(2,1)S(1)}, u32[]{:S(2)}, u32[]{:S(2)}) async-start(bf16[8,8,4096]{2,1,0:T(8,128)(2,1)} %get-tuple-element.15), calls=%async_computation.1 | async-start | bytes 1048576 | tf_op jit(solution)/shard_map/all_to_all | solution.py:483
  24.8 0.1 reshape.29.sub_ref
  24.9 9.9 %grid_rows.2 = (bf16[2,8,64,128]{3,2,1,0:T(8,128)(2,1)S(1)}, bf16[2,8,64,128]{3,2,1,0:T(8,128)(2,1)S(1)}) custom-call(s32[1]{0:T(128)} %bitcast.4.place_ref, s32[64]{0:T(128)S(1)} %reshape.29.sub_ref, f32[16,128]{1,0:T(8,128)S(1)} %pad_convert_fusion.taps_ref, bf16[8,8,5760]{2,1,0:T(8,128)(2,1)S(1)} %all-to-all-done.ids_ref.rows_ref, ...), custom_call_target="tpu_custom_call" | custom-call | flops 8589934592 | bytes 2097152 | tf_op jit(solution)/shard_map/grid_rows/pallas_call | solution.py:214
  34.9 1.5 %collective-permute-done.refs_1_ = bf16[2,8,64,128]{3,2,1,0:T(8,128)(2,1)S(1)} collective-permute-done((bf16[2,8,64,128]{3,2,1,0:T(8,128)(2,1)S(1)}, bf16[2,8,64,128]{3,2,1,0:T(8,128)(2,1)S(1)}, u32[]{:S(2)}, u32[]{:S(2)}) %collective-permute-start) | collective-permute-done | bytes 262176 | tf_op jit(solution)/shard_map/ppermute | solution.py:27
  36.5 2.7 %collective-permute-start.2 = (bf16[2,8,64,128]{3,2,1,0:T(8,128)(2,1)S(1)}, bf16[2,8,64,128]{3,2,1,0:T(8,128)(2,1)S(1)}, u32[]{:S(2)}, u32[]{:S(2)}) collective-permute-start(bf16[2,8,64,128]{3,2,1,0:T(8,128)(2,1)S(1)} %add_sums.4.refs_0_), channel_id=1, source_target_pairs={{0,4},{4,0},{1,5},{5,1},{2,6},{6,2},{3,7},{7,3},{8,12},{12,8},{9,1... | collective-permute-start | bytes 786440 | tf_op jit(solution)/shard_map/ppermute | solution.py:27
  39.1 9.9 %grid_rows.3 = (bf16[2,8,64,128]{3,2,1,0:T(8,128)(2,1)S(1)}, bf16[2,8,64,128]{3,2,1,0:T(8,128)(2,1)S(1)}) custom-call(s32[1]{0:T(128)} %bitcast.4.place_ref, s32[64]{0:T(128)S(1)} %reshape.29.sub_ref, f32[16,128]{1,0:T(8,128)S(1)} %pad_convert_fusion.taps_ref, bf16[8,8,5760]{2,1,0:T(8,128)(2,1)S(1)} %all-to-all-done.ids_ref.rows_ref, ...), custom_call_target="tpu_custom_call" | custom-call | flops 8589934592 | bytes 2097152 | tf_op jit(solution)/shard_map/grid_rows/pallas_call | solution.py:214
  49.0 0.1 collective-permute-start.1
  49.1 2.3 %collective-permute-done.2.refs_1_ = bf16[2,8,64,128]{3,2,1,0:T(8,128)(2,1)S(1)} collective-permute-done((bf16[2,8,64,128]{3,2,1,0:T(8,128)(2,1)S(1)}, bf16[2,8,64,128]{3,2,1,0:T(8,128)(2,1)S(1)}, u32[]{:S(2)}, u32[]{:S(2)}) %collective-permute-start.2) | collective-permute-done | bytes 262176 | tf_op jit(solution)/shard_map/ppermute | solution.py:27
  51.6 0.1 collective-permute-start.3
  51.6 5.4 %collective-permute-start.9 = (bf16[2,8,64,128]{3,2,1,0:T(8,128)(2,1)S(1)}, bf16[2,8,64,128]{3,2,1,0:T(8,128)(2,1)S(1)}, u32[]{:S(2)}, u32[]{:S(2)}) collective-permute-start(bf16[2,8,64,128]{3,2,1,0:T(8,128)(2,1)S(1)} %add_sums.5.refs_2_.refs_0_), channel_id=1, source_target_pairs={{0,3},{1,2},{2,1},{3,0},{4,7},{5,6},{6,5},{7,4},{8,11},{9,10},{10,... | collective-permute-start | bytes 786440 | tf_op jit(solution)/shard_map/ppermute | solution.py:507
  57.0 0.6 collective-permute-start.7
  57.6 0.1 pad_add_fusion.place_ref
  57.7 0.1 pad_add_fusion.1.place_ref
  57.8 8.9 %make_tables.1 = (bf16[2048,2176]{1,0:T(8,128)(2,1)S(1)}, bf16[8,128,256]{2,1,0:T(8,128)(2,1)S(1)}, f32[64,128]{1,0:T(8,128)S(1)}) custom-call(s32[1]{0:T(128)} %bitcast.9.facet_ref, s32[8,32]{1,0:T(8,128)S(1)} %copy-done, s32[8]{0:T(128)S(1)} %copy-done.1, bf16[2,8,64,128]{3,2,1,0:T(8,128)(2,1)S(1)} %add_sums.5.refs_2_.refs_0_), custom_call_target="tpu_custom_call" | custom-call | flops 35651584 | bytes 8912896 | tf_op jit(solution)/shard_map/make_tables/pallas_call | solution.py:329
  66.8 3.0 %collective-permute-start.6 = (bf16[2,8,64,128]{3,2,1,0:T(8,128)(2,1)S(1)}, bf16[2,8,64,128]{3,2,1,0:T(8,128)(2,1)S(1)}, u32[]{:S(2)}, u32[]{:S(2)}) collective-permute-start(bf16[2,8,64,128]{3,2,1,0:T(8,128)(2,1)S(1)} %add_sums.7.refs_7_.refs_0_), channel_id=1, source_target_pairs={{0,3},{1,2},{2,1},{3,0},{4,7},{5,6},{6,5},{7,4},{8,11},{9,10},{10,... | collective-permute-start | bytes 786440 | tf_op jit(solution)/shard_map/ppermute | solution.py:507
  69.8 0.6 collective-permute-start.4
  70.4 2.0 %collective-permute-done.8.refs_2_ = bf16[2,8,64,128]{3,2,1,0:T(8,128)(2,1)S(1)} collective-permute-done((bf16[2,8,64,128]{3,2,1,0:T(8,128)(2,1)S(1)}, bf16[2,8,64,128]{3,2,1,0:T(8,128)(2,1)S(1)}, u32[]{:S(2)}, u32[]{:S(2)}) %collective-permute-start.8) | collective-permute-done | bytes 262176 | tf_op jit(solution)/shard_map/ppermute | solution.py:507
  72.4 9.1 %add_image.2.refs_7_ = f32[16,64,2048]{2,1,0:T(8,128)} custom-call(s32[4]{0:T(128)S(1)} %pad_add_fusion.1.place_ref, bf16[2,8,64,128]{3,2,1,0:T(8,128)(2,1)S(1)} %add_sums.5.refs_2_.refs_0_, bf16[2,8,64,128]{3,2,1,0:T(8,128)(2,1)S(1)} %collective-permute-done.7.refs_1_, bf16[2,8,64,128]{3,2,1,0:T(8,128)(2,1)S(1)} %collective-permute-done.8.refs_2_, ...), custom_call_target="tpu_custom_call" | custom-call | flops 4294967296 | bytes 12582912 | tf_op jit(solution)/shard_map/add_image/pallas_call | solution.py:425
  81.5 1.3 %collective-permute-done.5.refs_2_ = bf16[2,8,64,128]{3,2,1,0:T(8,128)(2,1)S(1)} collective-permute-done((bf16[2,8,64,128]{3,2,1,0:T(8,128)(2,1)S(1)}, bf16[2,8,64,128]{3,2,1,0:T(8,128)(2,1)S(1)}, u32[]{:S(2)}, u32[]{:S(2)}) %collective-permute-start.5) | collective-permute-done | bytes 262176 | tf_op jit(solution)/shard_map/ppermute | solution.py:507
  82.8 9.1 %add_image.3 = f32[16,64,2048]{2,1,0:T(8,128)} custom-call(s32[4]{0:T(128)S(1)} %pad_add_fusion.place_ref, bf16[2,8,64,128]{3,2,1,0:T(8,128)(2,1)S(1)} %add_sums.7.refs_7_.refs_0_, bf16[2,8,64,128]{3,2,1,0:T(8,128)(2,1)S(1)} %collective-permute-done.4.refs_1_, ...), custom_call_target="tpu_custom_call", output_to_operand_aliasing={{}: (8, {})} | custom-call | flops 4294967296 | bytes 12582912 | tf_op jit(solution)/shard_map/add_image/pallas_call | solution.py:425
  (19 shorter events, 0.4 us)
Async XLA Ops:
  2.7 18.6 %all-to-all-start = ((bf16[8,8,5760]{2,1,0:T(8,128)(2,1)}), bf16[8,8,5760]{2,1,0:T(8,128)(2,1)S(1)}, u32[]{:S(2)}, u32[]{:S(2)}) async-start(bf16[8,8,5760]{2,1,0:T(8,128)(2,1)} %get-tuple-element.14), calls=%async_computation | async-start | bytes 1474560 | tf_op jit(solution)/shard_map/all_to_all | solution.py:483
  21.3 17.9 %all-to-all-start.1 = ((bf16[8,8,4096]{2,1,0:T(8,128)(2,1)}), bf16[8,8,4096]{2,1,0:T(8,128)(2,1)S(1)}, u32[]{:S(2)}, u32[]{:S(2)}) async-start(bf16[8,8,4096]{2,1,0:T(8,128)(2,1)} %get-tuple-element.15), calls=%async_computation.1 | async-start | bytes 1048576 | tf_op jit(solution)/shard_map/all_to_all | solution.py:483
  34.8 1.6 %collective-permute-start = (bf16[2,8,64,128]{3,2,1,0:T(8,128)(2,1)S(1)}, bf16[2,8,64,128]{3,2,1,0:T(8,128)(2,1)S(1)}, u32[]{:S(2)}, u32[]{:S(2)}) collective-permute-start(bf16[2,8,64,128]{3,2,1,0:T(8,128)(2,1)S(1)} %get-tuple-element.17), channel_id=1, source_target_pairs={{0,8},{8,0},{1,9},{9,1},{2,10},{10,2},{3,11},{11,3},{4,12},{12,4},... | collective-permute-start | bytes 786440 | tf_op jit(solution)/shard_map/ppermute | solution.py:27
  36.5 21.3 %copy-start = (s32[8,32]{1,0:T(8,128)S(1)}, s32[8,32]{1,0:T(8,128)}, u32[]{:S(2)}) copy-start(s32[8,32]{1,0:T(8,128)} %listed_ref.1) | copy-start | bytes 3076
  36.5 21.3 %copy-start.1 = (s32[8]{0:T(128)S(1)}, s32[8]{0:T(128)}, u32[]{:S(2)}) copy-start(s32[8]{0:T(128)} %count_ref.1) | copy-start | bytes 100
  36.5 14.9 %collective-permute-start.2 = (bf16[2,8,64,128]{3,2,1,0:T(8,128)(2,1)S(1)}, bf16[2,8,64,128]{3,2,1,0:T(8,128)(2,1)S(1)}, u32[]{:S(2)}, u32[]{:S(2)}) collective-permute-start(bf16[2,8,64,128]{3,2,1,0:T(8,128)(2,1)S(1)} %add_sums.4.refs_0_), channel_id=1, source_target_pairs={{0,4},{4,0},{1,5},{5,1},{2,6},{6,2},{3,7},{7,3},{8,12},{12,8},{9,1... | collective-permute-start | bytes 786440 | tf_op jit(solution)/shard_map/ppermute | solution.py:27
  49.0 2.4 %collective-permute-start.1 = (bf16[2,8,64,128]{3,2,1,0:T(8,128)(2,1)S(1)}, bf16[2,8,64,128]{3,2,1,0:T(8,128)(2,1)S(1)}, u32[]{:S(2)}, u32[]{:S(2)}) collective-permute-start(bf16[2,8,64,128]{3,2,1,0:T(8,128)(2,1)S(1)} %get-tuple-element.19), channel_id=1, source_target_pairs={{0,8},{8,0},{1,9},{9,1},{2,10},{10,2},{3,11},{11,3},{4,12},{12,4},... | collective-permute-start | bytes 786440 | tf_op jit(solution)/shard_map/ppermute | solution.py:27
  51.6 15.1 %collective-permute-start.3 = (bf16[2,8,64,128]{3,2,1,0:T(8,128)(2,1)S(1)}, bf16[2,8,64,128]{3,2,1,0:T(8,128)(2,1)S(1)}, u32[]{:S(2)}, u32[]{:S(2)}) collective-permute-start(bf16[2,8,64,128]{3,2,1,0:T(8,128)(2,1)S(1)} %add_sums.6.refs_0_), channel_id=1, source_target_pairs={{0,4},{4,0},{1,5},{5,1},{2,6},{6,2},{3,7},{7,3},{8,12},{12,8},{9,1... | collective-permute-start | bytes 786440 | tf_op jit(solution)/shard_map/ppermute | solution.py:27
  51.6 18.1 %collective-permute-start.9 = (bf16[2,8,64,128]{3,2,1,0:T(8,128)(2,1)S(1)}, bf16[2,8,64,128]{3,2,1,0:T(8,128)(2,1)S(1)}, u32[]{:S(2)}, u32[]{:S(2)}) collective-permute-start(bf16[2,8,64,128]{3,2,1,0:T(8,128)(2,1)S(1)} %add_sums.5.refs_2_.refs_0_), channel_id=1, source_target_pairs={{0,3},{1,2},{2,1},{3,0},{4,7},{5,6},{6,5},{7,4},{8,11},{9,10},{10,... | collective-permute-start | bytes 786440 | tf_op jit(solution)/shard_map/ppermute | solution.py:507
  57.0 15.4 %collective-permute-start.8 = (bf16[2,8,64,128]{3,2,1,0:T(8,128)(2,1)S(1)}, bf16[2,8,64,128]{3,2,1,0:T(8,128)(2,1)S(1)}, u32[]{:S(2)}, u32[]{:S(2)}) collective-permute-start(bf16[2,8,64,128]{3,2,1,0:T(8,128)(2,1)S(1)} %add_sums.5.refs_2_.refs_0_), channel_id=1, source_target_pairs={{0,2},{1,3},{2,0},{3,1},{4,6},{5,7},{6,4},{7,5},{8,10},{9,11},{10,... | collective-permute-start | bytes 786440 | tf_op jit(solution)/shard_map/ppermute | solution.py:507
  57.0 15.4 %collective-permute-start.7 = (bf16[2,8,64,128]{3,2,1,0:T(8,128)(2,1)S(1)}, bf16[2,8,64,128]{3,2,1,0:T(8,128)(2,1)S(1)}, u32[]{:S(2)}, u32[]{:S(2)}) collective-permute-start(bf16[2,8,64,128]{3,2,1,0:T(8,128)(2,1)S(1)} %add_sums.5.refs_2_.refs_0_), channel_id=1, source_target_pairs={{0,1},{1,0},{2,3},{3,2},{4,5},{5,4},{6,7},{7,6},{8,9},{9,8},{10,11... | collective-permute-start | bytes 786440 | tf_op jit(solution)/shard_map/ppermute | solution.py:507
  66.8 14.7 %collective-permute-start.6 = (bf16[2,8,64,128]{3,2,1,0:T(8,128)(2,1)S(1)}, bf16[2,8,64,128]{3,2,1,0:T(8,128)(2,1)S(1)}, u32[]{:S(2)}, u32[]{:S(2)}) collective-permute-start(bf16[2,8,64,128]{3,2,1,0:T(8,128)(2,1)S(1)} %add_sums.7.refs_7_.refs_0_), channel_id=1, source_target_pairs={{0,3},{1,2},{2,1},{3,0},{4,7},{5,6},{6,5},{7,4},{8,11},{9,10},{10,... | collective-permute-start | bytes 786440 | tf_op jit(solution)/shard_map/ppermute | solution.py:507
  69.7 13.0 %collective-permute-start.5 = (bf16[2,8,64,128]{3,2,1,0:T(8,128)(2,1)S(1)}, bf16[2,8,64,128]{3,2,1,0:T(8,128)(2,1)S(1)}, u32[]{:S(2)}, u32[]{:S(2)}) collective-permute-start(bf16[2,8,64,128]{3,2,1,0:T(8,128)(2,1)S(1)} %add_sums.7.refs_7_.refs_0_), channel_id=1, source_target_pairs={{0,2},{1,3},{2,0},{3,1},{4,6},{5,7},{6,4},{7,5},{8,10},{9,11},{10,... | collective-permute-start | bytes 786440 | tf_op jit(solution)/shard_map/ppermute | solution.py:507
  69.8 13.0 %collective-permute-start.4 = (bf16[2,8,64,128]{3,2,1,0:T(8,128)(2,1)S(1)}, bf16[2,8,64,128]{3,2,1,0:T(8,128)(2,1)S(1)}, u32[]{:S(2)}, u32[]{:S(2)}) collective-permute-start(bf16[2,8,64,128]{3,2,1,0:T(8,128)(2,1)S(1)} %add_sums.7.refs_7_.refs_0_), channel_id=1, source_target_pairs={{0,1},{1,0},{2,3},{3,2},{4,5},{5,4},{6,7},{7,6},{8,9},{9,8},{10,11... | collective-permute-start | bytes 786440 | tf_op jit(solution)/shard_map/ppermute | solution.py:507

commit v4 on v3

v4 whole, which is shorter than its diff:
```python
import functools
import math

import jax
import jax.numpy as jnp
from jax import lax
from jax.experimental import pallas as pl
from jax.experimental.pallas import tpu as pltpu
from jax.sharding import Mesh
from jax.sharding import PartitionSpec as P

BLK = 512
SG = 32
NSUB = 32
FX = 2048
FY = 64
MARGIN = 128
LANES = 128
PACK = LANES // SG
SETS = NSUB // PACK
CHAN = ("y", "core")
VMEM_LIMIT = 56 << 20
FACET = ("z1", "z0", "x")


def swap(block, axis):
    return lax.ppermute(block, axis, [(0, 1), (1, 0)])


def pack_kernel(
    group_ref, flip_ref, vis_from, plane_from, cell_from, sub_from, first_ref, second_ref, *refs, shares
):
    vis_ref, plane_ref, cell_ref, sub_ref, sems, vis_sems = refs
    chan_shares, pol_shares, per_chan, per_pol, cores, east = shares
    num_pols = vis_ref.shape[1] // 2
    row_len = vis_ref.shape[2]
    lines = first_ref.shape[1]
    width = row_len // lines
    half = per_pol // 2
    group = group_ref[0]
    small = [(plane_from, plane_ref), (cell_from, cell_ref), (sub_from, sub_ref)]
    small = [pltpu.make_async_copy(*pair, sems.at[k]) for k, pair in enumerate(small)]
    dests = first_ref.shape[0]
    step = vis_ref.shape[0] // (dests // (chan_shares * pol_shares))
    large = []
    for k in range(vis_ref.shape[0] // step):
        chans = pl.ds(k * step, step)
        large.append(
            pltpu.make_async_copy(vis_from.at[chans], vis_ref.at[chans], vis_sems.at[k])
        )
    for copy in small + large:
        copy.start()
    for copy in small:
        copy.wait()

    def folded(row):
        row = row.astype(jnp.float32)
        return jnp.concatenate([row[:, k * width : (k + 1) * width] for k in range(lines)], axis=0)

    subs = sub_ref[pl.ds(group, 1), :].astype(jnp.float32)
    subs = jnp.concatenate([subs, jnp.zeros((1, LANES - subs.shape[1]), jnp.float32)], axis=1)
    ids = [
        folded(plane_ref[pl.ds(group, 1), :]),
        folded(cell_ref[0, pl.ds(group, 1), :]),
        folded(cell_ref[1, pl.ds(group, 1), :]),
        jnp.broadcast_to(subs, (lines, LANES)),
    ]
    ids = jnp.concatenate(ids, axis=1).astype(jnp.bfloat16)
    def fill(flip):
        for north, copy in enumerate(large):
            copy.wait()
            for chan_share in range(chan_shares):
                for pol_share in range(pol_shares):
                    found = ([], [])
                    share = chan_share * pol_shares + pol_share
                    dest = north * chan_shares * pol_shares
                    dest = dest + (share // east + flip) % 2 * east + share % east
                    for core in range(cores):
                        chans = (north * cores + core) * chan_shares + chan_share
                        chans = [
                            vis_ref[chans * per_chan + k].astype(jnp.float32) for k in range(per_chan)
                        ]
                        for part in range(2):
                            start = part * num_pols + pol_share * per_pol
                            for vis in chans:
                                found[0].append(vis[start : start + half])
                                found[1].append(vis[start + half : start + per_pol])
                    first_ref[dest, :, :row_len] = jnp.concatenate(found[0], 0).astype(jnp.bfloat16)
                    first_ref[dest, :, row_len:] = ids
                    second_ref[dest] = jnp.concatenate(found[1], 0).astype(jnp.bfloat16)

    for flip in range(2):
        pl.when(flip_ref[0] == flip)(functools.partial(fill, flip))


def pack_rows(group, flip, vis, planes, cells, subs, shares, dests, lines):
    row_len = vis.shape[2]
    extra = 3 * row_len // lines + LANES
    norths = dests // (shares[0] * shares[1])
    vmem = pl.BlockSpec(memory_space=pltpu.VMEM)
    return pl.pallas_call(
        functools.partial(pack_kernel, shares=shares),
        out_shape=[
            jax.ShapeDtypeStruct((dests, lines, row_len + extra), jnp.bfloat16),
            jax.ShapeDtypeStruct((dests, lines, row_len), jnp.bfloat16),
        ],
        grid_spec=pltpu.PrefetchScalarGridSpec(
            num_scalar_prefetch=2,
            grid=(),
            in_specs=[pl.BlockSpec(memory_space=pl.ANY)] * 4,
            out_specs=[vmem] * 2,
            scratch_shapes=[pltpu.VMEM(a.shape, a.dtype) for a in (vis, planes, cells, subs)]
            + [pltpu.SemaphoreType.DMA((3,)), pltpu.SemaphoreType.DMA((norths,))],
        ),
        compiler_params=pltpu.CompilerParams(vmem_limit_bytes=VMEM_LIMIT),
        cost_estimate=pl.CostEstimate(flops=1 << 20, bytes_accessed=3 << 20, transcendentals=0),
        name="pack_rows",
    )(group, flip, vis, planes, cells, subs)


def grid_kernel(place_ref, taps_ref, ids_ref, rows_ref, *refs, row_len, ids_from):
    own_ref, other_ref, sums_ref, listed_ref, sub_ref, sem = refs[-6:]
    sources, lines = rows_ref.shape[:2]
    pols = lines // 4
    cells = 2 * pols * SG
    blocks = row_len // BLK
    width = row_len // lines

    for source in range(sources):
        subs = ids_ref[source, :, ids_from + 3 * width :].astype(jnp.float32)
        listed_ref[source : source + 1] = subs[:1].astype(jnp.int32)
    copy = pltpu.make_async_copy(listed_ref, sub_ref, sem)
    copy.start()
    sums_ref[...] = jnp.zeros_like(sums_ref)
    copy.wait()
    taps = taps_ref[...].astype(jnp.float32)
    taps = jnp.concatenate([taps, jnp.zeros((16, LANES - taps.shape[1]), jnp.float32)], axis=1)
    cell = lax.broadcasted_iota(jnp.int32, (8, BLK), 0)

    def listed(ids, kind, block):
        found = []
        for start in range(block * BLK, (block + 1) * BLK, min(BLK, width)):
            line, column = start // width, kind * width + start % width
            found.append(ids[line : line + 1, column : column + min(BLK, width)])
        return jnp.concatenate(found, axis=1) if len(found) > 1 else found[0]

    def pick(values, index, axis):
        found = [
            jnp.take_along_axis(
                values if axis else values[:, c : c + LANES], index[:, c : c + LANES], axis=axis
            )
            for c in range(0, BLK, LANES)
        ]
        return jnp.concatenate(found, axis=1)

    level = -(lax.broadcasted_iota(jnp.int32, (16, BLK), 0) >> 3)
    levels = [(level - 2 * k).astype(jnp.float32).astype(jnp.bfloat16) for k in range(SG // 16)]
    none = jnp.zeros((16, BLK), jnp.bfloat16)

    def doubled(part):
        return jnp.concatenate([part, part], axis=0).astype(jnp.bfloat16)

    def turned(values, offset):
        distance = cell - offset
        height = doubled((distance >> 3).astype(jnp.float32))
        parts = [pick(values[8 * q : 8 * q + 8], distance & 7, 0) for q in range(2)]
        return parts, [height == level for level in levels]

    def spread(part, masks):
        part = doubled(part)
        return jnp.concatenate([jnp.where(mask, part, none) for mask in masks], axis=0)

    def grid_source(source):
        ids = ids_ref[source, :, ids_from : ids_from + 3 * width]
        ids = ids.astype(jnp.float32).astype(jnp.int32)
        for block in range(blocks):
            plane = jnp.broadcast_to(listed(ids, 0, block), (16, BLK))
            values = pick(taps, plane, 1)
            parts, masks = turned(values, listed(ids, 1, block))
            left = jnp.concatenate([spread(part, masks) for part in parts], axis=0)
            (kern_re, kern_im), masks = turned(values, listed(ids, 2, block))
            vis = rows_ref[source, :, block * BLK : (block + 1) * BLK].astype(jnp.float32)
            vis = pltpu.roll(vis, place_ref[0] * (lines // 2), 0)
            real, imag = [], []
            for first in (0, 2 * pols):
                for row in range(first, first + pols):
                    vis_re = vis[row : row + 1]
                    vis_im = vis[row + pols : row + pols + 1]
                    real.append(spread(vis_re * kern_re - vis_im * kern_im, masks))
                    imag.append(spread(vis_re * kern_im + vis_im * kern_re, masks))
            weighted = jnp.concatenate(real + imag, axis=0)
            sub = sub_ref[source, block]
            sums_ref[sub] += lax.dot_general(
                left, weighted, (((1,), (1,)), ((), ())), preferred_element_type=jnp.float32
            )

    def grid_sources(step, carry):
        for k in range(unroll):
            grid_source(step * unroll + k)
        return carry

    unroll = math.gcd(sources, 4)
    lax.fori_loop(0, sources // unroll, grid_sources, 0)
    slot = lax.broadcasted_iota(jnp.int32, (2 * SG, LANES), 1) // SG

    def finish(group):
        parts = []
        for k in range(PACK):
            raw = sums_ref[group * PACK + k]
            real = raw[:SG, :cells] - raw[SG:, cells:]
            imag = raw[:SG, cells:] + raw[SG:, :cells]
            part = jnp.concatenate([real, imag], axis=0)
            if cells < LANES:
                part = jnp.concatenate([part, jnp.zeros_like(part)], axis=1)
            parts.append(part)
        for pol in range(2 * pols):
            tile = slice(pol // PACK * LANES, (pol // PACK + 1) * LANES)
            packed = jnp.zeros((2 * SG, LANES), jnp.float32)
            for k in range(PACK):
                move = (k - pol) % PACK * SG
                part = parts[k][:, tile]
                part = pltpu.roll(part, move, 1) if move else part
                packed = jnp.where(slot == k, part, packed)
            out_ref = own_ref if pol < pols else other_ref
            out_ref[pol % pols, group] = packed.astype(jnp.bfloat16)

    for group in range(SETS):
        finish(group)


def grid_rows(place, taps, ids, rows, row_len, after):
    sources, lines, _ = rows.shape
    pols = lines // 4
    shape = (pols, SETS, 2 * SG, LANES)
    vmem = pl.BlockSpec(memory_space=pltpu.VMEM)
    flops = 2 * sources * row_len * 2 * SG * 4 * pols * SG
    return pl.pallas_call(
        functools.partial(grid_kernel, row_len=row_len, ids_from=row_len),
        out_shape=[jax.ShapeDtypeStruct(shape, jnp.bfloat16)] * 2,
        grid_spec=pltpu.PrefetchScalarGridSpec(
            num_scalar_prefetch=1,
            grid=(),
            in_specs=[vmem] * 3 + [pl.BlockSpec(memory_space=pl.ANY)] * len(after),
            out_specs=[vmem] * 2,
            scratch_shapes=[
                pltpu.VMEM((NSUB, 2 * SG, 4 * pols * SG), jnp.float32),
                pltpu.VMEM((sources, LANES), jnp.int32),
                pltpu.SMEM((sources, LANES), jnp.int32),
                pltpu.SemaphoreType.DMA(()),
            ],
        ),
        compiler_params=pltpu.CompilerParams(vmem_limit_bytes=16 << 20),
        cost_estimate=pl.CostEstimate(
            flops=flops * 8, bytes_accessed=2 << 20, transcendentals=0
        ),
        name="grid_rows",
    )(place, taps, ids, rows, *after)


def add_kernel(*refs, terms):
    total = refs[0][...].astype(jnp.float32)
    for ref in refs[1:terms]:
        total = total + ref[...].astype(jnp.float32)
    refs[-1][...] = total.astype(jnp.bfloat16)


def add(terms, after=()):
    vmem = pl.BlockSpec(memory_space=pltpu.VMEM)
    return pl.pallas_call(
        functools.partial(add_kernel, terms=len(terms)),
        out_shape=jax.ShapeDtypeStruct(terms[0].shape, jnp.bfloat16),
        in_specs=[vmem] * len(terms) + [pl.BlockSpec(memory_space=pl.ANY)] * len(after),
        out_specs=vmem,
        compiler_params=pltpu.CompilerParams(vmem_limit_bytes=4 << 20),
        cost_estimate=pl.CostEstimate(flops=1 << 18, bytes_accessed=4 << 20, transcendentals=0),
        name="add_sums",
    )(*terms, *after)


def wrapped(value, period):
    if period & (period - 1):
        return jnp.mod(value, period)
    return value & (period - 1)


def circle(phase, period):
    phase = wrapped(phase, period)
    quarter = lax.div(phase + period // 8, period // 4)
    rest = phase - quarter * (period // 4)
    angle = rest.astype(jnp.float32) * (2.0 * math.pi / period)
    square = angle * angle
    sin = -1.0 / 5040 + square * (1.0 / 362880)
    sin = -1.0 / 6 + square * (1.0 / 120 + square * sin)
    sin = angle + angle * square * sin
    cos = -1.0 / 720 + square * (1.0 / 40320)
    cos = 1.0 + square * (-0.5 + square * (1.0 / 24 + square * cos))
    odd = (quarter & 1) == 1
    full_cos, full_sin = jnp.where(odd, sin, cos), jnp.where(odd, cos, sin)
    full_cos = jnp.where(((quarter + 1) & 2) == 2, -full_cos, full_cos)
    return full_cos, jnp.where((quarter & 2) == 2, -full_sin, full_sin)


def tables_kernel(facet_ref, listed_ref, count_ref, *refs, period):
    table_ref, turn_ref, keep_ref = refs[-3:]
    facet = facet_ref[0]
    span = period // SG
    cells = PACK * SG
    row = lax.broadcasted_iota(jnp.int32, (cells, LANES), 0)
    lane = lax.broadcasted_iota(jnp.int32, (cells, LANES), 1)
    tiles = table_ref.shape[1] // LANES
    room = LANES // PACK
    turn_shape = (FY, 2 * PACK * SG)
    turn_line = lax.broadcasted_iota(jnp.int32, turn_shape, 0) - FY // 2
    turn_lane = lax.broadcasted_iota(jnp.int32, turn_shape, 1)
    second = (turn_lane >> 5 & 1) == 1

    def col_cell(group):
        sub = group * PACK + (row >> 5)
        return (wrapped(sub * 53 + 5, span) - span // 2) * SG + (row & (SG - 1))

    tile_id = lane & (room - 1)
    start = jnp.where(tile_id == tiles - 1, -MARGIN, tile_id * LANES)
    start = facet * FX - period // 2 + start
    for batch in range(SETS // PACK):
        coarse_cos, coarse_sin = circle(col_cell(batch * PACK + (lane >> 5)) * start, period)
        for k in range(PACK):
            group = batch * PACK + k
            base = group * 2 * cells
            fine_cos, fine_sin = circle(col_cell(group) * lane, period)
            for tile in range(tiles):
                columns = slice(tile * LANES, (tile + 1) * LANES)
                at = k * room + tile
                tile_cos = coarse_cos[:, at : at + 1]
                tile_neg = -coarse_sin[:, at : at + 1]
                full_cos = tile_cos * fine_cos + tile_neg * fine_sin
                full_neg = tile_neg * fine_cos - tile_cos * fine_sin
                table_ref[base : base + cells, columns] = full_cos.astype(jnp.bfloat16)
                table_ref[base + cells : base + 2 * cells, columns] = full_neg.astype(
                    jnp.bfloat16
                )

            sub = group * PACK + (turn_lane >> 6)
            cell = (wrapped(sub * 37, span) - span // 2) * SG + (turn_lane & (SG - 1))
            cos, sin = circle(cell * turn_line, period)
            turn_ref[group, :FY] = jnp.where(second, -sin, cos).astype(jnp.bfloat16)
            turn_ref[group, FY:] = jnp.where(second, cos, sin).astype(jnp.bfloat16)

    line = lax.broadcasted_iota(jnp.int32, (FY, MARGIN), 0)
    before = jnp.maximum(facet - 1, 0)
    in_use = jnp.where(facet > 0, count_ref[before], 0)

    def mark(k, keep):
        return jnp.where((line == listed_ref[before, k]) & (k < in_use), 1.0, keep)

    keep_ref[...] = lax.fori_loop(
        0, listed_ref.shape[1], mark, jnp.zeros((FY, MARGIN), jnp.float32)
    )


def make_tables(facet, listed, counts, period, token):
    depth, width = 2 * NSUB * SG, FX + MARGIN
    vmem = pl.BlockSpec(memory_space=pltpu.VMEM)
    return pl.pallas_call(
        functools.partial(tables_kernel, period=period),
        out_shape=[
            jax.ShapeDtypeStruct((depth, width), jnp.bfloat16),
            jax.ShapeDtypeStruct((SETS, 2 * FY, 2 * PACK * SG), jnp.bfloat16),
            jax.ShapeDtypeStruct((FY, MARGIN), jnp.float32),
        ],
        grid_spec=pltpu.PrefetchScalarGridSpec(
            num_scalar_prefetch=3,
            grid=(),
            in_specs=[pl.BlockSpec(memory_space=pl.ANY)],
            out_specs=[vmem] * 3,
        ),
        compiler_params=pltpu.CompilerParams(vmem_limit_bytes=16 << 20),
        cost_estimate=pl.CostEstimate(
            flops=8 * depth * width, bytes_accessed=2 * depth * width, transcendentals=1 << 19
        ),
        name="make_tables",
    )(facet, listed, counts, token)


def image_kernel(z1_ref, z0_ref, x_ref, *refs, places, scale, columns):
    parts = len(places)
    piece_refs = refs[:parts]
    turn_ref, table_ref, keep_ref = refs[parts : parts + 3]
    out_ref, lines_ref, done_ref, sems = refs[-4:]
    per = piece_refs[0].shape[0]
    width = table_ref.shape[1] - MARGIN
    slot = lax.broadcasted_iota(jnp.int32, (2 * SG, 2 * LANES), 1) % LANES // SG
    flat = [(part, i) for part in range(parts) for i in range(per)]

    def group_rows(group):
        base = group * 2 * LANES
        for k in range(0, len(flat), 2):
            pair = [piece_refs[part][i, group] for part, i in flat[k : k + 2]]
            pair = jnp.concatenate(pair, axis=1)
            zero = jnp.zeros_like(pair)
            spread = [jnp.where(slot[:, : pair.shape[1]] == s, pair, zero) for s in range(PACK)]
            spread = jnp.concatenate(spread, axis=0)
            turned = jnp.dot(turn_ref[group], spread, preferred_element_type=jnp.float32)
            turned = (turned * scale).astype(jnp.bfloat16)
            for m in range(pair.shape[1] // LANES):
                for q in range(2):
                    lines_ref[
                        (k + m) * FY : (k + m + 1) * FY, base + q * LANES : base + (q + 1) * LANES
                    ] = turned[q * FY : (q + 1) * FY, m * LANES : (m + 1) * LANES]

    for group in range(SETS):
        group_rows(group)
    lines = lines_ref[...]

    def spot(part):
        z_step, x_step, east, half = places[part]
        share = lax.rem(z0_ref[0] + z1_ref[0] + z_step, 2) * east
        share = share + lax.rem(x_ref[0] + east - x_step, east)
        return (share * 2 + half) * per

    def copy(step, part):
        return pltpu.make_async_copy(
            done_ref.at[step % 2, pl.ds(part * per, per)],
            out_ref.at[pl.ds(spot(part), per), :, pl.ds(step * columns, columns)],
            sems.at[step % 2, part],
        )

    steps = width // columns
    for step in range(steps):
        if step >= 2:
            for part in range(parts):
                copy(step - 2, part).wait()
        block = table_ref[:, step * columns : (step + 1) * columns]
        total = jnp.dot(lines, block, preferred_element_type=jnp.float32)
        done_ref[step % 2] = total.reshape(parts * per, FY, columns)
        if step == 0:
            edge = jnp.dot(lines, table_ref[:, width:], preferred_element_type=jnp.float32)
            edge = edge.reshape(parts * per, FY, MARGIN) * keep_ref[...][None]
            done_ref[0, :, :, :MARGIN] += edge
        for part in range(parts):
            copy(step, part).start()
    for step in range(max(steps - 2, 0), steps):
        for part in range(parts):
            copy(step, part).wait()


def add_image(image, device, places, pieces, turn, table, keep, total_pols, scale, after):
    parts, per = len(pieces), pieces[0].shape[0]
    pols = parts * per
    columns = 1024
    depth = table.shape[0]
    width = table.shape[1] - MARGIN
    vmem = pl.BlockSpec(memory_space=pltpu.VMEM)
    operands = [*pieces, turn, table, keep]
    in_specs = [vmem] * len(operands)
    operands.extend(after)
    in_specs.extend([pl.BlockSpec(memory_space=pl.ANY)] * len(after))
    aliases = {}
    if image is not None:
        operands.append(image)
        in_specs.append(pl.BlockSpec(memory_space=pl.ANY))
        aliases = {len(operands) + 2: 0}
    return pl.pallas_call(
        functools.partial(image_kernel, places=places, scale=scale, columns=columns),
        out_shape=jax.ShapeDtypeStruct((total_pols, FY, width), jnp.float32),
        grid_spec=pltpu.PrefetchScalarGridSpec(
            num_scalar_prefetch=3,
            grid=(),
            in_specs=in_specs,
            out_specs=pl.BlockSpec(memory_space=pl.ANY),
            scratch_shapes=[
                pltpu.VMEM((pols * FY, depth), jnp.bfloat16),
                pltpu.VMEM((2, pols, FY, columns), jnp.float32),
                pltpu.SemaphoreType.DMA((2, parts)),
            ],
        ),
        input_output_aliases=aliases,
        compiler_params=pltpu.CompilerParams(vmem_limit_bytes=28 << 20),
        cost_estimate=pl.CostEstimate(
            flops=2 * pols * FY * depth * width,
            bytes_accessed=2 * depth * width + 4 * pols * FY * width,
            transcendentals=0,
        ),
        name="add_image",
    )(*device, *operands)


def shards(
    visibilities, w_kernel, w_index, cell_offsets, block_sub, intersection_rows, intersection_count
):
    cores, east = lax.axis_size("core"), lax.axis_size("x")
    north, upper = lax.axis_size("y"), lax.axis_size("z0")
    groups, facets = north * cores, lax.axis_size(FACET)
    num_chans, num_parts, _, row_len = visibilities.shape
    num_pols = num_parts // 2
    own_chans = num_chans // groups
    shares = upper * east
    chan_shares = math.gcd(shares, own_chans)
    pol_shares = shares // chan_shares
    per_chan, per_pol = own_chans // chan_shares, num_pols // pol_shares
    lines = 2 * per_chan * per_pol
    period = FX * facets
    z1, z0, x = (lax.axis_index(axis) for axis in ("z1", "z0", "x"))

    def scalar(value):
        return jnp.reshape(value, (1,)).astype(jnp.int32)

    vis = visibilities.reshape(num_chans, num_parts, row_len)
    sent = pack_rows(
        scalar(lax.axis_index(CHAN)),
        scalar(z1),
        vis,
        w_index,
        cell_offsets,
        block_sub,
        (chan_shares, pol_shares, per_chan, per_pol, cores, east),
        north * shares,
        lines,
    )
    rows = [
        lax.all_to_all(part, ("y", "z0", "x"), split_axis=0, concat_axis=0, tiled=True)
        for part in sent
    ]
    taps = w_kernel.transpose(1, 2, 0).reshape(-1, w_kernel.shape[0])
    place = scalar(lax.axis_index("core"))
    scale = 1.0 / math.sqrt(groups * facets * row_len)

    def gridded(half, after):
        own, other = grid_rows(place, taps, rows[0], rows[half], row_len, after)
        return own, swap(other, "core")

    def shifted(piece, z_step, x_step):
        if z_step + x_step == 0:
            return piece
        route = [
            (a * east + b, (a + z_step) % upper * east + (b + x_step) % east)
            for a in range(upper)
            for b in range(east)
        ]
        return lax.ppermute(piece, ("z0", "x"), route)

    def gathered(mine, relay):
        pieces = []
        for z_step in range(upper):
            here = shifted(mine, z_step, 0)
            for x_step in range(east):
                if relay or z_step + x_step == 0:
                    pieces.append(shifted(here, 0, x_step))
                else:
                    pieces.append(shifted(mine, z_step, x_step))
        return pieces

    def mirrored(block):
        return lax.ppermute(block, ("z1", "z0"), [(i, 3 - i) for i in range(4)])

    first = add(gridded(0, ()))
    first_far = mirrored(first)
    second = gridded(1, (first,))
    first = add((first, first_far), second[:1])
    second = add(second, (first,))
    second_far = mirrored(second)
    first_pieces = gathered(first, False)
    table, turn, keep = make_tables(
        scalar(lax.axis_index(FACET)), intersection_rows, intersection_count, period, first
    )
    second = add((second, second_far))
    second_pieces = gathered(second, False)
    total_pols = own_chans * num_pols
    device = [scalar(lax.axis_index(axis)) for axis in ("z1", "z0", "x")]
    places = [
        [(a, b, east, half) for a in range(upper) for b in range(east)] for half in range(2)
    ]
    pieces = first_pieces + second_pieces
    places = places[0] + places[1]
    parts = len(first_pieces)
    image = None
    cuts = (0, parts + 1, 2 * parts - 1, 2 * parts)
    for begin, end in zip(cuts, cuts[1:]):
        image = add_image(
            image,
            device,
            places[begin:end],
            pieces[begin:end],
            turn,
            table,
            keep,
            total_pols,
            scale,
            () if begin else (second,),
        )
    return image.reshape(own_chans, num_pols, FY, FX)


def solution(mesh):
    groups, facets = mesh.shape["chan"], mesh.shape["facet"]
    inner = Mesh(
        mesh.devices.reshape(groups // 2, 2, 2, 2, facets // 4), CHAN + FACET
    )
    return jax.shard_map(
        shards,
        mesh=inner,
        in_specs=(
            P(None, None, CHAN, FACET),
            P(),
            P(None, FACET),
            P(None, None, FACET),
            P(None, FACET),
            P(),
            P(),
        ),
        out_specs=P(CHAN, None, None, FACET),
        check_vma=False,
    )
```

time: 92.2 us -> 83.6 us (0.907)
  blocking collectives: 0 us -> 18.3 us
  waiting for transfers between devices: 18.8 us -> 6.5 us
  Pallas kernels: 49.8 us -> 39.1 us
  starting transfers between devices: 22.1 us -> 18.3 us
    all_to_all x0 -> x1, blocking collectives: none -> 18.3 us  [shards(): lax.all_to_all(part, ('y', 'z0', 'x'), split_axis=0, concat_axis=0, tiled...]
    all_to_all x2 -> x1, waiting for transfers between devices: 11.7 us -> 0.01 us  [shards(): lax.all_to_all(part, ('y', 'z0', 'x'), split_axis=0, concat_axis=0, tiled...]
    all_to_all x2 -> x1, starting transfers between devices: 9.69 us -> 3.49 us  [shards(): lax.all_to_all(part, ('y', 'z0', 'x'), split_axis=0, concat_axis=0, tiled...]
    pallas_call x2, Pallas kernels: 19.8 us -> 13.8 us  [grid_rows(): pl.pallas_call(functools.partial(grid_kernel, row_len=row_len, ids_from=r...]
    ppermute x6 -> x8, starting transfers between devices: 9.59 us -> 14.7 us  [the longest x6 8.88 us: shifted(): return lax.ppermute(piece, ('z0', 'x'), route)]
    pallas_call x2 -> x3, Pallas kernels: 18.1 us -> 15 us  [add_image(): pl.pallas_call(functools.partial(image_kernel, places=places, scale=scale...]
    ppermute x4 -> x2, starting transfers between devices: 2.87 us -> 0.14 us  [swap(): return lax.ppermute(block, axis, [(0, 1), (1, 0)])]
    pallas_call x1, Pallas kernels: 8.91 us -> 7.3 us  [make_tables(): pl.pallas_call(functools.partial(tables_kernel, period=period), out_shape...]
  transfers between devices with their start and end apart: 12 -> 11, of which waited for: 5 -> 3; matrix products, arithmetic and copies ran while one was open for 1% -> 0% of each run, Pallas kernels for 41% -> 41%
where the time goes in v4:
time: 83.6 us; the launch traced here: 83.3 us
  Pallas kernels  39.1 us (47%)
  blocking collectives  18.3 us (22%)
  starting transfers between devices  18.3 us (22%)
  waiting for transfers between devices  6.5 us (8%)
    all_to_all x1, blocking collectives, shards(): lax.all_to_all(part, ('y', 'z0', 'x'), split_axis=0, concat_axis=0, tiled...  18.3 us
    pallas_call x3, Pallas kernels, add_image(): pl.pallas_call(functools.partial(image_kernel, places=places, scale=scale...  15 us
    pallas_call x2, Pallas kernels, grid_rows(): pl.pallas_call(functools.partial(grid_kernel, row_len=row_len, ids_from=r...  13.8 us
    ppermute x6, starting transfers between devices, shifted(): return lax.ppermute(piece, ('z0', 'x'), route)  8.88 us
    pallas_call x1, Pallas kernels, make_tables(): pl.pallas_call(functools.partial(tables_kernel, period=period), out_shape...  7.3 us
    ppermute x2, starting transfers between devices, mirrored(): return lax.ppermute(block, ('z1', 'z0'), [(i, 3 - i) for i in range(4)])  5.8 us
    ppermute x6, waiting for transfers between devices, shifted(): return lax.ppermute(piece, ('z0', 'x'), route)  3.53 us
    all_to_all x1, starting transfers between devices, shards(): lax.all_to_all(part, ('y', 'z0', 'x'), split_axis=0, concat_axis=0, tiled...  3.49 us
  transfers between devices with their start and end apart: 11, of which 3 were waited for; matrix products, arithmetic and copies ran while one was open for 0% of the time, Pallas kernels for 41%

profile of v4, /device:TPU:0, one launch (start us, length us, event | category | flops | bytes accessed | tf_op | source)
XLA Modules:
  0.0 83.3 jit_solution(16920612339850247554)
XLA Ops:
  0.0 2.7 %pack_rows.1 = (bf16[8,8,5760]{2,1,0:T(8,128)(2,1)}, bf16[8,8,4096]{2,1,0:T(8,128)(2,1)}) custom-call(s32[1]{0:T(128)} %bitcast.6.group_ref, s32[1]{0:T(128)} %bitcast.flip_ref.z1_ref, bf16[16,8,4096]{2,1,0:T(8,128)(2,1)} %bitcast.13, s32[4,4096]{1,0:T(4,128)} %plane_from.1, s32[2,4,4096]{2,1,0:T(4,128)} %cell_from.1, s32[4,8]{1,0:T(4,128)} %sub_from.1), custom_call_target="tpu_custom_call" | custom-call | flops 1048576 | bytes 3145728 | tf_op jit(solution)/shard_map/pack_rows/pallas_call | solution.py:101
  2.8 18.3 %all_to_all.10.ids_ref.rows_ref = bf16[8,8,5760]{2,1,0:T(8,128)(2,1)S(1)} all-to-all(bf16[8,8,5760]{2,1,0:T(8,128)(2,1)} %get-tuple-element.14), channel_id=1, replica_groups=mesh['y'=2,'core'=2,'z1'=2,'z0'=2,'x'=2] {'y','z0','x'}, dimensions={0} | all-to-all | bytes 1474560 | tf_op jit(solution)/shard_map/all_to_all | solution.py:520
  21.0 3.5 %all-to-all-start.1 = ((bf16[8,8,4096]{2,1,0:T(8,128)(2,1)}), bf16[8,8,4096]{2,1,0:T(8,128)(2,1)S(1)}, u32[]{:S(2)}, u32[]{:S(2)}) async-start(bf16[8,8,4096]{2,1,0:T(8,128)(2,1)} %get-tuple-element.15), calls=%async_computation.1 | async-start | bytes 1048576 | tf_op jit(solution)/shard_map/all_to_all | solution.py:520
  24.6 0.7 copy-done
  25.2 6.8 %grid_rows.2 = (bf16[2,8,64,128]{3,2,1,0:T(8,128)(2,1)S(1)}, bf16[2,8,64,128]{3,2,1,0:T(8,128)(2,1)S(1)}) custom-call(s32[1]{0:T(128)} %bitcast.3.place_ref, bf16[16,32]{1,0:T(8,128)(2,1)S(1)} %bitcast.11, bf16[8,8,5760]{2,1,0:T(8,128)(2,1)S(1)} %all_to_all.10.ids_ref.rows_ref, bf16[8,8,5760]{2,1,0:T(8,128)(2,1)S(1)} %all_to_all.10.ids_ref.rows_ref), custom_call_target="tpu_custom_call" | custom-call | flops 8589934592 | bytes 2097152 | tf_op jit(solution)/shard_map/grid_rows/pallas_call | solution.py:237
  32.1 0.1 collective-permute-start
  32.2 1.5 %collective-permute-done.refs_1_ = bf16[2,8,64,128]{3,2,1,0:T(8,128)(2,1)S(1)} collective-permute-done((bf16[2,8,64,128]{3,2,1,0:T(8,128)(2,1)S(1)}, bf16[2,8,64,128]{3,2,1,0:T(8,128)(2,1)S(1)}, u32[]{:S(2)}, u32[]{:S(2)}) %collective-permute-start) | collective-permute-done | bytes 262176 | tf_op jit(solution)/shard_map/ppermute | solution.py:27
  33.8 4.0 %collective-permute-start.2 = (bf16[2,8,64,128]{3,2,1,0:T(8,128)(2,1)S(1)}, bf16[2,8,64,128]{3,2,1,0:T(8,128)(2,1)S(1)}, u32[]{:S(2)}, u32[]{:S(2)}) collective-permute-start(bf16[2,8,64,128]{3,2,1,0:T(8,128)(2,1)S(1)} %add_sums.4.refs_0_), channel_id=1, source_target_pairs={{0,6},{2,4},{4,2},{6,0},{1,7},{3,5},{5,3},{7,1},{8,14},{10,12},{12... | collective-permute-start | bytes 786440 | tf_op jit(solution)/shard_map/ppermute | solution.py:553
  37.8 7.0 %grid_rows.3 = (bf16[2,8,64,128]{3,2,1,0:T(8,128)(2,1)S(1)}, bf16[2,8,64,128]{3,2,1,0:T(8,128)(2,1)S(1)}) custom-call(s32[1]{0:T(128)} %bitcast.3.place_ref, bf16[16,32]{1,0:T(8,128)(2,1)S(1)} %bitcast.12, bf16[8,8,5760]{2,1,0:T(8,128)(2,1)S(1)} %all_to_all.10.ids_ref.rows_ref, bf16[8,8,4096]{2,1,0:T(8,128)(2,1)S(1)} %all-to-all-done.1.rows_ref, ...), custom_call_target="tpu_custom_call" | custom-call | flops 8589934592 | bytes 2097152 | tf_op jit(solution)/shard_map/grid_rows/pallas_call | solution.py:237
  44.8 0.1 collective-permute-start.1
  44.9 0.1 add_sums.5.refs_2_.refs_0_
  45.0 1.4 %collective-permute-done.1.refs_1_ = bf16[2,8,64,128]{3,2,1,0:T(8,128)(2,1)S(1)} collective-permute-done((bf16[2,8,64,128]{3,2,1,0:T(8,128)(2,1)S(1)}, bf16[2,8,64,128]{3,2,1,0:T(8,128)(2,1)S(1)}, u32[]{:S(2)}, u32[]{:S(2)}) %collective-permute-start.1) | collective-permute-done | bytes 262176 | tf_op jit(solution)/shard_map/ppermute | solution.py:27
  46.5 1.8 %collective-permute-start.3 = (bf16[2,8,64,128]{3,2,1,0:T(8,128)(2,1)S(1)}, bf16[2,8,64,128]{3,2,1,0:T(8,128)(2,1)S(1)}, u32[]{:S(2)}, u32[]{:S(2)}) collective-permute-start(bf16[2,8,64,128]{3,2,1,0:T(8,128)(2,1)S(1)} %add_sums.6.refs_0_), channel_id=1, source_target_pairs={{0,6},{2,4},{4,2},{6,0},{1,7},{3,5},{5,3},{7,1},{8,14},{10,12},{12... | collective-permute-start | bytes 786440 | tf_op jit(solution)/shard_map/ppermute | solution.py:553
  48.2 4.3 %collective-permute-start.9 = (bf16[2,8,64,128]{3,2,1,0:T(8,128)(2,1)S(1)}, bf16[2,8,64,128]{3,2,1,0:T(8,128)(2,1)S(1)}, u32[]{:S(2)}, u32[]{:S(2)}) collective-permute-start(bf16[2,8,64,128]{3,2,1,0:T(8,128)(2,1)S(1)} %add_sums.5.refs_2_.refs_0_), channel_id=1, source_target_pairs={{0,3},{1,2},{2,1},{3,0},{4,7},{5,6},{6,5},{7,4},{8,11},{9,10},{10,... | collective-permute-start | bytes 786440 | tf_op jit(solution)/shard_map/ppermute | solution.py:539
  52.5 0.6 collective-permute-start.7
  53.1 7.3 %make_tables.1 = (bf16[2048,2176]{1,0:T(8,128)(2,1)S(1)}, bf16[8,128,256]{2,1,0:T(8,128)(2,1)S(1)}, f32[64,128]{1,0:T(8,128)S(1)}) custom-call(s32[1]{0:T(128)} %bitcast.9.facet_ref, s32[8,32]{1,0:T(8,128)S(1)} %copy-done.2, s32[8]{0:T(128)S(1)} %copy-done.3, bf16[2,8,64,128]{3,2,1,0:T(8,128)(2,1)S(1)} %add_sums.5.refs_2_.refs_0_), custom_call_target="tpu_custom_call" | custom-call | flops 35651584 | bytes 8912896 | tf_op jit(solution)/shard_map/make_tables/pallas_call | solution.py:363
  60.4 0.1 add_sums.7.refs_4_.refs_8_
  60.5 2.5 %collective-permute-start.6 = (bf16[2,8,64,128]{3,2,1,0:T(8,128)(2,1)S(1)}, bf16[2,8,64,128]{3,2,1,0:T(8,128)(2,1)S(1)}, u32[]{:S(2)}, u32[]{:S(2)}) collective-permute-start(bf16[2,8,64,128]{3,2,1,0:T(8,128)(2,1)S(1)} %add_sums.7.refs_4_.refs_8_), channel_id=1, source_target_pairs={{0,2},{1,3},{2,0},{3,1},{4,6},{5,7},{6,4},{7,5},{8,10},{9,11},{10,... | collective-permute-start | bytes 786440 | tf_op jit(solution)/shard_map/ppermute | solution.py:539
  63.0 1.5 %collective-permute-start.5 = (bf16[2,8,64,128]{3,2,1,0:T(8,128)(2,1)S(1)}, bf16[2,8,64,128]{3,2,1,0:T(8,128)(2,1)S(1)}, u32[]{:S(2)}, u32[]{:S(2)}) collective-permute-start(bf16[2,8,64,128]{3,2,1,0:T(8,128)(2,1)S(1)} %add_sums.7.refs_4_.refs_8_), channel_id=1, source_target_pairs={{0,1},{1,0},{2,3},{3,2},{4,5},{5,4},{6,7},{7,6},{8,9},{9,8},{10,11... | collective-permute-start | bytes 786440 | tf_op jit(solution)/shard_map/ppermute | solution.py:539
  64.5 0.1 collective-permute-start.4
  64.5 3.5 %collective-permute-done.8.refs_2_ = bf16[2,8,64,128]{3,2,1,0:T(8,128)(2,1)S(1)} collective-permute-done((bf16[2,8,64,128]{3,2,1,0:T(8,128)(2,1)S(1)}, bf16[2,8,64,128]{3,2,1,0:T(8,128)(2,1)S(1)}, u32[]{:S(2)}, u32[]{:S(2)}) %collective-permute-start.8) | collective-permute-done | bytes 262176 | tf_op jit(solution)/shard_map/ppermute | solution.py:539
  68.0 8.6 %add_image.3.refs_5_ = f32[16,64,2048]{2,1,0:T(8,128)} custom-call(s32[1]{0:T(128)} %bitcast.flip_ref.z1_ref, s32[1]{0:T(128)} %bitcast.1.z0_ref, s32[1]{0:T(128)} %bitcast.2.x_ref, bf16[2,8,64,128]{3,2,1,0:T(8,128)(2,1)S(1)} %add_sums.5.refs_2_.refs_0_, bf16[2,8,64,128]{3,2,1,0:T(8,128)(2,1)S(1)} %collective-permute-done.7.refs_1_, ...), custom_call_target="tpu_custom_call" | custom-call | flops 5368709120 | bytes 13631488 | tf_op jit(solution)/shard_map/add_image/pallas_call | solution.py:462
  76.7 4.0 %add_image.4.refs_4_ = f32[16,64,2048]{2,1,0:T(8,128)} custom-call(s32[1]{0:T(128)} %bitcast.flip_ref.z1_ref, s32[1]{0:T(128)} %bitcast.1.z0_ref, s32[1]{0:T(128)} %bitcast.2.x_ref, bf16[2,8,64,128]{3,2,1,0:T(8,128)(2,1)S(1)} %collective-permute-done.5.refs_0_, ...), custom_call_target="tpu_custom_call", output_to_operand_aliasing={{}: (8, {})} | custom-call | flops 2147483648 | bytes 10485760 | tf_op jit(solution)/shard_map/add_image/pallas_call | solution.py:462
  80.7 2.4 %add_image.5 = f32[16,64,2048]{2,1,0:T(8,128)} custom-call(s32[1]{0:T(128)} %bitcast.flip_ref.z1_ref, s32[1]{0:T(128)} %bitcast.1.z0_ref, s32[1]{0:T(128)} %bitcast.2.x_ref, bf16[2,8,64,128]{3,2,1,0:T(8,128)(2,1)S(1)} %collective-permute-done.4.refs_0_, ...), custom_call_target="tpu_custom_call", output_to_operand_aliasing={{}: (7, {})} | custom-call | flops 1073741824 | bytes 9437184 | tf_op jit(solution)/shard_map/add_image/pallas_call | solution.py:462
  (18 shorter events, 0.2 us)
Async XLA Ops:
  21.0 16.7 %all-to-all-start.1 = ((bf16[8,8,4096]{2,1,0:T(8,128)(2,1)}), bf16[8,8,4096]{2,1,0:T(8,128)(2,1)S(1)}, u32[]{:S(2)}, u32[]{:S(2)}) async-start(bf16[8,8,4096]{2,1,0:T(8,128)(2,1)} %get-tuple-element.15), calls=%async_computation.1 | async-start | bytes 1048576 | tf_op jit(solution)/shard_map/all_to_all | solution.py:520
  24.5 0.7 copy-start
  25.2 12.5 %copy-start.1 = (bf16[32,2,8]{0,2,1:T(8,128)(2,1)S(1)}, bf16[32,2,8]{0,2,1:T(8,128)(2,1)}, u32[]{:S(2)}) copy-start(bf16[32,2,8]{0,2,1:T(8,128)(2,1)} %param.8) | copy-start | bytes 3076
  32.1 1.6 %collective-permute-start = (bf16[2,8,64,128]{3,2,1,0:T(8,128)(2,1)S(1)}, bf16[2,8,64,128]{3,2,1,0:T(8,128)(2,1)S(1)}, u32[]{:S(2)}, u32[]{:S(2)}) collective-permute-start(bf16[2,8,64,128]{3,2,1,0:T(8,128)(2,1)S(1)} %get-tuple-element.17), channel_id=1, source_target_pairs={{0,8},{8,0},{1,9},{9,1},{2,10},{10,2},{3,11},{11,3},{4,12},{12,4},... | collective-permute-start | bytes 786440 | tf_op jit(solution)/shard_map/ppermute | solution.py:27
  33.7 19.3 %copy-start.2 = (s32[8,32]{1,0:T(8,128)S(1)}, s32[8,32]{1,0:T(8,128)}, u32[]{:S(2)}) copy-start(s32[8,32]{1,0:T(8,128)} %listed_ref.1) | copy-start | bytes 3076
  33.8 19.3 %copy-start.3 = (s32[8]{0:T(128)S(1)}, s32[8]{0:T(128)}, u32[]{:S(2)}) copy-start(s32[8]{0:T(128)} %count_ref.1) | copy-start | bytes 100
  33.8 11.1 %collective-permute-start.2 = (bf16[2,8,64,128]{3,2,1,0:T(8,128)(2,1)S(1)}, bf16[2,8,64,128]{3,2,1,0:T(8,128)(2,1)S(1)}, u32[]{:S(2)}, u32[]{:S(2)}) collective-permute-start(bf16[2,8,64,128]{3,2,1,0:T(8,128)(2,1)S(1)} %add_sums.4.refs_0_), channel_id=1, source_target_pairs={{0,6},{2,4},{4,2},{6,0},{1,7},{3,5},{5,3},{7,1},{8,14},{10,12},{12... | collective-permute-start | bytes 786440 | tf_op jit(solution)/shard_map/ppermute | solution.py:553
  44.8 1.6 %collective-permute-start.1 = (bf16[2,8,64,128]{3,2,1,0:T(8,128)(2,1)S(1)}, bf16[2,8,64,128]{3,2,1,0:T(8,128)(2,1)S(1)}, u32[]{:S(2)}, u32[]{:S(2)}) collective-permute-start(bf16[2,8,64,128]{3,2,1,0:T(8,128)(2,1)S(1)} %get-tuple-element.19), channel_id=1, source_target_pairs={{0,8},{8,0},{1,9},{9,1},{2,10},{10,2},{3,11},{11,3},{4,12},{12,4},... | collective-permute-start | bytes 786440 | tf_op jit(solution)/shard_map/ppermute | solution.py:27
  46.5 13.9 %collective-permute-start.3 = (bf16[2,8,64,128]{3,2,1,0:T(8,128)(2,1)S(1)}, bf16[2,8,64,128]{3,2,1,0:T(8,128)(2,1)S(1)}, u32[]{:S(2)}, u32[]{:S(2)}) collective-permute-start(bf16[2,8,64,128]{3,2,1,0:T(8,128)(2,1)S(1)} %add_sums.6.refs_0_), channel_id=1, source_target_pairs={{0,6},{2,4},{4,2},{6,0},{1,7},{3,5},{5,3},{7,1},{8,14},{10,12},{12... | collective-permute-start | bytes 786440 | tf_op jit(solution)/shard_map/ppermute | solution.py:553
  48.2 16.2 %collective-permute-start.9 = (bf16[2,8,64,128]{3,2,1,0:T(8,128)(2,1)S(1)}, bf16[2,8,64,128]{3,2,1,0:T(8,128)(2,1)S(1)}, u32[]{:S(2)}, u32[]{:S(2)}) collective-permute-start(bf16[2,8,64,128]{3,2,1,0:T(8,128)(2,1)S(1)} %add_sums.5.refs_2_.refs_0_), channel_id=1, source_target_pairs={{0,3},{1,2},{2,1},{3,0},{4,7},{5,6},{6,5},{7,4},{8,11},{9,10},{10,... | collective-permute-start | bytes 786440 | tf_op jit(solution)/shard_map/ppermute | solution.py:539
  52.5 15.5 %collective-permute-start.8 = (bf16[2,8,64,128]{3,2,1,0:T(8,128)(2,1)S(1)}, bf16[2,8,64,128]{3,2,1,0:T(8,128)(2,1)S(1)}, u32[]{:S(2)}, u32[]{:S(2)}) collective-permute-start(bf16[2,8,64,128]{3,2,1,0:T(8,128)(2,1)S(1)} %add_sums.5.refs_2_.refs_0_), channel_id=1, source_target_pairs={{0,2},{1,3},{2,0},{3,1},{4,6},{5,7},{6,4},{7,5},{8,10},{9,11},{10,... | collective-permute-start | bytes 786440 | tf_op jit(solution)/shard_map/ppermute | solution.py:539
  52.5 15.5 %collective-permute-start.7 = (bf16[2,8,64,128]{3,2,1,0:T(8,128)(2,1)S(1)}, bf16[2,8,64,128]{3,2,1,0:T(8,128)(2,1)S(1)}, u32[]{:S(2)}, u32[]{:S(2)}) collective-permute-start(bf16[2,8,64,128]{3,2,1,0:T(8,128)(2,1)S(1)} %add_sums.5.refs_2_.refs_0_), channel_id=1, source_target_pairs={{0,1},{1,0},{2,3},{3,2},{4,5},{5,4},{6,7},{7,6},{8,9},{9,8},{10,11... | collective-permute-start | bytes 786440 | tf_op jit(solution)/shard_map/ppermute | solution.py:539
  60.5 16.2 %collective-permute-start.6 = (bf16[2,8,64,128]{3,2,1,0:T(8,128)(2,1)S(1)}, bf16[2,8,64,128]{3,2,1,0:T(8,128)(2,1)S(1)}, u32[]{:S(2)}, u32[]{:S(2)}) collective-permute-start(bf16[2,8,64,128]{3,2,1,0:T(8,128)(2,1)S(1)} %add_sums.7.refs_4_.refs_8_), channel_id=1, source_target_pairs={{0,2},{1,3},{2,0},{3,1},{4,6},{5,7},{6,4},{7,5},{8,10},{9,11},{10,... | collective-permute-start | bytes 786440 | tf_op jit(solution)/shard_map/ppermute | solution.py:539
  63.0 13.7 %collective-permute-start.5 = (bf16[2,8,64,128]{3,2,1,0:T(8,128)(2,1)S(1)}, bf16[2,8,64,128]{3,2,1,0:T(8,128)(2,1)S(1)}, u32[]{:S(2)}, u32[]{:S(2)}) collective-permute-start(bf16[2,8,64,128]{3,2,1,0:T(8,128)(2,1)S(1)} %add_sums.7.refs_4_.refs_8_), channel_id=1, source_target_pairs={{0,1},{1,0},{2,3},{3,2},{4,5},{5,4},{6,7},{7,6},{8,9},{9,8},{10,11... | collective-permute-start | bytes 786440 | tf_op jit(solution)/shard_map/ppermute | solution.py:539
  64.5 16.2 %collective-permute-start.4 = (bf16[2,8,64,128]{3,2,1,0:T(8,128)(2,1)S(1)}, bf16[2,8,64,128]{3,2,1,0:T(8,128)(2,1)S(1)}, u32[]{:S(2)}, u32[]{:S(2)}) collective-permute-start(bf16[2,8,64,128]{3,2,1,0:T(8,128)(2,1)S(1)} %add_sums.7.refs_4_.refs_8_), channel_id=1, source_target_pairs={{0,3},{1,2},{2,1},{3,0},{4,7},{5,6},{6,5},{7,4},{8,11},{9,10},{10,... | collective-permute-start | bytes 786440 | tf_op jit(solution)/shard_map/ppermute | solution.py:539

commit v5 on v4

--- a/solution.py
+++ b/solution.py
@@ -20,6 +20,7 @@
 SETS = NSUB // PACK
 CHAN = ("y", "core")
 VMEM_LIMIT = 56 << 20
+LATE = (4, 5, 6, 7)
 FACET = ("z1", "z0", "x")
 
 
@@ -28,27 +29,22 @@
 
 
 def pack_kernel(
-    group_ref, flip_ref, vis_from, plane_from, cell_from, sub_from, first_ref, second_ref, *refs, shares
+    group_ref, first_ref, flip_ref, vis_from, plane_from, cell_from, sub_from, *refs, shares
 ):
-    vis_ref, plane_ref, cell_ref, sub_ref, sems, vis_sems = refs
+    out_refs = refs[:-6]
+    vis_ref, plane_ref, cell_ref, sub_ref, sems, vis_sem = refs[-6:]
     chan_shares, pol_shares, per_chan, per_pol, cores, east = shares
+    all_shares = chan_shares * pol_shares
     num_pols = vis_ref.shape[1] // 2
     row_len = vis_ref.shape[2]
-    lines = first_ref.shape[1]
+    dests, lines = out_refs[0].shape[0] * len(out_refs), out_refs[0].shape[1]
     width = row_len // lines
     half = per_pol // 2
     group = group_ref[0]
     small = [(plane_from, plane_ref), (cell_from, cell_ref), (sub_from, sub_ref)]
     small = [pltpu.make_async_copy(*pair, sems.at[k]) for k, pair in enumerate(small)]
-    dests = first_ref.shape[0]
-    step = vis_ref.shape[0] // (dests // (chan_shares * pol_shares))
-    large = []
-    for k in range(vis_ref.shape[0] // step):
-        chans = pl.ds(k * step, step)
-        large.append(
-            pltpu.make_async_copy(vis_from.at[chans], vis_ref.at[chans], vis_sems.at[k])
-        )
-    for copy in small + large:
+    large = pltpu.make_async_copy(vis_from, vis_ref, vis_sem)
+    for copy in [large] + small:
         copy.start()
     for copy in small:
         copy.wait()
@@ -66,72 +62,70 @@
         jnp.broadcast_to(subs, (lines, LANES)),
     ]
     ids = jnp.concatenate(ids, axis=1).astype(jnp.bfloat16)
-    def fill(flip):
-        for north, copy in enumerate(large):
-            copy.wait()
-            for chan_share in range(chan_shares):
-                for pol_share in range(pol_shares):
-                    found = ([], [])
-                    share = chan_share * pol_shares + pol_share
-                    dest = north * chan_shares * pol_shares
-                    dest = dest + (share // east + flip) % 2 * east + share % east
-                    for core in range(cores):
-                        chans = (north * cores + core) * chan_shares + chan_share
-                        chans = [
-                            vis_ref[chans * per_chan + k].astype(jnp.float32) for k in range(per_chan)
-                        ]
-                        for part in range(2):
-                            start = part * num_pols + pol_share * per_pol
-                            for vis in chans:
-                                found[0].append(vis[start : start + half])
-                                found[1].append(vis[start + half : start + per_pol])
-                    first_ref[dest, :, :row_len] = jnp.concatenate(found[0], 0).astype(jnp.bfloat16)
-                    first_ref[dest, :, row_len:] = ids
-                    second_ref[dest] = jnp.concatenate(found[1], 0).astype(jnp.bfloat16)
-
-    for flip in range(2):
-        pl.when(flip_ref[0] == flip)(functools.partial(fill, flip))
-
-
-def pack_rows(group, flip, vis, planes, cells, subs, shares, dests, lines):
+    large.wait()
+    for k in range(dests):
+        dest = first_ref[0] ^ k if len(out_refs) > 1 else k
+        north, share = lax.div(dest, all_shares), lax.rem(dest, all_shares)
+        share = lax.rem(lax.div(share, east) + flip_ref[0], 2) * east + lax.rem(share, east)
+        chan_share, pol_share = lax.div(share, pol_shares), lax.rem(share, pol_shares)
+        found = ([], [])
+        for core in range(cores):
+            chan = ((north * cores + core) * chan_shares + chan_share) * per_chan
+            chans = [vis_ref[chan + i].astype(jnp.float32) for i in range(per_chan)]
+            for part in range(2):
+                for vis in chans:
+                    rows = vis[part * num_pols : part * num_pols + per_pol]
+                    for other in range(1, pol_shares):
+                        start = part * num_pols + other * per_pol
+                        rows = jnp.where(pol_share == other, vis[start : start + per_pol], rows)
+                    found[0].append(rows[:half])
+                    found[1].append(rows[half:])
+        ref, slot = (out_refs[k], 0) if len(out_refs) > 1 else (out_refs[0], k)
+        ref[slot, :, :row_len] = jnp.concatenate(found[0], 0).astype(jnp.bfloat16)
+        ref[slot, :, row_len : 2 * row_len] = jnp.concatenate(found[1], 0).astype(jnp.bfloat16)
+        ref[slot, :, 2 * row_len :] = ids
+
+
+def pack_rows(device, vis, planes, cells, subs, shares, dests, lines, apart):
     row_len = vis.shape[2]
-    extra = 3 * row_len // lines + LANES
-    norths = dests // (shares[0] * shares[1])
+    width = 2 * row_len + 3 * row_len // lines + LANES
+    count = dests if apart else 1
     vmem = pl.BlockSpec(memory_space=pltpu.VMEM)
     return pl.pallas_call(
         functools.partial(pack_kernel, shares=shares),
-        out_shape=[
-            jax.ShapeDtypeStruct((dests, lines, row_len + extra), jnp.bfloat16),
-            jax.ShapeDtypeStruct((dests, lines, row_len), jnp.bfloat16),
-        ],
+        out_shape=[jax.ShapeDtypeStruct((dests // count, lines, width), jnp.bfloat16)] * count,
         grid_spec=pltpu.PrefetchScalarGridSpec(
-            num_scalar_prefetch=2,
+            num_scalar_prefetch=3,
             grid=(),
             in_specs=[pl.BlockSpec(memory_space=pl.ANY)] * 4,
-            out_specs=[vmem] * 2,
+            out_specs=[vmem] * count,
             scratch_shapes=[pltpu.VMEM(a.shape, a.dtype) for a in (vis, planes, cells, subs)]
-            + [pltpu.SemaphoreType.DMA((3,)), pltpu.SemaphoreType.DMA((norths,))],
+            + [pltpu.SemaphoreType.DMA((3,)), pltpu.SemaphoreType.DMA(())],
         ),
         compiler_params=pltpu.CompilerParams(vmem_limit_bytes=VMEM_LIMIT),
         cost_estimate=pl.CostEstimate(flops=1 << 20, bytes_accessed=3 << 20, transcendentals=0),
         name="pack_rows",
-    )(group, flip, vis, planes, cells, subs)
-
-
-def grid_kernel(place_ref, taps_ref, ids_ref, rows_ref, *refs, row_len, ids_from):
-    own_ref, other_ref, sums_ref, listed_ref, sub_ref, sem = refs[-6:]
-    sources, lines = rows_ref.shape[:2]
+    )(*device, vis, planes, cells, subs)
+
+
+def grid_kernel(place_ref, taps_ref, *refs, row_len, half, parts, begins, ends):
+    rows_refs = refs[:parts]
+    sums_ref, listed_ref, sub_ref, sem = refs[-4:]
+    each, lines = rows_refs[0].shape[:2]
+    sources = parts * each
     pols = lines // 4
     cells = 2 * pols * SG
     blocks = row_len // BLK
     width = row_len // lines
 
+    ids_from = 2 * row_len
     for source in range(sources):
-        subs = ids_ref[source, :, ids_from + 3 * width :].astype(jnp.float32)
+        subs = rows_refs[source // each][source % each, :, ids_from + 3 * width :]
+        subs = subs.astype(jnp.float32)
         listed_ref[source : source + 1] = subs[:1].astype(jnp.int32)
     copy = pltpu.make_async_copy(listed_ref, sub_ref, sem)
     copy.start()
-    sums_ref[...] = jnp.zeros_like(sums_ref)
+    sums_ref[...] = jnp.zeros_like(sums_ref) if begins else refs[parts][...]
     copy.wait()
     taps = taps_ref[...].astype(jnp.float32)
     taps = jnp.concatenate([taps, jnp.zeros((16, LANES - taps.shape[1]), jnp.float32)], axis=1)
@@ -170,8 +164,8 @@
         part = doubled(part)
         return jnp.concatenate([jnp.where(mask, part, none) for mask in masks], axis=0)
 
-    def grid_source(source):
-        ids = ids_ref[source, :, ids_from : ids_from + 3 * width]
+    def grid_source(rows_ref, slot, source):
+        ids = rows_ref[slot, :, ids_from : ids_from + 3 * width]
         ids = ids.astype(jnp.float32).astype(jnp.int32)
         for block in range(blocks):
             plane = jnp.broadcast_to(listed(ids, 0, block), (16, BLK))
@@ -179,7 +173,8 @@
             parts, masks = turned(values, listed(ids, 1, block))
             left = jnp.concatenate([spread(part, masks) for part in parts], axis=0)
             (kern_re, kern_im), masks = turned(values, listed(ids, 2, block))
-            vis = rows_ref[source, :, block * BLK : (block + 1) * BLK].astype(jnp.float32)
+            start = half * row_len + block * BLK
+            vis = rows_ref[slot, :, start : start + BLK].astype(jnp.float32)
             vis = pltpu.roll(vis, place_ref[0] * (lines // 2), 0)
             real, imag = [], []
             for first in (0, 2 * pols):
@@ -194,13 +189,23 @@
                 left, weighted, (((1,), (1,)), ((), ())), preferred_element_type=jnp.float32
             )
 
+    unroll = math.gcd(each, 4)
+
     def grid_sources(step, carry):
         for k in range(unroll):
-            grid_source(step * unroll + k)
+            slot = step * unroll + k
+            grid_source(rows_refs[0], slot, slot)
         return carry
 
-    unroll = math.gcd(sources, 4)
-    lax.fori_loop(0, sources // unroll, grid_sources, 0)
+    if parts > 1:
+        for source in range(sources):
+            grid_source(rows_refs[source // each], source % each, source)
+    else:
+        lax.fori_loop(0, each // unroll, grid_sources, 0)
+    if not ends:
+        refs[-5][...] = sums_ref[...]
+        return
+    own_ref, other_ref = refs[-6:-4]
     slot = lax.broadcasted_iota(jnp.int32, (2 * SG, LANES), 1) // SG
 
     def finish(group):
@@ -228,22 +233,34 @@
         finish(group)
 
 
-def grid_rows(place, taps, ids, rows, row_len, after):
-    sources, lines, _ = rows.shape
+def grid_rows(place, taps, rows, row_len, half, after, begun=None, ends=True):
+    lines = rows[0].shape[1]
+    sources = len(rows) * rows[0].shape[0]
     pols = lines // 4
-    shape = (pols, SETS, 2 * SG, LANES)
+    sums = (NSUB, 2 * SG, 4 * pols * SG)
+    done = jax.ShapeDtypeStruct((pols, SETS, 2 * SG, LANES), jnp.bfloat16)
+    done = [done] * 2 if ends else [jax.ShapeDtypeStruct(sums, jnp.float32)]
+    begun = [] if begun is None else [begun]
     vmem = pl.BlockSpec(memory_space=pltpu.VMEM)
     flops = 2 * sources * row_len * 2 * SG * 4 * pols * SG
     return pl.pallas_call(
-        functools.partial(grid_kernel, row_len=row_len, ids_from=row_len),
-        out_shape=[jax.ShapeDtypeStruct(shape, jnp.bfloat16)] * 2,
+        functools.partial(
+            grid_kernel,
+            row_len=row_len,
+            half=half,
+            parts=len(rows),
+            begins=not begun,
+            ends=ends,
+        ),
+        out_shape=done,
         grid_spec=pltpu.PrefetchScalarGridSpec(
             num_scalar_prefetch=1,
             grid=(),
-            in_specs=[vmem] * 3 + [pl.BlockSpec(memory_space=pl.ANY)] * len(after),
-            out_specs=[vmem] * 2,
+            in_specs=[vmem] * (1 + len(rows) + len(begun))
+            + [pl.BlockSpec(memory_space=pl.ANY)] * len(after),
+            out_specs=[vmem] * len(done),
             scratch_shapes=[
-                pltpu.VMEM((NSUB, 2 * SG, 4 * pols * SG), jnp.float32),
+                pltpu.VMEM(sums, jnp.float32),
                 pltpu.VMEM((sources, LANES), jnp.int32),
                 pltpu.SMEM((sources, LANES), jnp.int32),
                 pltpu.SemaphoreType.DMA(()),
@@ -254,7 +271,7 @@
             flops=flops * 8, bytes_accessed=2 << 20, transcendentals=0
         ),
         name="grid_rows",
-    )(place, taps, ids, rows, *after)
+    )(place, taps, *rows, *begun, *after)
 
 
 def add_kernel(*refs, terms):
@@ -505,9 +522,10 @@
         return jnp.reshape(value, (1,)).astype(jnp.int32)
 
     vis = visibilities.reshape(num_chans, num_parts, row_len)
+    inner = ("y", "z0", "x")
+    apart = north == upper == east == 2
     sent = pack_rows(
-        scalar(lax.axis_index(CHAN)),
-        scalar(z1),
+        [scalar(lax.axis_index(CHAN)), scalar(lax.axis_index(inner)), scalar(z1)],
         vis,
         w_index,
         cell_offsets,
@@ -515,17 +533,26 @@
         (chan_shares, pol_shares, per_chan, per_pol, cores, east),
         north * shares,
         lines,
+        apart,
     )
-    rows = [
-        lax.all_to_all(part, ("y", "z0", "x"), split_axis=0, concat_axis=0, tiled=True)
-        for part in sent
-    ]
+    if apart:
+        rows = [sent[0]]
+        for k in range(1, len(sent)):
+            route = [(i, i ^ k) for i in range(len(sent))]
+            rows.append(lax.ppermute(sent[k], inner, route))
+    else:
+        rows = [lax.all_to_all(sent[0], inner, split_axis=0, concat_axis=0, tiled=True)]
     taps = w_kernel.transpose(1, 2, 0).reshape(-1, w_kernel.shape[0])
     place = scalar(lax.axis_index("core"))
     scale = 1.0 / math.sqrt(groups * facets * row_len)
 
     def gridded(half, after):
-        own, other = grid_rows(place, taps, rows[0], rows[half], row_len, after)
+        begun, left = None, rows
+        if half == 0 and len(rows) > 1:
+            left = [rows[k] for k in LATE]
+            begun = [rows[k] for k in range(len(rows)) if k not in LATE]
+            begun = grid_rows(place, taps, begun, row_len, half, after, ends=False)[0]
+        own, other = grid_rows(place, taps, left, row_len, half, after, begun)
         return own, swap(other, "core")
 
     def shifted(piece, z_step, x_step):
@@ -573,19 +600,24 @@
     places = places[0] + places[1]
     parts = len(first_pieces)
     image = None
-    cuts = (0, parts + 1, 2 * parts - 1, 2 * parts)
-    for begin, end in zip(cuts, cuts[1:]):
+    calls = (
+        [*range(east), parts],
+        range(east, parts),
+        range(parts + 1, 2 * parts - 1),
+        [2 * parts - 1],
+    )
+    for chosen in calls:
         image = add_image(
             image,
             device,
-            places[begin:end],
-            pieces[begin:end],
+            [places[k] for k in chosen],
+            [pieces[k] for k in chosen],
             turn,
             table,
             keep,
             total_pols,
             scale,
-            () if begin else (second,),
+            (second,),
         )
     return image.reshape(own_chans, num_pols, FY, FX)
 

time: 83.6 us -> 77.6 us (0.928)
  blocking collectives: 18.3 us -> 0 us
  starting transfers between devices: 18.3 us -> 26.9 us
  Pallas kernels: 39.1 us -> 40.6 us
  waiting for transfers between devices: 6.5 us -> 7.98 us
  local copies, waits for them, and re-layouts: 0.7 us -> 1.62 us
    all_to_all x1 -> x0, blocking collectives: 18.3 us -> none  [shards(): lax.all_to_all(part, ('y', 'z0', 'x'), split_axis=0, concat_axis=0, tiled...]
    ppermute x0 -> x7, starting transfers between devices: none -> 12.7 us  [shards(): rows.append(lax.ppermute(sent[k], inner, route))]
    all_to_all x1 -> x0, starting transfers between devices: 3.49 us -> none  [shards(): lax.all_to_all(part, ('y', 'z0', 'x'), split_axis=0, concat_axis=0, tiled...]
    ppermute x0 -> x7, waiting for transfers between devices: none -> 2.92 us  [shards(): rows.append(lax.ppermute(sent[k], inner, route))]
    ppermute x6, waiting for transfers between devices: 3.53 us -> 2.08 us  [shifted(): return lax.ppermute(piece, ('z0', 'x'), route)]
    pallas_call x3 -> x4, Pallas kernels: 15 us -> 16 us  [add_image(): pl.pallas_call(functools.partial(image_kernel, places=places, scale=scale...]
    unnamed x8 -> x12, local copies, waits for them, and re-layouts: 0.7 us -> 1.62 us
    pallas_call x2 -> x3, Pallas kernels: 13.8 us -> 14.3 us  [grid_rows(): pl.pallas_call(functools.partial(grid_kernel, row_len=row_len, half=half,...]
  transfers between devices with their start and end apart: 11 -> 17, of which waited for: 3 -> 7; matrix products, arithmetic and copies ran while one was open for 0% -> 0% of each run, Pallas kernels for 41% -> 41%
where the time goes in v5:
time: 77.6 us; the launch traced here: 77.4 us
  Pallas kernels  40.6 us (52%)
  starting transfers between devices  26.9 us (35%)
  waiting for transfers between devices  7.98 us (10%)
  local copies, waits for them, and re-layouts  1.62 us (2%)
    pallas_call x4, Pallas kernels, add_image(): pl.pallas_call(functools.partial(image_kernel, places=places, scale=scale...  16 us
    pallas_call x3, Pallas kernels, grid_rows(): pl.pallas_call(functools.partial(grid_kernel, row_len=row_len, half=half,...  14.3 us
    ppermute x7, starting transfers between devices, shards(): rows.append(lax.ppermute(sent[k], inner, route))  12.7 us
    ppermute x6, starting transfers between devices, shifted(): return lax.ppermute(piece, ('z0', 'x'), route)  8.64 us
    pallas_call x1, Pallas kernels, make_tables(): pl.pallas_call(functools.partial(tables_kernel, period=period), out_shape...  7.3 us
    ppermute x2, starting transfers between devices, mirrored(): return lax.ppermute(block, ('z1', 'z0'), [(i, 3 - i) for i in range(4)])  5.37 us
    ppermute x2, waiting for transfers between devices, swap(): return lax.ppermute(block, axis, [(0, 1), (1, 0)])  2.96 us
    ppermute x7, waiting for transfers between devices, shards(): rows.append(lax.ppermute(sent[k], inner, route))  2.92 us
  transfers between devices with their start and end apart: 17, of which 7 were waited for; matrix products, arithmetic and copies ran while one was open for 0% of the time, Pallas kernels for 41%

profile of v5, /device:TPU:0, one launch (start us, length us, event | category | flops | bytes accessed | tf_op | source)
XLA Modules:
  0.0 77.4 jit_solution(4962272524691790683)
XLA Ops:
  0.0 2.7 %pack_rows.1 = (bf16[1,8,9856]{2,1,0:T(8,128)(2,1)}, bf16[1,8,9856]{2,1,0:T(8,128)(2,1)}, bf16[1,8,9856]{2,1,0:T(8,128)(2,1)}, bf16[1,8,9856]{2,1,0:T(8,128)(2,1...) custom-call(s32[1]{0:T(128)} %bitcast.6.group_ref, ...), custom_call_target="tpu_custom_call" | custom-call | flops 1048576 | bytes 3145728 | tf_op jit(solution)/shard_map/pack_rows/pallas_call | solution.py:94
  2.7 3.0 %collective-permute-start = (bf16[1,8,9856]{2,1,0:T(8,128)(2,1)}, bf16[1,8,9856]{2,1,0:T(8,128)(2,1)S(1)}, u32[]{:S(2)}, u32[]{:S(2)}) collective-permute-start(bf16[1,8,9856]{2,1,0:T(8,128)(2,1)} %get-tuple-element.21), channel_id=1, source_target_pairs={{0,1},{1,0},{2,3},{3,2},{16,17},{17,16},{18,19},{19,18},{4,5},{5,4... | collective-permute-start | bytes 473096 | tf_op jit(solution)/shard_map/ppermute | solution.py:542
  5.7 1.6 %collective-permute-start.1 = (bf16[1,8,9856]{2,1,0:T(8,128)(2,1)}, bf16[1,8,9856]{2,1,0:T(8,128)(2,1)S(1)}, u32[]{:S(2)}, u32[]{:S(2)}) collective-permute-start(bf16[1,8,9856]{2,1,0:T(8,128)(2,1)} %get-tuple-element.22), channel_id=1, source_target_pairs={{0,2},{1,3},{2,0},{3,1},{16,18},{17,19},{18,16},{19,17},{4,6},{5,7... | collective-permute-start | bytes 473096 | tf_op jit(solution)/shard_map/ppermute | solution.py:542
  7.3 1.9 %collective-permute-start.3 = (bf16[1,8,9856]{2,1,0:T(8,128)(2,1)}, bf16[1,8,9856]{2,1,0:T(8,128)(2,1)S(1)}, u32[]{:S(2)}, u32[]{:S(2)}) collective-permute-start(bf16[1,8,9856]{2,1,0:T(8,128)(2,1)} %get-tuple-element.24), channel_id=1, source_target_pairs={{0,16},{1,17},{2,18},{3,19},{16,0},{17,1},{18,2},{19,3},{4,20},{5,... | collective-permute-start | bytes 473096 | tf_op jit(solution)/shard_map/ppermute | solution.py:542
  9.3 1.4 %collective-permute-start.4 = (bf16[1,8,9856]{2,1,0:T(8,128)(2,1)}, bf16[1,8,9856]{2,1,0:T(8,128)(2,1)S(1)}, u32[]{:S(2)}, u32[]{:S(2)}) collective-permute-start(bf16[1,8,9856]{2,1,0:T(8,128)(2,1)} %get-tuple-element.25), channel_id=1, source_target_pairs={{0,17},{1,16},{2,19},{3,18},{16,1},{17,0},{18,3},{19,2},{4,21},{5,... | collective-permute-start | bytes 473096 | tf_op jit(solution)/shard_map/ppermute | solution.py:542
  10.7 2.5 %collective-permute-start.5 = (bf16[1,8,9856]{2,1,0:T(8,128)(2,1)}, bf16[1,8,9856]{2,1,0:T(8,128)(2,1)S(1)}, u32[]{:S(2)}, u32[]{:S(2)}) collective-permute-start(bf16[1,8,9856]{2,1,0:T(8,128)(2,1)} %get-tuple-element.26), channel_id=1, source_target_pairs={{0,18},{1,19},{2,16},{3,17},{16,2},{17,3},{18,0},{19,1},{4,22},{5,... | collective-permute-start | bytes 473096 | tf_op jit(solution)/shard_map/ppermute | solution.py:542
  13.2 2.2 %collective-permute-start.6 = (bf16[1,8,9856]{2,1,0:T(8,128)(2,1)}, bf16[1,8,9856]{2,1,0:T(8,128)(2,1)S(1)}, u32[]{:S(2)}, u32[]{:S(2)}) collective-permute-start(bf16[1,8,9856]{2,1,0:T(8,128)(2,1)} %get-tuple-element.27), channel_id=1, source_target_pairs={{0,19},{1,18},{2,17},{3,16},{16,3},{17,2},{18,1},{19,0},{4,23},{5,... | collective-permute-start | bytes 473096 | tf_op jit(solution)/shard_map/ppermute | solution.py:542
  17.1 3.6 %grid_rows.3.refs_4_ = f32[32,64,256]{2,1,0:T(8,128)S(1)} custom-call(s32[1]{0:T(128)} %bitcast.3.place_ref, bf16[16,32]{1,0:T(8,128)(2,1)S(1)} %bitcast.12, bf16[1,8,9856]{2,1,0:T(8,128)(2,1)S(1)} %copy-done, bf16[1,8,9856]{2,1,0:T(8,128)(2,1)S(1)} %collective-permute-done.refs_1_, bf16[1,8,9856]{2,1,0:T(8,128)(2,1)S(1)} %collective-permute-done.1.refs_2_, ...), custom_call_target="tpu_custom_call" | custom-call | flops 4294967296 | bytes 2097152 | tf_op jit(solution)/shard_map/grid_rows/pallas_call | solution.py:246
  21.6 2.0 %collective-permute-done.6.refs_3_.refs_7_ = bf16[1,8,9856]{2,1,0:T(8,128)(2,1)S(1)} collective-permute-done((bf16[1,8,9856]{2,1,0:T(8,128)(2,1)}, bf16[1,8,9856]{2,1,0:T(8,128)(2,1)S(1)}, u32[]{:S(2)}, u32[]{:S(2)}) %collective-permute-start.6) | collective-permute-done | bytes 157728 | tf_op jit(solution)/shard_map/ppermute | solution.py:542
  23.6 3.9 %grid_rows.4 = (bf16[2,8,64,128]{3,2,1,0:T(8,128)(2,1)S(1)}, bf16[2,8,64,128]{3,2,1,0:T(8,128)(2,1)S(1)}) custom-call(s32[1]{0:T(128)} %bitcast.3.place_ref, bf16[16,32]{1,0:T(8,128)(2,1)S(1)} %bitcast.13, bf16[1,8,9856]{2,1,0:T(8,128)(2,1)S(1)} %collective-permute-done.3.refs_0_.refs_4_, bf16[1,8,9856]{2,1,0:T(8,128)(2,1)S(1)} %collective-permute-done.4.refs_1_.refs_5_, ...), custom_call_target="tpu_custom_call" | custom-call | flops 4294967296 | bytes 2097152 | tf_op jit(solution)/shard_map/grid_rows/pallas_call | solution.py:246
  27.6 1.5 %collective-permute-done.7.refs_1_ = bf16[2,8,64,128]{3,2,1,0:T(8,128)(2,1)S(1)} collective-permute-done((bf16[2,8,64,128]{3,2,1,0:T(8,128)(2,1)S(1)}, bf16[2,8,64,128]{3,2,1,0:T(8,128)(2,1)S(1)}, u32[]{:S(2)}, u32[]{:S(2)}) %collective-permute-start.7) | collective-permute-done | bytes 262176 | tf_op jit(solution)/shard_map/ppermute | solution.py:28
  29.2 3.4 %collective-permute-start.9 = (bf16[2,8,64,128]{3,2,1,0:T(8,128)(2,1)S(1)}, bf16[2,8,64,128]{3,2,1,0:T(8,128)(2,1)S(1)}, u32[]{:S(2)}, u32[]{:S(2)}) collective-permute-start(bf16[2,8,64,128]{3,2,1,0:T(8,128)(2,1)S(1)} %add_sums.4.refs_8_.refs_0_), channel_id=1, source_target_pairs={{0,6},{2,4},{4,2},{6,0},{1,7},{3,5},{5,3},{7,1},{8,14},{10,12},{12... | collective-permute-start | bytes 786440 | tf_op jit(solution)/shard_map/ppermute | solution.py:580
  32.6 6.8 %grid_rows.5 = (bf16[2,8,64,128]{3,2,1,0:T(8,128)(2,1)S(1)}, bf16[2,8,64,128]{3,2,1,0:T(8,128)(2,1)S(1)}) custom-call(s32[1]{0:T(128)} %bitcast.3.place_ref, bf16[16,32]{1,0:T(8,128)(2,1)S(1)} %bitcast.14, bf16[1,8,9856]{2,1,0:T(8,128)(2,1)S(1)} %copy-done.1, bf16[1,8,9856]{2,1,0:T(8,128)(2,1)S(1)} %collective-permute-done.refs_1_, ...), custom_call_target="tpu_custom_call" | custom-call | flops 8589934592 | bytes 2097152 | tf_op jit(solution)/shard_map/grid_rows/pallas_call | solution.py:246
  39.6 1.4 %collective-permute-done.8.refs_1_ = bf16[2,8,64,128]{3,2,1,0:T(8,128)(2,1)S(1)} collective-permute-done((bf16[2,8,64,128]{3,2,1,0:T(8,128)(2,1)S(1)}, bf16[2,8,64,128]{3,2,1,0:T(8,128)(2,1)S(1)}, u32[]{:S(2)}, u32[]{:S(2)}) %collective-permute-start.8) | collective-permute-done | bytes 262176 | tf_op jit(solution)/shard_map/ppermute | solution.py:28
  41.1 2.0 %collective-permute-start.10 = (bf16[2,8,64,128]{3,2,1,0:T(8,128)(2,1)S(1)}, bf16[2,8,64,128]{3,2,1,0:T(8,128)(2,1)S(1)}, u32[]{:S(2)}, u32[]{:S(2)}) collective-permute-start(bf16[2,8,64,128]{3,2,1,0:T(8,128)(2,1)S(1)} %add_sums.6.refs_0_), channel_id=1, source_target_pairs={{0,6},{2,4},{4,2},{6,0},{1,7},{3,5},{5,3},{7,1},{8,14},{10,12},{12... | collective-permute-start | bytes 786440 | tf_op jit(solution)/shard_map/ppermute | solution.py:580
  43.1 1.5 %collective-permute-start.16 = (bf16[2,8,64,128]{3,2,1,0:T(8,128)(2,1)S(1)}, bf16[2,8,64,128]{3,2,1,0:T(8,128)(2,1)S(1)}, u32[]{:S(2)}, u32[]{:S(2)}) collective-permute-start(bf16[2,8,64,128]{3,2,1,0:T(8,128)(2,1)S(1)} %add_sums.5.refs_2_.refs_0_), channel_id=1, source_target_pairs={{0,1},{1,0},{2,3},{3,2},{4,5},{5,4},{6,7},{7,6},{8,9},{9,8},{10,11... | collective-permute-start | bytes 786440 | tf_op jit(solution)/shard_map/ppermute | solution.py:566
  44.6 3.3 %collective-permute-start.14 = (bf16[2,8,64,128]{3,2,1,0:T(8,128)(2,1)S(1)}, bf16[2,8,64,128]{3,2,1,0:T(8,128)(2,1)S(1)}, u32[]{:S(2)}, u32[]{:S(2)}) collective-permute-start(bf16[2,8,64,128]{3,2,1,0:T(8,128)(2,1)S(1)} %add_sums.5.refs_2_.refs_0_), channel_id=1, source_target_pairs={{0,2},{1,3},{2,0},{3,1},{4,6},{5,7},{6,4},{7,5},{8,10},{9,11},{10,... | collective-permute-start | bytes 786440 | tf_op jit(solution)/shard_map/ppermute | solution.py:566
  48.1 7.3 %make_tables.1 = (bf16[2048,2176]{1,0:T(8,128)(2,1)S(1)}, bf16[8,128,256]{2,1,0:T(8,128)(2,1)S(1)}, f32[64,128]{1,0:T(8,128)S(1)}) custom-call(s32[1]{0:T(128)} %bitcast.10.facet_ref, s32[8,32]{1,0:T(8,128)S(1)} %copy-done.4, s32[8]{0:T(128)S(1)} %copy-done.5, bf16[2,8,64,128]{3,2,1,0:T(8,128)(2,1)S(1)} %add_sums.5.refs_2_.refs_0_), custom_call_target="tpu_custom_call" | custom-call | flops 35651584 | bytes 8912896 | tf_op jit(solution)/shard_map/make_tables/pallas_call | solution.py:380
  56.7 2.4 %collective-permute-start.13 = (bf16[2,8,64,128]{3,2,1,0:T(8,128)(2,1)S(1)}, bf16[2,8,64,128]{3,2,1,0:T(8,128)(2,1)S(1)}, u32[]{:S(2)}, u32[]{:S(2)}) collective-permute-start(bf16[2,8,64,128]{3,2,1,0:T(8,128)(2,1)S(1)} %add_sums.7.refs_2_.refs_6_.refs_5_.refs_4_), channel_id=1, source_target_pairs={{0,2},{1,3},{2,0},{3,1},{4,6},{5,7},{6,4},{7,5},{8,10},{9,11},{10,... | collective-permute-start | bytes 786440 | tf_op jit(solution)/shard_map/ppermute | solution.py:566
  59.1 5.5 %add_image.4.refs_6_ = f32[16,64,2048]{2,1,0:T(8,128)} custom-call(s32[1]{0:T(128)} %bitcast.flip_ref.z1_ref, s32[1]{0:T(128)} %bitcast.1.z0_ref, s32[1]{0:T(128)} %bitcast.2.x_ref, bf16[2,8,64,128]{3,2,1,0:T(8,128)(2,1)S(1)} %add_sums.5.refs_2_.refs_0_, bf16[2,8,64,128]{3,2,1,0:T(8,128)(2,1)S(1)} %collective-permute-done.16.refs_1_, ...), custom_call_target="tpu_custom_call" | custom-call | flops 3221225472 | bytes 11534336 | tf_op jit(solution)/shard_map/add_image/pallas_call | solution.py:479
  64.7 4.0 %add_image.5.refs_6_ = f32[16,64,2048]{2,1,0:T(8,128)} custom-call(s32[1]{0:T(128)} %bitcast.flip_ref.z1_ref, s32[1]{0:T(128)} %bitcast.1.z0_ref, s32[1]{0:T(128)} %bitcast.2.x_ref, bf16[2,8,64,128]{3,2,1,0:T(8,128)(2,1)S(1)} %collective-permute-done.14.refs_0_, ...), custom_call_target="tpu_custom_call", output_to_operand_aliasing={{}: (9, {})} | custom-call | flops 2147483648 | bytes 10485760 | tf_op jit(solution)/shard_map/add_image/pallas_call | solution.py:479
  68.7 4.0 %add_image.6.refs_5_ = f32[16,64,2048]{2,1,0:T(8,128)} custom-call(s32[1]{0:T(128)} %bitcast.flip_ref.z1_ref, s32[1]{0:T(128)} %bitcast.1.z0_ref, s32[1]{0:T(128)} %bitcast.2.x_ref, bf16[2,8,64,128]{3,2,1,0:T(8,128)(2,1)S(1)} %collective-permute-done.12.refs_0_, ...), custom_call_target="tpu_custom_call", output_to_operand_aliasing={{}: (9, {})} | custom-call | flops 2147483648 | bytes 10485760 | tf_op jit(solution)/shard_map/add_image/pallas_call | solution.py:479
  72.7 2.1 %collective-permute-done.11.refs_0_ = bf16[2,8,64,128]{3,2,1,0:T(8,128)(2,1)S(1)} collective-permute-done((bf16[2,8,64,128]{3,2,1,0:T(8,128)(2,1)S(1)}, bf16[2,8,64,128]{3,2,1,0:T(8,128)(2,1)S(1)}, u32[]{:S(2)}, u32[]{:S(2)}) %collective-permute-start.11) | collective-permute-done | bytes 262176 | tf_op jit(solution)/shard_map/ppermute | solution.py:566
  74.8 2.4 %add_image.7 = f32[16,64,2048]{2,1,0:T(8,128)} custom-call(s32[1]{0:T(128)} %bitcast.flip_ref.z1_ref, s32[1]{0:T(128)} %bitcast.1.z0_ref, s32[1]{0:T(128)} %bitcast.2.x_ref, bf16[2,8,64,128]{3,2,1,0:T(8,128)(2,1)S(1)} %collective-permute-done.11.refs_0_, ...), custom_call_target="tpu_custom_call", output_to_operand_aliasing={{}: (8, {})} | custom-call | flops 1073741824 | bytes 9437184 | tf_op jit(solution)/shard_map/add_image/pallas_call | solution.py:479
  (35 shorter events, 4.5 us)
Async XLA Ops:
  0.0 23.6 %copy-start.3 = (bf16[32,2,8]{0,2,1:T(8,128)(2,1)S(1)}, bf16[32,2,8]{0,2,1:T(8,128)(2,1)}, u32[]{:S(2)}) copy-start(bf16[32,2,8]{0,2,1:T(8,128)(2,1)} %param.8) | copy-start | bytes 3076
  2.7 8.0 %collective-permute-start = (bf16[1,8,9856]{2,1,0:T(8,128)(2,1)}, bf16[1,8,9856]{2,1,0:T(8,128)(2,1)S(1)}, u32[]{:S(2)}, u32[]{:S(2)}) collective-permute-start(bf16[1,8,9856]{2,1,0:T(8,128)(2,1)} %get-tuple-element.21), channel_id=1, source_target_pairs={{0,1},{1,0},{2,3},{3,2},{16,17},{17,16},{18,19},{19,18},{4,5},{5,4... | collective-permute-start | bytes 473096 | tf_op jit(solution)/shard_map/ppermute | solution.py:542
  5.7 7.5 %collective-permute-start.1 = (bf16[1,8,9856]{2,1,0:T(8,128)(2,1)}, bf16[1,8,9856]{2,1,0:T(8,128)(2,1)S(1)}, u32[]{:S(2)}, u32[]{:S(2)}) collective-permute-start(bf16[1,8,9856]{2,1,0:T(8,128)(2,1)} %get-tuple-element.22), channel_id=1, source_target_pairs={{0,2},{1,3},{2,0},{3,1},{16,18},{17,19},{18,16},{19,17},{4,6},{5,7... | collective-permute-start | bytes 473096 | tf_op jit(solution)/shard_map/ppermute | solution.py:542
  7.3 8.2 %collective-permute-start.2 = (bf16[1,8,9856]{2,1,0:T(8,128)(2,1)}, bf16[1,8,9856]{2,1,0:T(8,128)(2,1)S(1)}, u32[]{:S(2)}, u32[]{:S(2)}) collective-permute-start(bf16[1,8,9856]{2,1,0:T(8,128)(2,1)} %get-tuple-element.23), channel_id=1, source_target_pairs={{0,3},{1,2},{2,1},{3,0},{16,19},{17,18},{18,17},{19,16},{4,7},{5,6... | collective-permute-start | bytes 473096 | tf_op jit(solution)/shard_map/ppermute | solution.py:542
  7.3 13.5 %collective-permute-start.3 = (bf16[1,8,9856]{2,1,0:T(8,128)(2,1)}, bf16[1,8,9856]{2,1,0:T(8,128)(2,1)S(1)}, u32[]{:S(2)}, u32[]{:S(2)}) collective-permute-start(bf16[1,8,9856]{2,1,0:T(8,128)(2,1)} %get-tuple-element.24), channel_id=1, source_target_pairs={{0,16},{1,17},{2,18},{3,19},{16,0},{17,1},{18,2},{19,3},{4,20},{5,... | collective-permute-start | bytes 473096 | tf_op jit(solution)/shard_map/ppermute | solution.py:542
  9.3 12.1 %collective-permute-start.4 = (bf16[1,8,9856]{2,1,0:T(8,128)(2,1)}, bf16[1,8,9856]{2,1,0:T(8,128)(2,1)S(1)}, u32[]{:S(2)}, u32[]{:S(2)}) collective-permute-start(bf16[1,8,9856]{2,1,0:T(8,128)(2,1)} %get-tuple-element.25), channel_id=1, source_target_pairs={{0,17},{1,16},{2,19},{3,18},{16,1},{17,0},{18,3},{19,2},{4,21},{5,... | collective-permute-start | bytes 473096 | tf_op jit(solution)/shard_map/ppermute | solution.py:542
  10.7 10.9 %collective-permute-start.5 = (bf16[1,8,9856]{2,1,0:T(8,128)(2,1)}, bf16[1,8,9856]{2,1,0:T(8,128)(2,1)S(1)}, u32[]{:S(2)}, u32[]{:S(2)}) collective-permute-start(bf16[1,8,9856]{2,1,0:T(8,128)(2,1)} %get-tuple-element.26), channel_id=1, source_target_pairs={{0,18},{1,19},{2,16},{3,17},{16,2},{17,3},{18,0},{19,1},{4,22},{5,... | collective-permute-start | bytes 473096 | tf_op jit(solution)/shard_map/ppermute | solution.py:542
  13.2 10.4 %collective-permute-start.6 = (bf16[1,8,9856]{2,1,0:T(8,128)(2,1)}, bf16[1,8,9856]{2,1,0:T(8,128)(2,1)S(1)}, u32[]{:S(2)}, u32[]{:S(2)}) collective-permute-start(bf16[1,8,9856]{2,1,0:T(8,128)(2,1)} %get-tuple-element.27), channel_id=1, source_target_pairs={{0,19},{1,18},{2,17},{3,16},{16,3},{17,2},{18,1},{19,0},{4,23},{5,... | collective-permute-start | bytes 473096 | tf_op jit(solution)/shard_map/ppermute | solution.py:542
  15.5 0.9 %copy-start = (bf16[1,8,9856]{2,1,0:T(8,128)(2,1)S(1)}, bf16[1,8,9856]{2,1,0:T(8,128)(2,1)}, u32[]{:S(2)}) copy-start(bf16[1,8,9856]{2,1,0:T(8,128)(2,1)} %get-tuple-element.20.refs_0_) | copy-start | bytes 473092
  16.4 0.7 copy-start.2
  20.8 11.8 %copy-start.1 = (bf16[1,8,9856]{2,1,0:T(8,128)(2,1)S(1)}, bf16[1,8,9856]{2,1,0:T(8,128)(2,1)}, u32[]{:S(2)}) copy-start(bf16[1,8,9856]{2,1,0:T(8,128)(2,1)} %get-tuple-element.20.refs_0_) | copy-start | bytes 473092
  27.5 1.6 %collective-permute-start.7 = (bf16[2,8,64,128]{3,2,1,0:T(8,128)(2,1)S(1)}, bf16[2,8,64,128]{3,2,1,0:T(8,128)(2,1)S(1)}, u32[]{:S(2)}, u32[]{:S(2)}) collective-permute-start(bf16[2,8,64,128]{3,2,1,0:T(8,128)(2,1)S(1)} %get-tuple-element.29), channel_id=1, source_target_pairs={{0,8},{8,0},{1,9},{9,1},{2,10},{10,2},{3,11},{11,3},{4,12},{12,4},... | collective-permute-start | bytes 786440 | tf_op jit(solution)/shard_map/ppermute | solution.py:28
  29.2 18.9 %copy-start.4 = (s32[8,32]{1,0:T(8,128)S(1)}, s32[8,32]{1,0:T(8,128)}, u32[]{:S(2)}) copy-start(s32[8,32]{1,0:T(8,128)} %listed_ref.1) | copy-start | bytes 3076
  29.2 18.9 %copy-start.5 = (s32[8]{0:T(128)S(1)}, s32[8]{0:T(128)}, u32[]{:S(2)}) copy-start(s32[8]{0:T(128)} %count_ref.1) | copy-start | bytes 100
  29.2 10.3 %collective-permute-start.9 = (bf16[2,8,64,128]{3,2,1,0:T(8,128)(2,1)S(1)}, bf16[2,8,64,128]{3,2,1,0:T(8,128)(2,1)S(1)}, u32[]{:S(2)}, u32[]{:S(2)}) collective-permute-start(bf16[2,8,64,128]{3,2,1,0:T(8,128)(2,1)S(1)} %add_sums.4.refs_8_.refs_0_), channel_id=1, source_target_pairs={{0,6},{2,4},{4,2},{6,0},{1,7},{3,5},{5,3},{7,1},{8,14},{10,12},{12... | collective-permute-start | bytes 786440 | tf_op jit(solution)/shard_map/ppermute | solution.py:580
  39.4 1.6 %collective-permute-start.8 = (bf16[2,8,64,128]{3,2,1,0:T(8,128)(2,1)S(1)}, bf16[2,8,64,128]{3,2,1,0:T(8,128)(2,1)S(1)}, u32[]{:S(2)}, u32[]{:S(2)}) collective-permute-start(bf16[2,8,64,128]{3,2,1,0:T(8,128)(2,1)S(1)} %get-tuple-element.31), channel_id=1, source_target_pairs={{0,8},{8,0},{1,9},{9,1},{2,10},{10,2},{3,11},{11,3},{4,12},{12,4},... | collective-permute-start | bytes 786440 | tf_op jit(solution)/shard_map/ppermute | solution.py:28
  41.1 14.3 %collective-permute-start.10 = (bf16[2,8,64,128]{3,2,1,0:T(8,128)(2,1)S(1)}, bf16[2,8,64,128]{3,2,1,0:T(8,128)(2,1)S(1)}, u32[]{:S(2)}, u32[]{:S(2)}) collective-permute-start(bf16[2,8,64,128]{3,2,1,0:T(8,128)(2,1)S(1)} %add_sums.6.refs_0_), channel_id=1, source_target_pairs={{0,6},{2,4},{4,2},{6,0},{1,7},{3,5},{5,3},{7,1},{8,14},{10,12},{12... | collective-permute-start | bytes 786440 | tf_op jit(solution)/shard_map/ppermute | solution.py:580
  43.1 16.0 %collective-permute-start.16 = (bf16[2,8,64,128]{3,2,1,0:T(8,128)(2,1)S(1)}, bf16[2,8,64,128]{3,2,1,0:T(8,128)(2,1)S(1)}, u32[]{:S(2)}, u32[]{:S(2)}) collective-permute-start(bf16[2,8,64,128]{3,2,1,0:T(8,128)(2,1)S(1)} %add_sums.5.refs_2_.refs_0_), channel_id=1, source_target_pairs={{0,1},{1,0},{2,3},{3,2},{4,5},{5,4},{6,7},{7,6},{8,9},{9,8},{10,11... | collective-permute-start | bytes 786440 | tf_op jit(solution)/shard_map/ppermute | solution.py:566
  44.6 20.1 %collective-permute-start.14 = (bf16[2,8,64,128]{3,2,1,0:T(8,128)(2,1)S(1)}, bf16[2,8,64,128]{3,2,1,0:T(8,128)(2,1)S(1)}, u32[]{:S(2)}, u32[]{:S(2)}) collective-permute-start(bf16[2,8,64,128]{3,2,1,0:T(8,128)(2,1)S(1)} %add_sums.5.refs_2_.refs_0_), channel_id=1, source_target_pairs={{0,2},{1,3},{2,0},{3,1},{4,6},{5,7},{6,4},{7,5},{8,10},{9,11},{10,... | collective-permute-start | bytes 786440 | tf_op jit(solution)/shard_map/ppermute | solution.py:566
  47.8 16.9 %collective-permute-start.15 = (bf16[2,8,64,128]{3,2,1,0:T(8,128)(2,1)S(1)}, bf16[2,8,64,128]{3,2,1,0:T(8,128)(2,1)S(1)}, u32[]{:S(2)}, u32[]{:S(2)}) collective-permute-start(bf16[2,8,64,128]{3,2,1,0:T(8,128)(2,1)S(1)} %add_sums.5.refs_2_.refs_0_), channel_id=1, source_target_pairs={{0,3},{1,2},{2,1},{3,0},{4,7},{5,6},{6,5},{7,4},{8,11},{9,10},{10,... | collective-permute-start | bytes 786440 | tf_op jit(solution)/shard_map/ppermute | solution.py:566
  55.5 13.2 %collective-permute-start.12 = (bf16[2,8,64,128]{3,2,1,0:T(8,128)(2,1)S(1)}, bf16[2,8,64,128]{3,2,1,0:T(8,128)(2,1)S(1)}, u32[]{:S(2)}, u32[]{:S(2)}) collective-permute-start(bf16[2,8,64,128]{3,2,1,0:T(8,128)(2,1)S(1)} %add_sums.7.refs_2_.refs_6_.refs_5_.refs_4_), channel_id=1, source_target_pairs={{0,1},{1,0},{2,3},{3,2},{4,5},{5,4},{6,7},{7,6},{8,9},{9,8},{10,11... | collective-permute-start | bytes 786440 | tf_op jit(solution)/shard_map/ppermute | solution.py:566
  56.7 12.0 %collective-permute-start.13 = (bf16[2,8,64,128]{3,2,1,0:T(8,128)(2,1)S(1)}, bf16[2,8,64,128]{3,2,1,0:T(8,128)(2,1)S(1)}, u32[]{:S(2)}, u32[]{:S(2)}) collective-permute-start(bf16[2,8,64,128]{3,2,1,0:T(8,128)(2,1)S(1)} %add_sums.7.refs_2_.refs_6_.refs_5_.refs_4_), channel_id=1, source_target_pairs={{0,2},{1,3},{2,0},{3,1},{4,6},{5,7},{6,4},{7,5},{8,10},{9,11},{10,... | collective-permute-start | bytes 786440 | tf_op jit(solution)/shard_map/ppermute | solution.py:566
  59.1 15.7 %collective-permute-start.11 = (bf16[2,8,64,128]{3,2,1,0:T(8,128)(2,1)S(1)}, bf16[2,8,64,128]{3,2,1,0:T(8,128)(2,1)S(1)}, u32[]{:S(2)}, u32[]{:S(2)}) collective-permute-start(bf16[2,8,64,128]{3,2,1,0:T(8,128)(2,1)S(1)} %add_sums.7.refs_2_.refs_6_.refs_5_.refs_4_), channel_id=1, source_target_pairs={{0,3},{1,2},{2,1},{3,0},{4,7},{5,6},{6,5},{7,4},{8,11},{9,10},{10,... | collective-permute-start | bytes 786440 | tf_op jit(solution)/shard_map/ppermute | solution.py:566

commit v6 on v5

--- a/solution.py
+++ b/solution.py
@@ -20,7 +20,6 @@
 SETS = NSUB // PACK
 CHAN = ("y", "core")
 VMEM_LIMIT = 56 << 20
-LATE = (4, 5, 6, 7)
 FACET = ("z1", "z0", "x")
 
 
@@ -53,15 +52,20 @@
         row = row.astype(jnp.float32)
         return jnp.concatenate([row[:, k * width : (k + 1) * width] for k in range(lines)], axis=0)
 
-    subs = sub_ref[pl.ds(group, 1), :].astype(jnp.float32)
-    subs = jnp.concatenate([subs, jnp.zeros((1, LANES - subs.shape[1]), jnp.float32)], axis=1)
-    ids = [
-        folded(plane_ref[pl.ds(group, 1), :]),
-        folded(cell_ref[0, pl.ds(group, 1), :]),
-        folded(cell_ref[1, pl.ds(group, 1), :]),
-        jnp.broadcast_to(subs, (lines, LANES)),
-    ]
-    ids = jnp.concatenate(ids, axis=1).astype(jnp.bfloat16)
+    def listed(group):
+        subs = sub_ref[pl.ds(group, 1), :].astype(jnp.float32)
+        subs = jnp.concatenate([subs, jnp.zeros((1, LANES - subs.shape[1]), jnp.float32)], axis=1)
+        found = [
+            folded(plane_ref[pl.ds(group, 1), :]),
+            folded(cell_ref[0, pl.ds(group, 1), :]),
+            folded(cell_ref[1, pl.ds(group, 1), :]),
+            jnp.broadcast_to(subs, (lines, LANES)),
+        ]
+        return jnp.concatenate(found, axis=1).astype(jnp.bfloat16)
+
+    ids = listed(group)
+    if len(out_refs) > 1:
+        ids = jnp.concatenate([ids, listed(group ^ cores)], axis=1)
     large.wait()
     for k in range(dests):
         dest = first_ref[0] ^ k if len(out_refs) > 1 else k
@@ -83,17 +87,23 @@
         ref, slot = (out_refs[k], 0) if len(out_refs) > 1 else (out_refs[0], k)
         ref[slot, :, :row_len] = jnp.concatenate(found[0], 0).astype(jnp.bfloat16)
         ref[slot, :, row_len : 2 * row_len] = jnp.concatenate(found[1], 0).astype(jnp.bfloat16)
-        ref[slot, :, 2 * row_len :] = ids
+        if ref.shape[2] > 2 * row_len:
+            ref[slot, :, 2 * row_len :] = ids
 
 
 def pack_rows(device, vis, planes, cells, subs, shares, dests, lines, apart):
     row_len = vis.shape[2]
-    width = 2 * row_len + 3 * row_len // lines + LANES
-    count = dests if apart else 1
+    ids = 3 * row_len // lines + LANES
+    widths = [2 * row_len + ids]
+    if apart:
+        widths = [2 * row_len + 2 * ids] * (dests // 2) + [2 * row_len] * (dests // 2)
+    count = len(widths)
     vmem = pl.BlockSpec(memory_space=pltpu.VMEM)
     return pl.pallas_call(
         functools.partial(pack_kernel, shares=shares),
-        out_shape=[jax.ShapeDtypeStruct((dests // count, lines, width), jnp.bfloat16)] * count,
+        out_shape=[
+            jax.ShapeDtypeStruct((dests // count, lines, width), jnp.bfloat16) for width in widths
+        ],
         grid_spec=pltpu.PrefetchScalarGridSpec(
             num_scalar_prefetch=3,
             grid=(),
@@ -108,8 +118,9 @@
     )(*device, vis, planes, cells, subs)
 
 
-def grid_kernel(place_ref, taps_ref, *refs, row_len, half, parts, begins, ends):
-    rows_refs = refs[:parts]
+def grid_kernel(place_ref, taps_ref, *refs, row_len, half, slots, begins, ends):
+    parts = len(slots)
+    rows_refs, ids_refs = refs[:parts], refs[parts : 2 * parts]
     sums_ref, listed_ref, sub_ref, sem = refs[-4:]
     each, lines = rows_refs[0].shape[:2]
     sources = parts * each
@@ -118,14 +129,17 @@
     blocks = row_len // BLK
     width = row_len // lines
 
-    ids_from = 2 * row_len
+    ids_width = 3 * width + LANES
+    ids_from = [2 * row_len + slot * ids_width for slot in slots]
     for source in range(sources):
-        subs = rows_refs[source // each][source % each, :, ids_from + 3 * width :]
+        part = source // each
+        start = ids_from[part] + 3 * width
+        subs = ids_refs[part][source % each, :, start : start + LANES]
         subs = subs.astype(jnp.float32)
         listed_ref[source : source + 1] = subs[:1].astype(jnp.int32)
     copy = pltpu.make_async_copy(listed_ref, sub_ref, sem)
     copy.start()
-    sums_ref[...] = jnp.zeros_like(sums_ref) if begins else refs[parts][...]
+    sums_ref[...] = jnp.zeros_like(sums_ref) if begins else refs[2 * parts][...]
     copy.wait()
     taps = taps_ref[...].astype(jnp.float32)
     taps = jnp.concatenate([taps, jnp.zeros((16, LANES - taps.shape[1]), jnp.float32)], axis=1)
@@ -164,8 +178,9 @@
         part = doubled(part)
         return jnp.concatenate([jnp.where(mask, part, none) for mask in masks], axis=0)
 
-    def grid_source(rows_ref, slot, source):
-        ids = rows_ref[slot, :, ids_from : ids_from + 3 * width]
+    def grid_source(part, slot, source):
+        rows_ref = rows_refs[part]
+        ids = ids_refs[part][slot, :, ids_from[part] : ids_from[part] + 3 * width]
         ids = ids.astype(jnp.float32).astype(jnp.int32)
         for block in range(blocks):
             plane = jnp.broadcast_to(listed(ids, 0, block), (16, BLK))
@@ -194,12 +209,12 @@
     def grid_sources(step, carry):
         for k in range(unroll):
             slot = step * unroll + k
-            grid_source(rows_refs[0], slot, slot)
+            grid_source(0, slot, slot)
         return carry
 
     if parts > 1:
         for source in range(sources):
-            grid_source(rows_refs[source // each], source % each, source)
+            grid_source(source // each, source % each, source)
     else:
         lax.fori_loop(0, each // unroll, grid_sources, 0)
     if not ends:
@@ -233,7 +248,7 @@
         finish(group)
 
 
-def grid_rows(place, taps, rows, row_len, half, after, begun=None, ends=True):
+def grid_rows(place, taps, rows, ids, slots, row_len, half, after, begun=None, ends=True):
     lines = rows[0].shape[1]
     sources = len(rows) * rows[0].shape[0]
     pols = lines // 4
@@ -248,7 +263,7 @@
             grid_kernel,
             row_len=row_len,
             half=half,
-            parts=len(rows),
+            slots=slots,
             begins=not begun,
             ends=ends,
         ),
@@ -256,7 +271,7 @@
         grid_spec=pltpu.PrefetchScalarGridSpec(
             num_scalar_prefetch=1,
             grid=(),
-            in_specs=[vmem] * (1 + len(rows) + len(begun))
+            in_specs=[vmem] * (1 + 2 * len(rows) + len(begun))
             + [pl.BlockSpec(memory_space=pl.ANY)] * len(after),
             out_specs=[vmem] * len(done),
             scratch_shapes=[
@@ -271,7 +286,7 @@
             flops=flops * 8, bytes_accessed=2 << 20, transcendentals=0
         ),
         name="grid_rows",
-    )(place, taps, *rows, *begun, *after)
+    )(place, taps, *rows, *ids, *begun, *after)
 
 
 def add_kernel(*refs, terms):
@@ -547,12 +562,25 @@
     scale = 1.0 / math.sqrt(groups * facets * row_len)
 
     def gridded(half, after):
-        begun, left = None, rows
-        if half == 0 and len(rows) > 1:
-            left = [rows[k] for k in LATE]
-            begun = [rows[k] for k in range(len(rows)) if k not in LATE]
-            begun = grid_rows(place, taps, begun, row_len, half, after, ends=False)[0]
-        own, other = grid_rows(place, taps, left, row_len, half, after, begun)
+        parts = len(rows)
+        ids = [rows[k % (parts // 2)] for k in range(parts)] if parts > 1 else rows
+        slots = [k * 2 // parts for k in range(parts)]
+        begun, begin = None, 0
+        if half == 0 and parts > 1:
+            begun, begin = grid_rows(
+                place,
+                taps,
+                rows[: parts // 2],
+                ids[: parts // 2],
+                slots[: parts // 2],
+                row_len,
+                half,
+                after,
+                ends=False,
+            )[0], parts // 2
+        own, other = grid_rows(
+            place, taps, rows[begin:], ids[begin:], slots[begin:], row_len, half, after, begun
+        )
         return own, swap(other, "core")
 
     def shifted(piece, z_step, x_step):

time: 77.6 us -> 77 us (level)
  waiting for transfers between devices: 7.98 us -> 6.48 us
  starting transfers between devices: 26.9 us -> 27.7 us
    ppermute x7, waiting for transfers between devices: 2.92 us -> 1.46 us  [shards(): rows.append(lax.ppermute(sent[k], inner, route))]
    unnamed x12 -> x8, local copies, waits for them, and re-layouts: 1.62 us -> 1.62 us
  transfers between devices with their start and end apart: 17 -> 17, of which waited for: 7 -> 5; matrix products, arithmetic and copies ran while one was open for 0% -> 0% of each run, Pallas kernels for 41% -> 41%
where the time goes in v6:
time: 77 us; the launch traced here: 76.8 us
  Pallas kernels  40.6 us (53%)
  starting transfers between devices  27.7 us (36%)
  waiting for transfers between devices  6.48 us (8%)
  local copies, waits for them, and re-layouts  1.62 us (2%)
    pallas_call x4, Pallas kernels, add_image(): pl.pallas_call(functools.partial(image_kernel, places=places, scale=scale...  16 us
    pallas_call x3, Pallas kernels, grid_rows(): pl.pallas_call(functools.partial(grid_kernel, row_len=row_len, half=half,...  14.3 us
    ppermute x7, starting transfers between devices, shards(): rows.append(lax.ppermute(sent[k], inner, route))  13.3 us
    ppermute x6, starting transfers between devices, shifted(): return lax.ppermute(piece, ('z0', 'x'), route)  8.63 us
    pallas_call x1, Pallas kernels, make_tables(): pl.pallas_call(functools.partial(tables_kernel, period=period), out_shape...  7.3 us
    ppermute x2, starting transfers between devices, mirrored(): return lax.ppermute(block, ('z1', 'z0'), [(i, 3 - i) for i in range(4)])  5.68 us
    ppermute x2, waiting for transfers between devices, swap(): return lax.ppermute(block, axis, [(0, 1), (1, 0)])  2.96 us
    pallas_call x1, Pallas kernels, pack_rows(): pl.pallas_call(functools.partial(pack_kernel, shares=shares), out_shape=[...  2.7 us
  transfers between devices with their start and end apart: 17, of which 5 were waited for; matrix products, arithmetic and copies ran while one was open for 0% of the time, Pallas kernels for 41%

profile of v6, /device:TPU:0, one launch (start us, length us, event | category | flops | bytes accessed | tf_op | source)
XLA Modules:
  0.0 76.8 jit_solution(3421124682015193520)
XLA Ops:
  0.0 2.7 %pack_rows.1 = (bf16[1,8,11520]{2,1,0:T(8,128)(2,1)}, bf16[1,8,11520]{2,1,0:T(8,128)(2,1)}, bf16[1,8,11520]{2,1,0:T(8,128)(2,1)}, bf16[1,8,11520]{2,1,0:T(8,128)...) custom-call(s32[1]{0:T(128)} %bitcast.6.group_ref, ...), custom_call_target="tpu_custom_call" | custom-call | flops 1048576 | bytes 3145728 | tf_op jit(solution)/shard_map/pack_rows/pallas_call | solution.py:102
  2.7 3.0 %collective-permute-start = (bf16[1,8,11520]{2,1,0:T(8,128)(2,1)}, bf16[1,8,11520]{2,1,0:T(8,128)(2,1)S(1)}, u32[]{:S(2)}, u32[]{:S(2)}) collective-permute-start(bf16[1,8,11520]{2,1,0:T(8,128)(2,1)} %get-tuple-element.21), channel_id=1, source_target_pairs={{0,1},{1,0},{2,3},{3,2},{16,17},{17,16},{18,19},{19,18},{4,5},{5,4... | collective-permute-start | bytes 552968 | tf_op jit(solution)/shard_map/ppermute | solution.py:557
  5.7 1.6 %collective-permute-start.1 = (bf16[1,8,11520]{2,1,0:T(8,128)(2,1)}, bf16[1,8,11520]{2,1,0:T(8,128)(2,1)S(1)}, u32[]{:S(2)}, u32[]{:S(2)}) collective-permute-start(bf16[1,8,11520]{2,1,0:T(8,128)(2,1)} %get-tuple-element.22), channel_id=1, source_target_pairs={{0,2},{1,3},{2,0},{3,1},{16,18},{17,19},{18,16},{19,17},{4,6},{5,7... | collective-permute-start | bytes 552968 | tf_op jit(solution)/shard_map/ppermute | solution.py:557
  7.3 1.9 %collective-permute-start.3 = (bf16[1,8,8192]{2,1,0:T(8,128)(2,1)}, bf16[1,8,8192]{2,1,0:T(8,128)(2,1)S(1)}, u32[]{:S(2)}, u32[]{:S(2)}) collective-permute-start(bf16[1,8,8192]{2,1,0:T(8,128)(2,1)} %get-tuple-element.24), channel_id=1, source_target_pairs={{0,16},{1,17},{2,18},{3,19},{16,0},{17,1},{18,2},{19,3},{4,20},{5,... | collective-permute-start | bytes 393224 | tf_op jit(solution)/shard_map/ppermute | solution.py:557
  9.2 1.4 %collective-permute-start.4 = (bf16[1,8,8192]{2,1,0:T(8,128)(2,1)}, bf16[1,8,8192]{2,1,0:T(8,128)(2,1)S(1)}, u32[]{:S(2)}, u32[]{:S(2)}) collective-permute-start(bf16[1,8,8192]{2,1,0:T(8,128)(2,1)} %get-tuple-element.25), channel_id=1, source_target_pairs={{0,17},{1,16},{2,19},{3,18},{16,1},{17,0},{18,3},{19,2},{4,21},{5,... | collective-permute-start | bytes 393224 | tf_op jit(solution)/shard_map/ppermute | solution.py:557
  10.7 3.2 %collective-permute-start.5 = (bf16[1,8,8192]{2,1,0:T(8,128)(2,1)}, bf16[1,8,8192]{2,1,0:T(8,128)(2,1)S(1)}, u32[]{:S(2)}, u32[]{:S(2)}) collective-permute-start(bf16[1,8,8192]{2,1,0:T(8,128)(2,1)} %get-tuple-element.26), channel_id=1, source_target_pairs={{0,18},{1,19},{2,16},{3,17},{16,2},{17,3},{18,0},{19,1},{4,22},{5,... | collective-permute-start | bytes 393224 | tf_op jit(solution)/shard_map/ppermute | solution.py:557
  13.9 2.1 %collective-permute-start.6 = (bf16[1,8,8192]{2,1,0:T(8,128)(2,1)}, bf16[1,8,8192]{2,1,0:T(8,128)(2,1)S(1)}, u32[]{:S(2)}, u32[]{:S(2)}) collective-permute-start(bf16[1,8,8192]{2,1,0:T(8,128)(2,1)} %get-tuple-element.27), channel_id=1, source_target_pairs={{0,19},{1,18},{2,17},{3,16},{16,3},{17,2},{18,1},{19,0},{4,23},{5,... | collective-permute-start | bytes 393224 | tf_op jit(solution)/shard_map/ppermute | solution.py:557
  18.6 3.6 %grid_rows.3.refs_8_ = f32[32,64,256]{2,1,0:T(8,128)S(1)} custom-call(s32[1]{0:T(128)} %bitcast.3.place_ref, bf16[16,32]{1,0:T(8,128)(2,1)S(1)} %bitcast.12, bf16[1,8,11520]{2,1,0:T(8,128)(2,1)S(1)} %copy-done, bf16[1,8,11520]{2,1,0:T(8,128)(2,1)S(1)} %collective-permute-done.refs_1_.refs_5_.refs_9_.refs_13_, ...), custom_call_target="tpu_custom_call" | custom-call | flops 4294967296 | bytes 2097152 | tf_op jit(solution)/shard_map/grid_rows/pallas_call | solution.py:261
  22.7 3.9 %grid_rows.4 = (bf16[2,8,64,128]{3,2,1,0:T(8,128)(2,1)S(1)}, bf16[2,8,64,128]{3,2,1,0:T(8,128)(2,1)S(1)}) custom-call(s32[1]{0:T(128)} %bitcast.3.place_ref, bf16[16,32]{1,0:T(8,128)(2,1)S(1)} %bitcast.13, bf16[1,8,8192]{2,1,0:T(8,128)(2,1)S(1)} %collective-permute-done.3.refs_0_.refs_4_, bf16[1,8,8192]{2,1,0:T(8,128)(2,1)S(1)} %collective-permute-done.4.refs_1_.refs_5_, ...), custom_call_target="tpu_custom_call" | custom-call | flops 4294967296 | bytes 2097152 | tf_op jit(solution)/shard_map/grid_rows/pallas_call | solution.py:261
  26.7 1.5 %collective-permute-done.7.refs_1_ = bf16[2,8,64,128]{3,2,1,0:T(8,128)(2,1)S(1)} collective-permute-done((bf16[2,8,64,128]{3,2,1,0:T(8,128)(2,1)S(1)}, bf16[2,8,64,128]{3,2,1,0:T(8,128)(2,1)S(1)}, u32[]{:S(2)}, u32[]{:S(2)}) %collective-permute-start.7) | collective-permute-done | bytes 262176 | tf_op jit(solution)/shard_map/ppermute | solution.py:27
  28.3 3.7 %collective-permute-start.9 = (bf16[2,8,64,128]{3,2,1,0:T(8,128)(2,1)S(1)}, bf16[2,8,64,128]{3,2,1,0:T(8,128)(2,1)S(1)}, u32[]{:S(2)}, u32[]{:S(2)}) collective-permute-start(bf16[2,8,64,128]{3,2,1,0:T(8,128)(2,1)S(1)} %add_sums.4.refs_16_.refs_0_), channel_id=1, source_target_pairs={{0,6},{2,4},{4,2},{6,0},{1,7},{3,5},{5,3},{7,1},{8,14},{10,12},{12... | collective-permute-start | bytes 786440 | tf_op jit(solution)/shard_map/ppermute | solution.py:608
  32.0 6.8 %grid_rows.5 = (bf16[2,8,64,128]{3,2,1,0:T(8,128)(2,1)S(1)}, bf16[2,8,64,128]{3,2,1,0:T(8,128)(2,1)S(1)}) custom-call(s32[1]{0:T(128)} %bitcast.3.place_ref, bf16[16,32]{1,0:T(8,128)(2,1)S(1)} %bitcast.14, bf16[1,8,11520]{2,1,0:T(8,128)(2,1)S(1)} %copy-done, bf16[1,8,11520]{2,1,0:T(8,128)(2,1)S(1)} %collective-permute-done.refs_1_.refs_5_.refs_9_.refs_13_, ...), custom_call_target="tpu_custom_call" | custom-call | flops 8589934592 | bytes 2097152 | tf_op jit(solution)/shard_map/grid_rows/pallas_call | solution.py:261
  39.0 1.4 %collective-permute-done.8.refs_1_ = bf16[2,8,64,128]{3,2,1,0:T(8,128)(2,1)S(1)} collective-permute-done((bf16[2,8,64,128]{3,2,1,0:T(8,128)(2,1)S(1)}, bf16[2,8,64,128]{3,2,1,0:T(8,128)(2,1)S(1)}, u32[]{:S(2)}, u32[]{:S(2)}) %collective-permute-start.8) | collective-permute-done | bytes 262176 | tf_op jit(solution)/shard_map/ppermute | solution.py:27
  40.5 2.0 %collective-permute-start.10 = (bf16[2,8,64,128]{3,2,1,0:T(8,128)(2,1)S(1)}, bf16[2,8,64,128]{3,2,1,0:T(8,128)(2,1)S(1)}, u32[]{:S(2)}, u32[]{:S(2)}) collective-permute-start(bf16[2,8,64,128]{3,2,1,0:T(8,128)(2,1)S(1)} %add_sums.6.refs_0_), channel_id=1, source_target_pairs={{0,6},{2,4},{4,2},{6,0},{1,7},{3,5},{5,3},{7,1},{8,14},{10,12},{12... | collective-permute-start | bytes 786440 | tf_op jit(solution)/shard_map/ppermute | solution.py:608
  42.5 1.5 %collective-permute-start.16 = (bf16[2,8,64,128]{3,2,1,0:T(8,128)(2,1)S(1)}, bf16[2,8,64,128]{3,2,1,0:T(8,128)(2,1)S(1)}, u32[]{:S(2)}, u32[]{:S(2)}) collective-permute-start(bf16[2,8,64,128]{3,2,1,0:T(8,128)(2,1)S(1)} %add_sums.5.refs_2_.refs_0_), channel_id=1, source_target_pairs={{0,1},{1,0},{2,3},{3,2},{4,5},{5,4},{6,7},{7,6},{8,9},{9,8},{10,11... | collective-permute-start | bytes 786440 | tf_op jit(solution)/shard_map/ppermute | solution.py:594
  44.0 3.3 %collective-permute-start.14 = (bf16[2,8,64,128]{3,2,1,0:T(8,128)(2,1)S(1)}, bf16[2,8,64,128]{3,2,1,0:T(8,128)(2,1)S(1)}, u32[]{:S(2)}, u32[]{:S(2)}) collective-permute-start(bf16[2,8,64,128]{3,2,1,0:T(8,128)(2,1)S(1)} %add_sums.5.refs_2_.refs_0_), channel_id=1, source_target_pairs={{0,2},{1,3},{2,0},{3,1},{4,6},{5,7},{6,4},{7,5},{8,10},{9,11},{10,... | collective-permute-start | bytes 786440 | tf_op jit(solution)/shard_map/ppermute | solution.py:594
  47.2 7.3 %make_tables.1 = (bf16[2048,2176]{1,0:T(8,128)(2,1)S(1)}, bf16[8,128,256]{2,1,0:T(8,128)(2,1)S(1)}, f32[64,128]{1,0:T(8,128)S(1)}) custom-call(s32[1]{0:T(128)} %bitcast.10.facet_ref, s32[8,32]{1,0:T(8,128)S(1)} %copy-done.2, s32[8]{0:T(128)S(1)} %copy-done.3, bf16[2,8,64,128]{3,2,1,0:T(8,128)(2,1)S(1)} %add_sums.5.refs_2_.refs_0_), custom_call_target="tpu_custom_call" | custom-call | flops 35651584 | bytes 8912896 | tf_op jit(solution)/shard_map/make_tables/pallas_call | solution.py:395
  54.6 1.5 %collective-permute-start.12 = (bf16[2,8,64,128]{3,2,1,0:T(8,128)(2,1)S(1)}, bf16[2,8,64,128]{3,2,1,0:T(8,128)(2,1)S(1)}, u32[]{:S(2)}, u32[]{:S(2)}) collective-permute-start(bf16[2,8,64,128]{3,2,1,0:T(8,128)(2,1)S(1)} %add_sums.7.refs_2_.refs_6_.refs_5_.refs_4_), channel_id=1, source_target_pairs={{0,1},{1,0},{2,3},{3,2},{4,5},{5,4},{6,7},{7,6},{8,9},{9,8},{10,11... | collective-permute-start | bytes 786440 | tf_op jit(solution)/shard_map/ppermute | solution.py:594
  56.1 2.4 %collective-permute-start.13 = (bf16[2,8,64,128]{3,2,1,0:T(8,128)(2,1)S(1)}, bf16[2,8,64,128]{3,2,1,0:T(8,128)(2,1)S(1)}, u32[]{:S(2)}, u32[]{:S(2)}) collective-permute-start(bf16[2,8,64,128]{3,2,1,0:T(8,128)(2,1)S(1)} %add_sums.7.refs_2_.refs_6_.refs_5_.refs_4_), channel_id=1, source_target_pairs={{0,2},{1,3},{2,0},{3,1},{4,6},{5,7},{6,4},{7,5},{8,10},{9,11},{10,... | collective-permute-start | bytes 786440 | tf_op jit(solution)/shard_map/ppermute | solution.py:594
  58.5 5.6 %add_image.4.refs_6_ = f32[16,64,2048]{2,1,0:T(8,128)} custom-call(s32[1]{0:T(128)} %bitcast.flip_ref.z1_ref, s32[1]{0:T(128)} %bitcast.1.z0_ref, s32[1]{0:T(128)} %bitcast.2.x_ref, bf16[2,8,64,128]{3,2,1,0:T(8,128)(2,1)S(1)} %add_sums.5.refs_2_.refs_0_, bf16[2,8,64,128]{3,2,1,0:T(8,128)(2,1)S(1)} %collective-permute-done.16.refs_1_, ...), custom_call_target="tpu_custom_call" | custom-call | flops 3221225472 | bytes 11534336 | tf_op jit(solution)/shard_map/add_image/pallas_call | solution.py:494
  64.1 4.0 %add_image.5.refs_6_ = f32[16,64,2048]{2,1,0:T(8,128)} custom-call(s32[1]{0:T(128)} %bitcast.flip_ref.z1_ref, s32[1]{0:T(128)} %bitcast.1.z0_ref, s32[1]{0:T(128)} %bitcast.2.x_ref, bf16[2,8,64,128]{3,2,1,0:T(8,128)(2,1)S(1)} %collective-permute-done.14.refs_0_, ...), custom_call_target="tpu_custom_call", output_to_operand_aliasing={{}: (9, {})} | custom-call | flops 2147483648 | bytes 10485760 | tf_op jit(solution)/shard_map/add_image/pallas_call | solution.py:494
  68.1 4.0 %add_image.6.refs_5_ = f32[16,64,2048]{2,1,0:T(8,128)} custom-call(s32[1]{0:T(128)} %bitcast.flip_ref.z1_ref, s32[1]{0:T(128)} %bitcast.1.z0_ref, s32[1]{0:T(128)} %bitcast.2.x_ref, bf16[2,8,64,128]{3,2,1,0:T(8,128)(2,1)S(1)} %collective-permute-done.12.refs_0_, ...), custom_call_target="tpu_custom_call", output_to_operand_aliasing={{}: (9, {})} | custom-call | flops 2147483648 | bytes 10485760 | tf_op jit(solution)/shard_map/add_image/pallas_call | solution.py:494
  72.1 2.0 %collective-permute-done.11.refs_0_ = bf16[2,8,64,128]{3,2,1,0:T(8,128)(2,1)S(1)} collective-permute-done((bf16[2,8,64,128]{3,2,1,0:T(8,128)(2,1)S(1)}, bf16[2,8,64,128]{3,2,1,0:T(8,128)(2,1)S(1)}, u32[]{:S(2)}, u32[]{:S(2)}) %collective-permute-start.11) | collective-permute-done | bytes 262176 | tf_op jit(solution)/shard_map/ppermute | solution.py:594
  74.2 2.4 %add_image.7 = f32[16,64,2048]{2,1,0:T(8,128)} custom-call(s32[1]{0:T(128)} %bitcast.flip_ref.z1_ref, s32[1]{0:T(128)} %bitcast.1.z0_ref, s32[1]{0:T(128)} %bitcast.2.x_ref, bf16[2,8,64,128]{3,2,1,0:T(8,128)(2,1)S(1)} %collective-permute-done.11.refs_0_, ...), custom_call_target="tpu_custom_call", output_to_operand_aliasing={{}: (8, {})} | custom-call | flops 1073741824 | bytes 9437184 | tf_op jit(solution)/shard_map/add_image/pallas_call | solution.py:494
  (31 shorter events, 3.5 us)
Async XLA Ops:
  2.7 8.0 %collective-permute-start = (bf16[1,8,11520]{2,1,0:T(8,128)(2,1)}, bf16[1,8,11520]{2,1,0:T(8,128)(2,1)S(1)}, u32[]{:S(2)}, u32[]{:S(2)}) collective-permute-start(bf16[1,8,11520]{2,1,0:T(8,128)(2,1)} %get-tuple-element.21), channel_id=1, source_target_pairs={{0,1},{1,0},{2,3},{3,2},{16,17},{17,16},{18,19},{19,18},{4,5},{5,4... | collective-permute-start | bytes 552968 | tf_op jit(solution)/shard_map/ppermute | solution.py:557
  5.7 8.2 %collective-permute-start.1 = (bf16[1,8,11520]{2,1,0:T(8,128)(2,1)}, bf16[1,8,11520]{2,1,0:T(8,128)(2,1)S(1)}, u32[]{:S(2)}, u32[]{:S(2)}) collective-permute-start(bf16[1,8,11520]{2,1,0:T(8,128)(2,1)} %get-tuple-element.22), channel_id=1, source_target_pairs={{0,2},{1,3},{2,0},{3,1},{16,18},{17,19},{18,16},{19,17},{4,6},{5,7... | collective-permute-start | bytes 552968 | tf_op jit(solution)/shard_map/ppermute | solution.py:557
  7.3 9.7 %collective-permute-start.2 = (bf16[1,8,11520]{2,1,0:T(8,128)(2,1)}, bf16[1,8,11520]{2,1,0:T(8,128)(2,1)S(1)}, u32[]{:S(2)}, u32[]{:S(2)}) collective-permute-start(bf16[1,8,11520]{2,1,0:T(8,128)(2,1)} %get-tuple-element.23), channel_id=1, source_target_pairs={{0,3},{1,2},{2,1},{3,0},{16,19},{17,18},{18,17},{19,16},{4,7},{5,6... | collective-permute-start | bytes 552968 | tf_op jit(solution)/shard_map/ppermute | solution.py:557
  7.3 14.9 %collective-permute-start.3 = (bf16[1,8,8192]{2,1,0:T(8,128)(2,1)}, bf16[1,8,8192]{2,1,0:T(8,128)(2,1)S(1)}, u32[]{:S(2)}, u32[]{:S(2)}) collective-permute-start(bf16[1,8,8192]{2,1,0:T(8,128)(2,1)} %get-tuple-element.24), channel_id=1, source_target_pairs={{0,16},{1,17},{2,18},{3,19},{16,0},{17,1},{18,2},{19,3},{4,20},{5,... | collective-permute-start | bytes 393224 | tf_op jit(solution)/shard_map/ppermute | solution.py:557
  9.2 13.0 %collective-permute-start.4 = (bf16[1,8,8192]{2,1,0:T(8,128)(2,1)}, bf16[1,8,8192]{2,1,0:T(8,128)(2,1)S(1)}, u32[]{:S(2)}, u32[]{:S(2)}) collective-permute-start(bf16[1,8,8192]{2,1,0:T(8,128)(2,1)} %get-tuple-element.25), channel_id=1, source_target_pairs={{0,17},{1,16},{2,19},{3,18},{16,1},{17,0},{18,3},{19,2},{4,21},{5,... | collective-permute-start | bytes 393224 | tf_op jit(solution)/shard_map/ppermute | solution.py:557
  10.7 11.6 %collective-permute-start.5 = (bf16[1,8,8192]{2,1,0:T(8,128)(2,1)}, bf16[1,8,8192]{2,1,0:T(8,128)(2,1)S(1)}, u32[]{:S(2)}, u32[]{:S(2)}) collective-permute-start(bf16[1,8,8192]{2,1,0:T(8,128)(2,1)} %get-tuple-element.26), channel_id=1, source_target_pairs={{0,18},{1,19},{2,16},{3,17},{16,2},{17,3},{18,0},{19,1},{4,22},{5,... | collective-permute-start | bytes 393224 | tf_op jit(solution)/shard_map/ppermute | solution.py:557
  13.9 8.8 %collective-permute-start.6 = (bf16[1,8,8192]{2,1,0:T(8,128)(2,1)}, bf16[1,8,8192]{2,1,0:T(8,128)(2,1)S(1)}, u32[]{:S(2)}, u32[]{:S(2)}) collective-permute-start(bf16[1,8,8192]{2,1,0:T(8,128)(2,1)} %get-tuple-element.27), channel_id=1, source_target_pairs={{0,19},{1,18},{2,17},{3,16},{16,3},{17,2},{18,1},{19,0},{4,23},{5,... | collective-permute-start | bytes 393224 | tf_op jit(solution)/shard_map/ppermute | solution.py:557
  17.0 0.9 %copy-start = (bf16[1,8,11520]{2,1,0:T(8,128)(2,1)S(1)}, bf16[1,8,11520]{2,1,0:T(8,128)(2,1)}, u32[]{:S(2)}) copy-start(bf16[1,8,11520]{2,1,0:T(8,128)(2,1)} %get-tuple-element.20.refs_0_.refs_4_.refs_8_.refs_12_) | copy-start | bytes 552964
  17.9 0.7 copy-start.1
  26.6 1.6 %collective-permute-start.7 = (bf16[2,8,64,128]{3,2,1,0:T(8,128)(2,1)S(1)}, bf16[2,8,64,128]{3,2,1,0:T(8,128)(2,1)S(1)}, u32[]{:S(2)}, u32[]{:S(2)}) collective-permute-start(bf16[2,8,64,128]{3,2,1,0:T(8,128)(2,1)S(1)} %get-tuple-element.29), channel_id=1, source_target_pairs={{0,8},{8,0},{1,9},{9,1},{2,10},{10,2},{3,11},{11,3},{4,12},{12,4},... | collective-permute-start | bytes 786440 | tf_op jit(solution)/shard_map/ppermute | solution.py:27
  28.3 18.9 %copy-start.2 = (s32[8,32]{1,0:T(8,128)S(1)}, s32[8,32]{1,0:T(8,128)}, u32[]{:S(2)}) copy-start(s32[8,32]{1,0:T(8,128)} %listed_ref.1) | copy-start | bytes 3076
  28.3 18.9 %copy-start.3 = (s32[8]{0:T(128)S(1)}, s32[8]{0:T(128)}, u32[]{:S(2)}) copy-start(s32[8]{0:T(128)} %count_ref.1) | copy-start | bytes 100
  28.3 10.6 %collective-permute-start.9 = (bf16[2,8,64,128]{3,2,1,0:T(8,128)(2,1)S(1)}, bf16[2,8,64,128]{3,2,1,0:T(8,128)(2,1)S(1)}, u32[]{:S(2)}, u32[]{:S(2)}) collective-permute-start(bf16[2,8,64,128]{3,2,1,0:T(8,128)(2,1)S(1)} %add_sums.4.refs_16_.refs_0_), channel_id=1, source_target_pairs={{0,6},{2,4},{4,2},{6,0},{1,7},{3,5},{5,3},{7,1},{8,14},{10,12},{12... | collective-permute-start | bytes 786440 | tf_op jit(solution)/shard_map/ppermute | solution.py:608
  38.8 1.6 %collective-permute-start.8 = (bf16[2,8,64,128]{3,2,1,0:T(8,128)(2,1)S(1)}, bf16[2,8,64,128]{3,2,1,0:T(8,128)(2,1)S(1)}, u32[]{:S(2)}, u32[]{:S(2)}) collective-permute-start(bf16[2,8,64,128]{3,2,1,0:T(8,128)(2,1)S(1)} %get-tuple-element.31), channel_id=1, source_target_pairs={{0,8},{8,0},{1,9},{9,1},{2,10},{10,2},{3,11},{11,3},{4,12},{12,4},... | collective-permute-start | bytes 786440 | tf_op jit(solution)/shard_map/ppermute | solution.py:27
  40.5 14.1 %collective-permute-start.10 = (bf16[2,8,64,128]{3,2,1,0:T(8,128)(2,1)S(1)}, bf16[2,8,64,128]{3,2,1,0:T(8,128)(2,1)S(1)}, u32[]{:S(2)}, u32[]{:S(2)}) collective-permute-start(bf16[2,8,64,128]{3,2,1,0:T(8,128)(2,1)S(1)} %add_sums.6.refs_0_), channel_id=1, source_target_pairs={{0,6},{2,4},{4,2},{6,0},{1,7},{3,5},{5,3},{7,1},{8,14},{10,12},{12... | collective-permute-start | bytes 786440 | tf_op jit(solution)/shard_map/ppermute | solution.py:608
  42.5 16.0 %collective-permute-start.16 = (bf16[2,8,64,128]{3,2,1,0:T(8,128)(2,1)S(1)}, bf16[2,8,64,128]{3,2,1,0:T(8,128)(2,1)S(1)}, u32[]{:S(2)}, u32[]{:S(2)}) collective-permute-start(bf16[2,8,64,128]{3,2,1,0:T(8,128)(2,1)S(1)} %add_sums.5.refs_2_.refs_0_), channel_id=1, source_target_pairs={{0,1},{1,0},{2,3},{3,2},{4,5},{5,4},{6,7},{7,6},{8,9},{9,8},{10,11... | collective-permute-start | bytes 786440 | tf_op jit(solution)/shard_map/ppermute | solution.py:594
  44.0 20.1 %collective-permute-start.14 = (bf16[2,8,64,128]{3,2,1,0:T(8,128)(2,1)S(1)}, bf16[2,8,64,128]{3,2,1,0:T(8,128)(2,1)S(1)}, u32[]{:S(2)}, u32[]{:S(2)}) collective-permute-start(bf16[2,8,64,128]{3,2,1,0:T(8,128)(2,1)S(1)} %add_sums.5.refs_2_.refs_0_), channel_id=1, source_target_pairs={{0,2},{1,3},{2,0},{3,1},{4,6},{5,7},{6,4},{7,5},{8,10},{9,11},{10,... | collective-permute-start | bytes 786440 | tf_op jit(solution)/shard_map/ppermute | solution.py:594
  47.2 16.9 %collective-permute-start.15 = (bf16[2,8,64,128]{3,2,1,0:T(8,128)(2,1)S(1)}, bf16[2,8,64,128]{3,2,1,0:T(8,128)(2,1)S(1)}, u32[]{:S(2)}, u32[]{:S(2)}) collective-permute-start(bf16[2,8,64,128]{3,2,1,0:T(8,128)(2,1)S(1)} %add_sums.5.refs_2_.refs_0_), channel_id=1, source_target_pairs={{0,3},{1,2},{2,1},{3,0},{4,7},{5,6},{6,5},{7,4},{8,11},{9,10},{10,... | collective-permute-start | bytes 786440 | tf_op jit(solution)/shard_map/ppermute | solution.py:594
  54.6 13.5 %collective-permute-start.12 = (bf16[2,8,64,128]{3,2,1,0:T(8,128)(2,1)S(1)}, bf16[2,8,64,128]{3,2,1,0:T(8,128)(2,1)S(1)}, u32[]{:S(2)}, u32[]{:S(2)}) collective-permute-start(bf16[2,8,64,128]{3,2,1,0:T(8,128)(2,1)S(1)} %add_sums.7.refs_2_.refs_6_.refs_5_.refs_4_), channel_id=1, source_target_pairs={{0,1},{1,0},{2,3},{3,2},{4,5},{5,4},{6,7},{7,6},{8,9},{9,8},{10,11... | collective-permute-start | bytes 786440 | tf_op jit(solution)/shard_map/ppermute | solution.py:594
  56.1 12.0 %collective-permute-start.13 = (bf16[2,8,64,128]{3,2,1,0:T(8,128)(2,1)S(1)}, bf16[2,8,64,128]{3,2,1,0:T(8,128)(2,1)S(1)}, u32[]{:S(2)}, u32[]{:S(2)}) collective-permute-start(bf16[2,8,64,128]{3,2,1,0:T(8,128)(2,1)S(1)} %add_sums.7.refs_2_.refs_6_.refs_5_.refs_4_), channel_id=1, source_target_pairs={{0,2},{1,3},{2,0},{3,1},{4,6},{5,7},{6,4},{7,5},{8,10},{9,11},{10,... | collective-permute-start | bytes 786440 | tf_op jit(solution)/shard_map/ppermute | solution.py:594
  58.5 15.7 %collective-permute-start.11 = (bf16[2,8,64,128]{3,2,1,0:T(8,128)(2,1)S(1)}, bf16[2,8,64,128]{3,2,1,0:T(8,128)(2,1)S(1)}, u32[]{:S(2)}, u32[]{:S(2)}) collective-permute-start(bf16[2,8,64,128]{3,2,1,0:T(8,128)(2,1)S(1)} %add_sums.7.refs_2_.refs_6_.refs_5_.refs_4_), channel_id=1, source_target_pairs={{0,3},{1,2},{2,1},{3,0},{4,7},{5,6},{6,5},{7,4},{8,11},{9,10},{10,... | collective-permute-start | bytes 786440 | tf_op jit(solution)/shard_map/ppermute | solution.py:594

commit v7 on v6

--- a/solution.py
+++ b/solution.py
@@ -629,9 +629,8 @@
     parts = len(first_pieces)
     image = None
     calls = (
-        [*range(east), parts],
-        range(east, parts),
-        range(parts + 1, 2 * parts - 1),
+        [*range(parts - 1), parts],
+        [parts - 1, *range(parts + 1, 2 * parts - 1)],
         [2 * parts - 1],
     )
     for chosen in calls:

time: 77 us -> 77 us (level)
  waiting for transfers between devices: 6.48 us -> 7.38 us
  Pallas kernels: 40.6 us -> 39.7 us
    ppermute x6, waiting for transfers between devices: 2.05 us -> 2.95 us  [shifted(): return lax.ppermute(piece, ('z0', 'x'), route)]
    pallas_call x4 -> x3, Pallas kernels: 16 us -> 15.1 us  [add_image(): pl.pallas_call(functools.partial(image_kernel, places=places, scale=scale...]
  transfers between devices with their start and end apart: 17 -> 17, of which waited for: 5 -> 7; matrix products, arithmetic and copies ran while one was open for 0% -> 0% of each run, Pallas kernels for 41% -> 40%
where the time goes in v7:
time: 77 us; the launch traced here: 76.8 us
  Pallas kernels  39.7 us (52%)
  starting transfers between devices  27.7 us (36%)
  waiting for transfers between devices  7.38 us (10%)
  local copies, waits for them, and re-layouts  1.62 us (2%)
    pallas_call x3, Pallas kernels, add_image(): pl.pallas_call(functools.partial(image_kernel, places=places, scale=scale...  15.1 us
    pallas_call x3, Pallas kernels, grid_rows(): pl.pallas_call(functools.partial(grid_kernel, row_len=row_len, half=half,...  14.3 us
    ppermute x7, starting transfers between devices, shards(): rows.append(lax.ppermute(sent[k], inner, route))  13.3 us
    ppermute x6, starting transfers between devices, shifted(): return lax.ppermute(piece, ('z0', 'x'), route)  8.64 us
    pallas_call x1, Pallas kernels, make_tables(): pl.pallas_call(functools.partial(tables_kernel, period=period), out_shape...  7.3 us
    ppermute x2, starting transfers between devices, mirrored(): return lax.ppermute(block, ('z1', 'z0'), [(i, 3 - i) for i in range(4)])  5.67 us
    ppermute x2, waiting for transfers between devices, swap(): return lax.ppermute(block, axis, [(0, 1), (1, 0)])  2.96 us
    ppermute x6, waiting for transfers between devices, shifted(): return lax.ppermute(piece, ('z0', 'x'), route)  2.95 us
  transfers between devices with their start and end apart: 17, of which 7 were waited for; matrix products, arithmetic and copies ran while one was open for 0% of the time, Pallas kernels for 40%

profile of v7, /device:TPU:0, one launch (start us, length us, event | category | flops | bytes accessed | tf_op | source)
XLA Modules:
  0.0 76.8 jit_solution(10533212493990808546)
XLA Ops:
  0.0 2.7 %pack_rows.1 = (bf16[1,8,11520]{2,1,0:T(8,128)(2,1)}, bf16[1,8,11520]{2,1,0:T(8,128)(2,1)}, bf16[1,8,11520]{2,1,0:T(8,128)(2,1)}, bf16[1,8,11520]{2,1,0:T(8,128)...) custom-call(s32[1]{0:T(128)} %bitcast.6.group_ref, ...), custom_call_target="tpu_custom_call" | custom-call | flops 1048576 | bytes 3145728 | tf_op jit(solution)/shard_map/pack_rows/pallas_call | solution.py:102
  2.7 3.0 %collective-permute-start = (bf16[1,8,11520]{2,1,0:T(8,128)(2,1)}, bf16[1,8,11520]{2,1,0:T(8,128)(2,1)S(1)}, u32[]{:S(2)}, u32[]{:S(2)}) collective-permute-start(bf16[1,8,11520]{2,1,0:T(8,128)(2,1)} %get-tuple-element.21), channel_id=1, source_target_pairs={{0,1},{1,0},{2,3},{3,2},{16,17},{17,16},{18,19},{19,18},{4,5},{5,4... | collective-permute-start | bytes 552968 | tf_op jit(solution)/shard_map/ppermute | solution.py:557
  5.7 1.6 %collective-permute-start.1 = (bf16[1,8,11520]{2,1,0:T(8,128)(2,1)}, bf16[1,8,11520]{2,1,0:T(8,128)(2,1)S(1)}, u32[]{:S(2)}, u32[]{:S(2)}) collective-permute-start(bf16[1,8,11520]{2,1,0:T(8,128)(2,1)} %get-tuple-element.22), channel_id=1, source_target_pairs={{0,2},{1,3},{2,0},{3,1},{16,18},{17,19},{18,16},{19,17},{4,6},{5,7... | collective-permute-start | bytes 552968 | tf_op jit(solution)/shard_map/ppermute | solution.py:557
  7.3 1.9 %collective-permute-start.3 = (bf16[1,8,8192]{2,1,0:T(8,128)(2,1)}, bf16[1,8,8192]{2,1,0:T(8,128)(2,1)S(1)}, u32[]{:S(2)}, u32[]{:S(2)}) collective-permute-start(bf16[1,8,8192]{2,1,0:T(8,128)(2,1)} %get-tuple-element.24), channel_id=1, source_target_pairs={{0,16},{1,17},{2,18},{3,19},{16,0},{17,1},{18,2},{19,3},{4,20},{5,... | collective-permute-start | bytes 393224 | tf_op jit(solution)/shard_map/ppermute | solution.py:557
  9.2 1.4 %collective-permute-start.4 = (bf16[1,8,8192]{2,1,0:T(8,128)(2,1)}, bf16[1,8,8192]{2,1,0:T(8,128)(2,1)S(1)}, u32[]{:S(2)}, u32[]{:S(2)}) collective-permute-start(bf16[1,8,8192]{2,1,0:T(8,128)(2,1)} %get-tuple-element.25), channel_id=1, source_target_pairs={{0,17},{1,16},{2,19},{3,18},{16,1},{17,0},{18,3},{19,2},{4,21},{5,... | collective-permute-start | bytes 393224 | tf_op jit(solution)/shard_map/ppermute | solution.py:557
  10.7 3.2 %collective-permute-start.5 = (bf16[1,8,8192]{2,1,0:T(8,128)(2,1)}, bf16[1,8,8192]{2,1,0:T(8,128)(2,1)S(1)}, u32[]{:S(2)}, u32[]{:S(2)}) collective-permute-start(bf16[1,8,8192]{2,1,0:T(8,128)(2,1)} %get-tuple-element.26), channel_id=1, source_target_pairs={{0,18},{1,19},{2,16},{3,17},{16,2},{17,3},{18,0},{19,1},{4,22},{5,... | collective-permute-start | bytes 393224 | tf_op jit(solution)/shard_map/ppermute | solution.py:557
  13.9 2.1 %collective-permute-start.6 = (bf16[1,8,8192]{2,1,0:T(8,128)(2,1)}, bf16[1,8,8192]{2,1,0:T(8,128)(2,1)S(1)}, u32[]{:S(2)}, u32[]{:S(2)}) collective-permute-start(bf16[1,8,8192]{2,1,0:T(8,128)(2,1)} %get-tuple-element.27), channel_id=1, source_target_pairs={{0,19},{1,18},{2,17},{3,16},{16,3},{17,2},{18,1},{19,0},{4,23},{5,... | collective-permute-start | bytes 393224 | tf_op jit(solution)/shard_map/ppermute | solution.py:557
  16.0 1.0 %collective-permute-done.2.refs_3_.refs_7_.refs_11_.refs_15_ = bf16[1,8,11520]{2,1,0:T(8,128)(2,1)S(1)} collective-permute-done((bf16[1,8,11520]{2,1,0:T(8,128)(2,1)}, bf16[1,8,11520]{2,1,0:T(8,128)(2,1)S(1)}, u32[]{:S(2)}, u32[]{:S(2)}) %collective-permute-start.2) | collective-permute-done | bytes 184352 | tf_op jit(solution)/shard_map/ppermute | solution.py:557
  18.6 3.6 %grid_rows.3.refs_8_ = f32[32,64,256]{2,1,0:T(8,128)S(1)} custom-call(s32[1]{0:T(128)} %bitcast.3.place_ref, bf16[16,32]{1,0:T(8,128)(2,1)S(1)} %bitcast.12, bf16[1,8,11520]{2,1,0:T(8,128)(2,1)S(1)} %copy-done, bf16[1,8,11520]{2,1,0:T(8,128)(2,1)S(1)} %collective-permute-done.refs_1_.refs_5_.refs_9_.refs_13_, ...), custom_call_target="tpu_custom_call" | custom-call | flops 4294967296 | bytes 2097152 | tf_op jit(solution)/shard_map/grid_rows/pallas_call | solution.py:261
  22.7 3.9 %grid_rows.4 = (bf16[2,8,64,128]{3,2,1,0:T(8,128)(2,1)S(1)}, bf16[2,8,64,128]{3,2,1,0:T(8,128)(2,1)S(1)}) custom-call(s32[1]{0:T(128)} %bitcast.3.place_ref, bf16[16,32]{1,0:T(8,128)(2,1)S(1)} %bitcast.13, bf16[1,8,8192]{2,1,0:T(8,128)(2,1)S(1)} %collective-permute-done.3.refs_0_.refs_4_, bf16[1,8,8192]{2,1,0:T(8,128)(2,1)S(1)} %collective-permute-done.4.refs_1_.refs_5_, ...), custom_call_target="tpu_custom_call" | custom-call | flops 4294967296 | bytes 2097152 | tf_op jit(solution)/shard_map/grid_rows/pallas_call | solution.py:261
  26.7 1.5 %collective-permute-done.7.refs_1_ = bf16[2,8,64,128]{3,2,1,0:T(8,128)(2,1)S(1)} collective-permute-done((bf16[2,8,64,128]{3,2,1,0:T(8,128)(2,1)S(1)}, bf16[2,8,64,128]{3,2,1,0:T(8,128)(2,1)S(1)}, u32[]{:S(2)}, u32[]{:S(2)}) %collective-permute-start.7) | collective-permute-done | bytes 262176 | tf_op jit(solution)/shard_map/ppermute | solution.py:27
  28.3 3.7 %collective-permute-start.9 = (bf16[2,8,64,128]{3,2,1,0:T(8,128)(2,1)S(1)}, bf16[2,8,64,128]{3,2,1,0:T(8,128)(2,1)S(1)}, u32[]{:S(2)}, u32[]{:S(2)}) collective-permute-start(bf16[2,8,64,128]{3,2,1,0:T(8,128)(2,1)S(1)} %add_sums.4.refs_16_.refs_0_), channel_id=1, source_target_pairs={{0,6},{2,4},{4,2},{6,0},{1,7},{3,5},{5,3},{7,1},{8,14},{10,12},{12... | collective-permute-start | bytes 786440 | tf_op jit(solution)/shard_map/ppermute | solution.py:608
  32.0 6.8 %grid_rows.5 = (bf16[2,8,64,128]{3,2,1,0:T(8,128)(2,1)S(1)}, bf16[2,8,64,128]{3,2,1,0:T(8,128)(2,1)S(1)}) custom-call(s32[1]{0:T(128)} %bitcast.3.place_ref, bf16[16,32]{1,0:T(8,128)(2,1)S(1)} %bitcast.14, bf16[1,8,11520]{2,1,0:T(8,128)(2,1)S(1)} %copy-done, bf16[1,8,11520]{2,1,0:T(8,128)(2,1)S(1)} %collective-permute-done.refs_1_.refs_5_.refs_9_.refs_13_, ...), custom_call_target="tpu_custom_call" | custom-call | flops 8589934592 | bytes 2097152 | tf_op jit(solution)/shard_map/grid_rows/pallas_call | solution.py:261
  39.0 1.4 %collective-permute-done.8.refs_1_ = bf16[2,8,64,128]{3,2,1,0:T(8,128)(2,1)S(1)} collective-permute-done((bf16[2,8,64,128]{3,2,1,0:T(8,128)(2,1)S(1)}, bf16[2,8,64,128]{3,2,1,0:T(8,128)(2,1)S(1)}, u32[]{:S(2)}, u32[]{:S(2)}) %collective-permute-start.8) | collective-permute-done | bytes 262176 | tf_op jit(solution)/shard_map/ppermute | solution.py:27
  40.5 2.0 %collective-permute-start.10 = (bf16[2,8,64,128]{3,2,1,0:T(8,128)(2,1)S(1)}, bf16[2,8,64,128]{3,2,1,0:T(8,128)(2,1)S(1)}, u32[]{:S(2)}, u32[]{:S(2)}) collective-permute-start(bf16[2,8,64,128]{3,2,1,0:T(8,128)(2,1)S(1)} %add_sums.6.refs_0_), channel_id=1, source_target_pairs={{0,6},{2,4},{4,2},{6,0},{1,7},{3,5},{5,3},{7,1},{8,14},{10,12},{12... | collective-permute-start | bytes 786440 | tf_op jit(solution)/shard_map/ppermute | solution.py:608
  42.5 1.5 %collective-permute-start.15 = (bf16[2,8,64,128]{3,2,1,0:T(8,128)(2,1)S(1)}, bf16[2,8,64,128]{3,2,1,0:T(8,128)(2,1)S(1)}, u32[]{:S(2)}, u32[]{:S(2)}) collective-permute-start(bf16[2,8,64,128]{3,2,1,0:T(8,128)(2,1)S(1)} %add_sums.5.refs_2_.refs_0_), channel_id=1, source_target_pairs={{0,1},{1,0},{2,3},{3,2},{4,5},{5,4},{6,7},{7,6},{8,9},{9,8},{10,11... | collective-permute-start | bytes 786440 | tf_op jit(solution)/shard_map/ppermute | solution.py:594
  44.0 3.3 %collective-permute-start.16 = (bf16[2,8,64,128]{3,2,1,0:T(8,128)(2,1)S(1)}, bf16[2,8,64,128]{3,2,1,0:T(8,128)(2,1)S(1)}, u32[]{:S(2)}, u32[]{:S(2)}) collective-permute-start(bf16[2,8,64,128]{3,2,1,0:T(8,128)(2,1)S(1)} %add_sums.5.refs_2_.refs_0_), channel_id=1, source_target_pairs={{0,2},{1,3},{2,0},{3,1},{4,6},{5,7},{6,4},{7,5},{8,10},{9,11},{10,... | collective-permute-start | bytes 786440 | tf_op jit(solution)/shard_map/ppermute | solution.py:594
  47.2 7.3 %make_tables.1 = (bf16[2048,2176]{1,0:T(8,128)(2,1)S(1)}, bf16[8,128,256]{2,1,0:T(8,128)(2,1)S(1)}, f32[64,128]{1,0:T(8,128)S(1)}) custom-call(s32[1]{0:T(128)} %bitcast.10.facet_ref, s32[8,32]{1,0:T(8,128)S(1)} %copy-done.2, s32[8]{0:T(128)S(1)} %copy-done.3, bf16[2,8,64,128]{3,2,1,0:T(8,128)(2,1)S(1)} %add_sums.5.refs_2_.refs_0_), custom_call_target="tpu_custom_call" | custom-call | flops 35651584 | bytes 8912896 | tf_op jit(solution)/shard_map/make_tables/pallas_call | solution.py:395
  54.6 1.5 %collective-permute-start.13 = (bf16[2,8,64,128]{3,2,1,0:T(8,128)(2,1)S(1)}, bf16[2,8,64,128]{3,2,1,0:T(8,128)(2,1)S(1)}, u32[]{:S(2)}, u32[]{:S(2)}) collective-permute-start(bf16[2,8,64,128]{3,2,1,0:T(8,128)(2,1)S(1)} %add_sums.7.refs_3_.refs_7_.refs_6_.refs_4_), channel_id=1, source_target_pairs={{0,1},{1,0},{2,3},{3,2},{4,5},{5,4},{6,7},{7,6},{8,9},{9,8},{10,11... | collective-permute-start | bytes 786440 | tf_op jit(solution)/shard_map/ppermute | solution.py:594
  56.1 2.4 %collective-permute-start.14 = (bf16[2,8,64,128]{3,2,1,0:T(8,128)(2,1)S(1)}, bf16[2,8,64,128]{3,2,1,0:T(8,128)(2,1)S(1)}, u32[]{:S(2)}, u32[]{:S(2)}) collective-permute-start(bf16[2,8,64,128]{3,2,1,0:T(8,128)(2,1)S(1)} %add_sums.7.refs_3_.refs_7_.refs_6_.refs_4_), channel_id=1, source_target_pairs={{0,2},{1,3},{2,0},{3,1},{4,6},{5,7},{6,4},{7,5},{8,10},{9,11},{10,... | collective-permute-start | bytes 786440 | tf_op jit(solution)/shard_map/ppermute | solution.py:594
  58.5 7.2 %add_image.3.refs_7_ = f32[16,64,2048]{2,1,0:T(8,128)} custom-call(s32[1]{0:T(128)} %bitcast.flip_ref.z1_ref, s32[1]{0:T(128)} %bitcast.1.z0_ref, s32[1]{0:T(128)} %bitcast.2.x_ref, bf16[2,8,64,128]{3,2,1,0:T(8,128)(2,1)S(1)} %add_sums.5.refs_2_.refs_0_, bf16[2,8,64,128]{3,2,1,0:T(8,128)(2,1)S(1)} %collective-permute-done.15.refs_1_, ...), custom_call_target="tpu_custom_call" | custom-call | flops 4294967296 | bytes 12582912 | tf_op jit(solution)/shard_map/add_image/pallas_call | solution.py:494
  65.7 1.3 %collective-permute-done.13.refs_1_ = bf16[2,8,64,128]{3,2,1,0:T(8,128)(2,1)S(1)} collective-permute-done((bf16[2,8,64,128]{3,2,1,0:T(8,128)(2,1)S(1)}, bf16[2,8,64,128]{3,2,1,0:T(8,128)(2,1)S(1)}, u32[]{:S(2)}, u32[]{:S(2)}) %collective-permute-start.13) | collective-permute-done | bytes 262176 | tf_op jit(solution)/shard_map/ppermute | solution.py:594
  67.8 5.5 %add_image.4.refs_5_ = f32[16,64,2048]{2,1,0:T(8,128)} custom-call(s32[1]{0:T(128)} %bitcast.flip_ref.z1_ref, s32[1]{0:T(128)} %bitcast.1.z0_ref, s32[1]{0:T(128)} %bitcast.2.x_ref, bf16[2,8,64,128]{3,2,1,0:T(8,128)(2,1)S(1)} %collective-permute-done.12.refs_0_, ...), custom_call_target="tpu_custom_call", output_to_operand_aliasing={{}: (10, {})} | custom-call | flops 3221225472 | bytes 11534336 | tf_op jit(solution)/shard_map/add_image/pallas_call | solution.py:494
  74.2 2.4 %add_image.5 = f32[16,64,2048]{2,1,0:T(8,128)} custom-call(s32[1]{0:T(128)} %bitcast.flip_ref.z1_ref, s32[1]{0:T(128)} %bitcast.1.z0_ref, s32[1]{0:T(128)} %bitcast.2.x_ref, bf16[2,8,64,128]{3,2,1,0:T(8,128)(2,1)S(1)} %collective-permute-done.11.refs_0_, ...), custom_call_target="tpu_custom_call", output_to_operand_aliasing={{}: (8, {})} | custom-call | flops 1073741824 | bytes 9437184 | tf_op jit(solution)/shard_map/add_image/pallas_call | solution.py:494
  (30 shorter events, 4.2 us)
Async XLA Ops:
  2.7 8.0 %collective-permute-start = (bf16[1,8,11520]{2,1,0:T(8,128)(2,1)}, bf16[1,8,11520]{2,1,0:T(8,128)(2,1)S(1)}, u32[]{:S(2)}, u32[]{:S(2)}) collective-permute-start(bf16[1,8,11520]{2,1,0:T(8,128)(2,1)} %get-tuple-element.21), channel_id=1, source_target_pairs={{0,1},{1,0},{2,3},{3,2},{16,17},{17,16},{18,19},{19,18},{4,5},{5,4... | collective-permute-start | bytes 552968 | tf_op jit(solution)/shard_map/ppermute | solution.py:557
  5.7 8.2 %collective-permute-start.1 = (bf16[1,8,11520]{2,1,0:T(8,128)(2,1)}, bf16[1,8,11520]{2,1,0:T(8,128)(2,1)S(1)}, u32[]{:S(2)}, u32[]{:S(2)}) collective-permute-start(bf16[1,8,11520]{2,1,0:T(8,128)(2,1)} %get-tuple-element.22), channel_id=1, source_target_pairs={{0,2},{1,3},{2,0},{3,1},{16,18},{17,19},{18,16},{19,17},{4,6},{5,7... | collective-permute-start | bytes 552968 | tf_op jit(solution)/shard_map/ppermute | solution.py:557
  7.3 9.7 %collective-permute-start.2 = (bf16[1,8,11520]{2,1,0:T(8,128)(2,1)}, bf16[1,8,11520]{2,1,0:T(8,128)(2,1)S(1)}, u32[]{:S(2)}, u32[]{:S(2)}) collective-permute-start(bf16[1,8,11520]{2,1,0:T(8,128)(2,1)} %get-tuple-element.23), channel_id=1, source_target_pairs={{0,3},{1,2},{2,1},{3,0},{16,19},{17,18},{18,17},{19,16},{4,7},{5,6... | collective-permute-start | bytes 552968 | tf_op jit(solution)/shard_map/ppermute | solution.py:557
  7.3 14.9 %collective-permute-start.3 = (bf16[1,8,8192]{2,1,0:T(8,128)(2,1)}, bf16[1,8,8192]{2,1,0:T(8,128)(2,1)S(1)}, u32[]{:S(2)}, u32[]{:S(2)}) collective-permute-start(bf16[1,8,8192]{2,1,0:T(8,128)(2,1)} %get-tuple-element.24), channel_id=1, source_target_pairs={{0,16},{1,17},{2,18},{3,19},{16,0},{17,1},{18,2},{19,3},{4,20},{5,... | collective-permute-start | bytes 393224 | tf_op jit(solution)/shard_map/ppermute | solution.py:557
  9.2 13.0 %collective-permute-start.4 = (bf16[1,8,8192]{2,1,0:T(8,128)(2,1)}, bf16[1,8,8192]{2,1,0:T(8,128)(2,1)S(1)}, u32[]{:S(2)}, u32[]{:S(2)}) collective-permute-start(bf16[1,8,8192]{2,1,0:T(8,128)(2,1)} %get-tuple-element.25), channel_id=1, source_target_pairs={{0,17},{1,16},{2,19},{3,18},{16,1},{17,0},{18,3},{19,2},{4,21},{5,... | collective-permute-start | bytes 393224 | tf_op jit(solution)/shard_map/ppermute | solution.py:557
  10.7 11.6 %collective-permute-start.5 = (bf16[1,8,8192]{2,1,0:T(8,128)(2,1)}, bf16[1,8,8192]{2,1,0:T(8,128)(2,1)S(1)}, u32[]{:S(2)}, u32[]{:S(2)}) collective-permute-start(bf16[1,8,8192]{2,1,0:T(8,128)(2,1)} %get-tuple-element.26), channel_id=1, source_target_pairs={{0,18},{1,19},{2,16},{3,17},{16,2},{17,3},{18,0},{19,1},{4,22},{5,... | collective-permute-start | bytes 393224 | tf_op jit(solution)/shard_map/ppermute | solution.py:557
  13.9 8.8 %collective-permute-start.6 = (bf16[1,8,8192]{2,1,0:T(8,128)(2,1)}, bf16[1,8,8192]{2,1,0:T(8,128)(2,1)S(1)}, u32[]{:S(2)}, u32[]{:S(2)}) collective-permute-start(bf16[1,8,8192]{2,1,0:T(8,128)(2,1)} %get-tuple-element.27), channel_id=1, source_target_pairs={{0,19},{1,18},{2,17},{3,16},{16,3},{17,2},{18,1},{19,0},{4,23},{5,... | collective-permute-start | bytes 393224 | tf_op jit(solution)/shard_map/ppermute | solution.py:557
  17.0 0.9 %copy-start = (bf16[1,8,11520]{2,1,0:T(8,128)(2,1)S(1)}, bf16[1,8,11520]{2,1,0:T(8,128)(2,1)}, u32[]{:S(2)}) copy-start(bf16[1,8,11520]{2,1,0:T(8,128)(2,1)} %get-tuple-element.20.refs_0_.refs_4_.refs_8_.refs_12_) | copy-start | bytes 552964
  17.9 0.7 copy-start.1
  26.6 1.6 %collective-permute-start.7 = (bf16[2,8,64,128]{3,2,1,0:T(8,128)(2,1)S(1)}, bf16[2,8,64,128]{3,2,1,0:T(8,128)(2,1)S(1)}, u32[]{:S(2)}, u32[]{:S(2)}) collective-permute-start(bf16[2,8,64,128]{3,2,1,0:T(8,128)(2,1)S(1)} %get-tuple-element.29), channel_id=1, source_target_pairs={{0,8},{8,0},{1,9},{9,1},{2,10},{10,2},{3,11},{11,3},{4,12},{12,4},... | collective-permute-start | bytes 786440 | tf_op jit(solution)/shard_map/ppermute | solution.py:27
  28.3 18.9 %copy-start.2 = (s32[8,32]{1,0:T(8,128)S(1)}, s32[8,32]{1,0:T(8,128)}, u32[]{:S(2)}) copy-start(s32[8,32]{1,0:T(8,128)} %listed_ref.1) | copy-start | bytes 3076
  28.3 18.9 %copy-start.3 = (s32[8]{0:T(128)S(1)}, s32[8]{0:T(128)}, u32[]{:S(2)}) copy-start(s32[8]{0:T(128)} %count_ref.1) | copy-start | bytes 100
  28.3 10.6 %collective-permute-start.9 = (bf16[2,8,64,128]{3,2,1,0:T(8,128)(2,1)S(1)}, bf16[2,8,64,128]{3,2,1,0:T(8,128)(2,1)S(1)}, u32[]{:S(2)}, u32[]{:S(2)}) collective-permute-start(bf16[2,8,64,128]{3,2,1,0:T(8,128)(2,1)S(1)} %add_sums.4.refs_16_.refs_0_), channel_id=1, source_target_pairs={{0,6},{2,4},{4,2},{6,0},{1,7},{3,5},{5,3},{7,1},{8,14},{10,12},{12... | collective-permute-start | bytes 786440 | tf_op jit(solution)/shard_map/ppermute | solution.py:608
  38.8 1.6 %collective-permute-start.8 = (bf16[2,8,64,128]{3,2,1,0:T(8,128)(2,1)S(1)}, bf16[2,8,64,128]{3,2,1,0:T(8,128)(2,1)S(1)}, u32[]{:S(2)}, u32[]{:S(2)}) collective-permute-start(bf16[2,8,64,128]{3,2,1,0:T(8,128)(2,1)S(1)} %get-tuple-element.31), channel_id=1, source_target_pairs={{0,8},{8,0},{1,9},{9,1},{2,10},{10,2},{3,11},{11,3},{4,12},{12,4},... | collective-permute-start | bytes 786440 | tf_op jit(solution)/shard_map/ppermute | solution.py:27
  40.5 14.1 %collective-permute-start.10 = (bf16[2,8,64,128]{3,2,1,0:T(8,128)(2,1)S(1)}, bf16[2,8,64,128]{3,2,1,0:T(8,128)(2,1)S(1)}, u32[]{:S(2)}, u32[]{:S(2)}) collective-permute-start(bf16[2,8,64,128]{3,2,1,0:T(8,128)(2,1)S(1)} %add_sums.6.refs_0_), channel_id=1, source_target_pairs={{0,6},{2,4},{4,2},{6,0},{1,7},{3,5},{5,3},{7,1},{8,14},{10,12},{12... | collective-permute-start | bytes 786440 | tf_op jit(solution)/shard_map/ppermute | solution.py:608
  42.5 16.0 %collective-permute-start.15 = (bf16[2,8,64,128]{3,2,1,0:T(8,128)(2,1)S(1)}, bf16[2,8,64,128]{3,2,1,0:T(8,128)(2,1)S(1)}, u32[]{:S(2)}, u32[]{:S(2)}) collective-permute-start(bf16[2,8,64,128]{3,2,1,0:T(8,128)(2,1)S(1)} %add_sums.5.refs_2_.refs_0_), channel_id=1, source_target_pairs={{0,1},{1,0},{2,3},{3,2},{4,5},{5,4},{6,7},{7,6},{8,9},{9,8},{10,11... | collective-permute-start | bytes 786440 | tf_op jit(solution)/shard_map/ppermute | solution.py:594
  44.0 14.6 %collective-permute-start.16 = (bf16[2,8,64,128]{3,2,1,0:T(8,128)(2,1)S(1)}, bf16[2,8,64,128]{3,2,1,0:T(8,128)(2,1)S(1)}, u32[]{:S(2)}, u32[]{:S(2)}) collective-permute-start(bf16[2,8,64,128]{3,2,1,0:T(8,128)(2,1)S(1)} %add_sums.5.refs_2_.refs_0_), channel_id=1, source_target_pairs={{0,2},{1,3},{2,0},{3,1},{4,6},{5,7},{6,4},{7,5},{8,10},{9,11},{10,... | collective-permute-start | bytes 786440 | tf_op jit(solution)/shard_map/ppermute | solution.py:594
  47.2 18.5 %collective-permute-start.12 = (bf16[2,8,64,128]{3,2,1,0:T(8,128)(2,1)S(1)}, bf16[2,8,64,128]{3,2,1,0:T(8,128)(2,1)S(1)}, u32[]{:S(2)}, u32[]{:S(2)}) collective-permute-start(bf16[2,8,64,128]{3,2,1,0:T(8,128)(2,1)S(1)} %add_sums.5.refs_2_.refs_0_), channel_id=1, source_target_pairs={{0,3},{1,2},{2,1},{3,0},{4,7},{5,6},{6,5},{7,4},{8,11},{9,10},{10,... | collective-permute-start | bytes 786440 | tf_op jit(solution)/shard_map/ppermute | solution.py:594
  54.6 12.4 %collective-permute-start.13 = (bf16[2,8,64,128]{3,2,1,0:T(8,128)(2,1)S(1)}, bf16[2,8,64,128]{3,2,1,0:T(8,128)(2,1)S(1)}, u32[]{:S(2)}, u32[]{:S(2)}) collective-permute-start(bf16[2,8,64,128]{3,2,1,0:T(8,128)(2,1)S(1)} %add_sums.7.refs_3_.refs_7_.refs_6_.refs_4_), channel_id=1, source_target_pairs={{0,1},{1,0},{2,3},{3,2},{4,5},{5,4},{6,7},{7,6},{8,9},{9,8},{10,11... | collective-permute-start | bytes 786440 | tf_op jit(solution)/shard_map/ppermute | solution.py:594
  56.1 11.6 %collective-permute-start.14 = (bf16[2,8,64,128]{3,2,1,0:T(8,128)(2,1)S(1)}, bf16[2,8,64,128]{3,2,1,0:T(8,128)(2,1)S(1)}, u32[]{:S(2)}, u32[]{:S(2)}) collective-permute-start(bf16[2,8,64,128]{3,2,1,0:T(8,128)(2,1)S(1)} %add_sums.7.refs_3_.refs_7_.refs_6_.refs_4_), channel_id=1, source_target_pairs={{0,2},{1,3},{2,0},{3,1},{4,6},{5,7},{6,4},{7,5},{8,10},{9,11},{10,... | collective-permute-start | bytes 786440 | tf_op jit(solution)/shard_map/ppermute | solution.py:594
  58.5 15.7 %collective-permute-start.11 = (bf16[2,8,64,128]{3,2,1,0:T(8,128)(2,1)S(1)}, bf16[2,8,64,128]{3,2,1,0:T(8,128)(2,1)S(1)}, u32[]{:S(2)}, u32[]{:S(2)}) collective-permute-start(bf16[2,8,64,128]{3,2,1,0:T(8,128)(2,1)S(1)} %add_sums.7.refs_3_.refs_7_.refs_6_.refs_4_), channel_id=1, source_target_pairs={{0,3},{1,2},{2,1},{3,0},{4,7},{5,6},{6,5},{7,4},{8,11},{9,10},{10,... | collective-permute-start | bytes 786440 | tf_op jit(solution)/shard_map/ppermute | solution.py:594
